TPU v7x, 1024 devices: a whole 4x8x16 slice. The times are simulated.
1024 devices in a mesh: row: 64 (over z, x_lo, core), col: 16 (over y, x_hi).
Axes of the slice: x: 4 (x_hi: 2, x_lo: 2; x = x_hi * 2 + x_lo), y: 8, z: 16, core: 2. Of those that a mesh axis runs over, the one named last changes fastest.
Arguments:
- vectors: bfloat16 [8, 131072], P(None, ('row', 'col')), may hold values from -6 to 6
- tiles: bfloat16 [64, 16, 32, 128, 128], P('row', 'col'), may hold values from -0.125 to 0.125
- tile_rows: int32 [64, 16, 32], P('row', 'col'), may hold values from 0 to 15, as said below
- tile_cols: int32 [64, 16, 32], P('row', 'col'), may hold values from 0 to 63, as said below
- tile_live: int32 [64, 16, 32], P('row', 'col'), may hold values 0 or 1
Outputs:
- image: float32 [8, 131072], P(None, ('row', 'col'))
Inputs may be any that keep to these rules, and one draw needn't show every extreme that they name: `tile_rows`: at least one slot of one device has the largest tile row. On grid row r, tile_cols is at most r.
All inputs are finite; a program needn't handle non-finite values. No bound on the sum of `tile_live` on one device may be relied on, other than what follows from the above.
Results may differ from a plain program's by a relative error of at most 0.0003.
Values may be sent and summed in bfloat16 or wider, within the bound.
No kernel may reach another device: no remote copies, remote signals or barrier semaphores. Data moves between devices by JAX's collectives and lax.ppermute only.
A program may use at most 32 MiB of HBM per device.

v0:
```python
import jax
import jax.numpy as jnp
from jax import lax
from jax.sharding import PartitionSpec as P


def body(vectors, tiles, tile_rows, tile_cols, tile_live):
    nvec, seg = vectors.shape
    per_seg = seg // 128
    n_row = lax.axis_size("row")
    n_col = lax.axis_size("col")
    my_row = lax.axis_index("row")
    my_col = lax.axis_index("col")
    blocks = tiles.reshape(-1, 128, 128)
    rows_local = tile_rows.reshape(-1)
    cols_local = tile_cols.reshape(-1)
    grow = my_row * n_col * per_seg + rows_local
    gcol = (cols_local // per_seg * n_col + my_col) * per_seg + cols_local % per_seg
    keep = tile_live.reshape(-1) == 1
    direct_weight = (keep & (grow >= gcol)).astype(jnp.float32)
    mirror_weight = (keep & (grow > gcol)).astype(jnp.float32)
    column_set = lax.all_gather(vectors, "row", axis=1, tiled=True)
    picked = column_set.reshape(nvec, n_row * per_seg, 128)[:, cols_local, :]
    product = jnp.einsum("vkj,kij->kvi", picked, blocks, preferred_element_type=jnp.float32)
    targets = lax.broadcasted_iota(jnp.int32, (1, n_col * per_seg), 1)
    placing = (rows_local[:, None] == targets).astype(jnp.float32) * direct_weight[:, None]
    partial_value = jnp.einsum("kr,kvi->vri", placing, product, precision=lax.Precision.HIGHEST)
    straight = lax.psum_scatter(
        partial_value.reshape(nvec, n_col * seg), "col", scatter_dimension=1, tiled=True
    )
    row_set = lax.all_gather(vectors, "col", axis=1, tiled=True)
    picked = row_set.reshape(nvec, n_col * per_seg, 128)[:, rows_local, :]
    product = jnp.einsum("vki,kij->kvj", picked, blocks, preferred_element_type=jnp.float32)
    targets = lax.broadcasted_iota(jnp.int32, (1, n_row * per_seg), 1)
    placing = (cols_local[:, None] == targets).astype(jnp.float32) * mirror_weight[:, None]
    partial_value = jnp.einsum("kr,kvj->vrj", placing, product, precision=lax.Precision.HIGHEST)
    mirrored = lax.psum_scatter(
        partial_value.reshape(nvec, n_row * seg), "row", scatter_dimension=1, tiled=True
    )
    return straight + mirrored


def solution(mesh):
    return jax.shard_map(
        body,
        mesh=mesh,
        in_specs=(
            P(None, ("row", "col")),
            P("row", "col", None, None, None),
            P("row", "col", None),
            P("row", "col", None),
            P("row", "col", None),
        ),
        out_specs=P(None, ("row", "col")),
        check_vma=False,
    )
```

profile of v0, /device:TPU:8, one launch (start us, length us, event | category | flops | bytes accessed | tf_op | source)
XLA Modules:
  0.0 487.8 jit_solution(15786450438600451382)
XLA Ops:
  6.5 0.0 copy-start
  6.5 0.0 reduce-scatter.3.cloned.1.call-start
  6.5 0.0 copy-start.1
  6.5 0.8 copy-done.1
  7.3 0.0 copy-start.3
  7.3 76.9 %all_gather.6 = bf16[8,8192]{1,0:T(8,128)(2,1)S(1)} all-gather(bf16[8,128]{1,0:T(8,128)(2,1)S(1)} %copy-done.1), channel_id=1, replica_groups=mesh['row'=64,'col'=16] {'row'}, dimensions={1}, use_global_device_ids=true | all-gather | bytes 133120 | tf_op jit(solution)/shard_map/all_gather | solution.py:22
  84.2 0.0 copy-done.3
  84.2 0.6 gather_fusion
  84.8 0.0 copy-done
  84.9 0.0 copy-start.2
  84.9 0.0 copy-start.4
  84.9 0.6 fusion.2
  85.5 0.0 copy-done.2
  85.5 0.0 copy-done.4
  85.5 0.2 convolution_bitcast_fusion.1
  85.8 0.6 copy.17
  86.4 0.0 reduce-scatter.3.cloned.1.call-update
  86.4 0.0 reduce-scatter.5.cloned.1.call-start
  86.5 39.1 %all_gather.7 = bf16[8,2048]{1,0:T(8,128)(2,1)S(1)} all-gather(bf16[8,128]{1,0:T(8,128)(2,1)S(1)} %copy-done.1), channel_id=1, replica_groups=mesh['row'=64,'col'=16] {'col'}, dimensions={1}, use_global_device_ids=true | all-gather | bytes 34816 | tf_op jit(solution)/shard_map/all_gather | solution.py:31
  125.6 0.6 gather_fusion.1
  126.2 0.4 fusion
  126.6 0.5 convolution_bitcast_fusion
  127.1 0.9 copy.16
  127.9 0.0 reduce-scatter.5.cloned.1.call-update
  128.0 117.4 %reduce-scatter.3.cloned.1.call-done = f32[8,128]{1,0:T(8,128)} async-done(((f32[8,2048]{1,0:T(8,128)}), f32[8,128]{1,0:T(8,128)}) %reduce-scatter.3.cloned.1.call-update) | async-done | bytes 4112 | tf_op jit(solution)/shard_map/reduce_scatter | solution.py:28
  245.4 234.2 %reduce-scatter.5.cloned.1.call-done = f32[8,128]{1,0:T(8,128)} async-done(((f32[8,8192]{1,0:T(8,128)}), f32[8,128]{1,0:T(8,128)}) %reduce-scatter.5.cloned.1.call-update) | async-done | bytes 4112 | tf_op jit(solution)/shard_map/reduce_scatter | solution.py:37
  479.6 1.3 add.80
  (5 shorter events, 0.0 us)
Async XLA Ops:
  6.5 78.3 %copy-start = (bf16[1,1,32,128,128]{4,3,2,1,0:T(8,128)(2,1)S(1)}, bf16[1,1,32,128,128]{4,3,2,1,0:T(8,128)(2,1)}, u32[]{:S(2)}) copy-start(bf16[1,1,32,128,128]{4,3,2,1,0:T(8,128)(2,1)} %param.6) | copy-start | bytes 3145732
  6.5 238.9 %reduce-scatter.3.cloned.1.call-start = ((), (), s32[]{:S(2)}) async-start(), calls=%async_computation.2 | async-start | bytes 69632 | tf_op jit(solution)/shard_map/reduce_scatter | solution.py:28
  6.5 0.8 copy-start.1
  7.3 76.9 %copy-start.3 = (s32[1,1,32]{2,1,0:T(1,128)S(1)}, s32[1,1,32]{2,1,0:T(1,128)}, u32[]{:S(2)}) copy-start(s32[1,1,32]{2,1,0:T(1,128)} %param.8) | copy-start | bytes 388
  84.9 0.7 copy-start.2
  84.9 0.7 copy-start.4
  86.4 393.2 %reduce-scatter.5.cloned.1.call-start = ((), (), s32[]{:S(2)}) async-start(), calls=%async_computation.3 | async-start | bytes 266240 | tf_op jit(solution)/shard_map/reduce_scatter | solution.py:37
Sparse Core Ops, SparseCore 0:
  86.6 158.7 reduce-scatter.2
  249.1 230.4 reduce-scatter.4
where the time goes:
time: 488 us
  waiting for transfers between devices  352 us (72%)
  blocking collectives  116 us (24%)
  between operations  13.4 us (3%)
    reduce_scatter x1, waiting for transfers between devices, body(): lax.psum_scatter(partial_value.reshape(nvec, n_row * seg), 'row', scatter...  234 us
    reduce_scatter x1, waiting for transfers between devices, body(): lax.psum_scatter(partial_value.reshape(nvec, n_col * seg), 'col', scatter...  117 us
    all_gather x1, blocking collectives, body(): column_set = lax.all_gather(vectors, 'row', axis=1, tiled=True)  76.9 us
    all_gather x1, blocking collectives, body(): row_set = lax.all_gather(vectors, 'col', axis=1, tiled=True)  39.1 us
  transfers between devices with their start and end apart: 2, of which 2 were waited for; matrix products, arithmetic and copies ran while one was open for 0% of the time, Pallas kernels for 0%

commit v1 on v0

v1 whole, which is shorter than its diff:
```python
import jax
import jax.numpy as jnp
from jax import lax
from jax.sharding import PartitionSpec as P


def exchange(parts, axis):
    return lax.all_to_all(parts, axis, 0, 0, tiled=True)


def body(vectors, tiles, tile_rows, tile_cols, tile_live):
    nvec, seg = vectors.shape
    n_row = lax.axis_size("row")
    n_col = lax.axis_size("col")
    my_row = lax.axis_index("row")
    my_col = lax.axis_index("col")
    blocks = tiles.reshape(-1, 128, 128)
    rows_local = tile_rows.reshape(-1)
    cols_local = tile_cols.reshape(-1)
    grow = my_row * n_col + rows_local
    gcol = cols_local * n_col + my_col
    keep = tile_live.reshape(-1) == 1
    direct_weight = (keep & (grow >= gcol)).astype(jnp.float32)
    mirror_weight = (keep & (grow > gcol)).astype(jnp.float32)

    row_set = exchange(jnp.broadcast_to(vectors[None], (n_col, nvec, seg)), "col")
    column_set = exchange(jnp.broadcast_to(vectors[None], (n_row, nvec, seg)), "row")

    picked = row_set[rows_local]
    product = jnp.einsum("kvi,kij->kvj", picked, blocks, preferred_element_type=jnp.float32)
    targets = lax.broadcasted_iota(jnp.int32, (n_row, 1), 0)
    placing = (cols_local[None, :] == targets).astype(jnp.float32) * mirror_weight[None, :]
    mirrored = exchange(jnp.einsum("rk,kvj->rvj", placing, product, precision=lax.Precision.HIGHEST), "row")

    picked = column_set[cols_local]
    product = jnp.einsum("kvj,kij->kvi", picked, blocks, preferred_element_type=jnp.float32)
    targets = lax.broadcasted_iota(jnp.int32, (n_col, 1), 0)
    placing = (rows_local[None, :] == targets).astype(jnp.float32) * direct_weight[None, :]
    straight = exchange(jnp.einsum("rk,kvi->rvi", placing, product, precision=lax.Precision.HIGHEST), "col")
    return jnp.sum(straight, axis=0) + jnp.sum(mirrored, axis=0)


def solution(mesh):
    return jax.shard_map(
        body,
        mesh=mesh,
        in_specs=(
            P(None, ("row", "col")),
            P("row", "col", None, None, None),
            P("row", "col", None),
            P("row", "col", None),
            P("row", "col", None),
        ),
        out_specs=P(None, ("row", "col")),
        check_vma=False,
    )
```

time: 488 us -> 104 us (0.21)
  the two profiles are of different devices: /device:TPU:8 before, /device:TPU:1 now
where the time goes in v1:
time: 104 us
  waiting for transfers between devices  54.3 us (52%)
  starting transfers between devices  40.9 us (39%)
  local copies, waits for them, and re-layouts  6.02 us (6%)
  matrix products  1.71 us (2%)
    all_to_all x4, waiting for transfers between devices, exchange(): return lax.all_to_all(parts, axis, 0, 0, tiled=True)  54.3 us
    all_to_all x4, starting transfers between devices, exchange(): return lax.all_to_all(parts, axis, 0, 0, tiled=True)  40.9 us
  transfers between devices with their start and end apart: 4, of which 4 were waited for; matrix products, arithmetic and copies ran while one was open for 2% of the time, Pallas kernels for 0%

profile of v1, /device:TPU:1, one launch (start us, length us, event | category | flops | bytes accessed | tf_op | source)
XLA Modules:
  0.0 103.7 jit_solution(17731600498967696626)
XLA Ops:
  0.0 0.0 copy-start
  0.0 1.4 %broadcast_in_dim.5 = bf16[16,8,128]{2,1,0:T(8,128)(2,1)} broadcast(bf16[8,128]{1,0:T(8,128)(2,1)} %param.5), dimensions={1,2} | broadcast | bytes 34816 | tf_op jit(solution)/shard_map/broadcast_in_dim | solution.py:26
  1.4 0.0 copy-start.2
  1.4 10.3 %all-to-all-start.2 = ((bf16[16,8,128]{2,1,0:T(8,128)(2,1)}), bf16[16,8,128]{2,1,0:T(8,128)(2,1)S(1)}, u32[]{:S(2)}, u32[]{:S(2)}) async-start(bf16[16,8,128]{2,1,0:T(8,128)(2,1)} %broadcast_in_dim.5), calls=%async_computation.2 | async-start | bytes 65536 | tf_op jit(solution)/shard_map/all_to_all | solution.py:8
  11.7 0.0 copy-done.2
  11.7 0.0 copy-start.3
  11.8 0.6 copy-done.3
  12.4 0.0 copy-start.1
  12.4 8.4 %all-to-all-done.2 = bf16[16,8,128]{2,1,0:T(8,128)(2,1)S(1)} async-done(((bf16[16,8,128]{2,1,0:T(8,128)(2,1)}), bf16[16,8,128]{2,1,0:T(8,128)(2,1)S(1)}, u32[]{:S(2)}, u32[]{:S(2)}) %all-to-all-start.2) | async-done | bytes 32800 | tf_op jit(solution)/shard_map/all_to_all | solution.py:8
  20.9 0.0 copy-done.1
  20.9 0.7 broadcast_in_dim.4
  21.5 21.4 %all-to-all-start = ((bf16[64,8,128]{2,1,0:T(8,128)(2,1)}), bf16[64,8,128]{2,1,0:T(8,128)(2,1)S(1)}, u32[]{:S(2)}, u32[]{:S(2)}) async-start(bf16[64,8,128]{2,1,0:T(8,128)(2,1)} %broadcast_in_dim.4), calls=%async_computation | async-start | bytes 262144 | tf_op jit(solution)/shard_map/all_to_all | solution.py:8
  43.0 0.0 copy-start.4
  43.0 0.6 copy-done.4
  43.7 0.6 gather_fusion.1
  44.3 0.0 copy-done
  44.3 0.4 fusion
  44.7 15.4 %all-to-all-done = bf16[64,8,128]{2,1,0:T(8,128)(2,1)S(1)} async-done(((bf16[64,8,128]{2,1,0:T(8,128)(2,1)}), bf16[64,8,128]{2,1,0:T(8,128)(2,1)S(1)}, u32[]{:S(2)}, u32[]{:S(2)}) %all-to-all-start) | async-done | bytes 131104 | tf_op jit(solution)/shard_map/all_to_all | solution.py:8
  60.1 0.6 gather_fusion
  60.7 0.6 fusion.2
  61.3 0.2 fusion.6
  61.5 0.6 copy.6
  62.2 3.5 %all-to-all-start.1 = ((f32[16,8,128]{2,1,0:T(8,128)}), f32[16,8,128]{2,1,0:T(8,128)S(1)}, u32[]{:S(2)}, u32[]{:S(2)}) async-start(f32[16,8,128]{2,1,0:T(8,128)} %copy.6), calls=%async_computation.1 | async-start | bytes 131072 | tf_op jit(solution)/shard_map/all_to_all | solution.py:8
  65.7 0.5 fusion.4
  66.2 0.8 copy.7
  67.0 8.1 %all-to-all-done.1 = f32[16,8,128]{2,1,0:T(8,128)S(1)} async-done(((f32[16,8,128]{2,1,0:T(8,128)}), f32[16,8,128]{2,1,0:T(8,128)S(1)}, u32[]{:S(2)}, u32[]{:S(2)}) %all-to-all-start.1) | async-done | bytes 65568 | tf_op jit(solution)/shard_map/all_to_all | solution.py:8
  75.1 5.6 %all-to-all-start.3 = ((f32[64,8,128]{2,1,0:T(8,128)}), f32[64,8,128]{2,1,0:T(8,128)S(1)}, u32[]{:S(2)}, u32[]{:S(2)}) async-start(f32[64,8,128]{2,1,0:T(8,128)} %copy.7), calls=%async_computation.3 | async-start | bytes 524288 | tf_op jit(solution)/shard_map/all_to_all | solution.py:8
  80.7 22.3 %all-to-all-done.3 = f32[64,8,128]{2,1,0:T(8,128)S(1)} async-done(((f32[64,8,128]{2,1,0:T(8,128)}), f32[64,8,128]{2,1,0:T(8,128)S(1)}, u32[]{:S(2)}, u32[]{:S(2)}) %all-to-all-start.3) | async-done | bytes 262176 | tf_op jit(solution)/shard_map/all_to_all | solution.py:8
  103.0 0.1 reduce_sum.19
  103.1 0.6 add.59
  (6 shorter events, 0.0 us)
Async XLA Ops:
  0.0 44.3 %copy-start = (bf16[1,1,32,128,128]{4,3,2,1,0:T(8,128)(2,1)S(1)}, bf16[1,1,32,128,128]{4,3,2,1,0:T(8,128)(2,1)}, u32[]{:S(2)}) copy-start(bf16[1,1,32,128,128]{4,3,2,1,0:T(8,128)(2,1)} %param.6) | copy-start | bytes 3145732
  1.4 10.4 %copy-start.2 = (s32[1,1,32]{2,1,0:T(1,128)S(1)}, s32[1,1,32]{2,1,0:T(1,128)}, u32[]{:S(2)}) copy-start(s32[1,1,32]{2,1,0:T(1,128)} %param.7) | copy-start | bytes 388
  1.4 19.5 %all-to-all-start.2 = ((bf16[16,8,128]{2,1,0:T(8,128)(2,1)}), bf16[16,8,128]{2,1,0:T(8,128)(2,1)S(1)}, u32[]{:S(2)}, u32[]{:S(2)}) async-start(bf16[16,8,128]{2,1,0:T(8,128)(2,1)} %broadcast_in_dim.5), calls=%async_computation.2 | async-start | bytes 65536 | tf_op jit(solution)/shard_map/all_to_all | solution.py:8
  11.7 0.7 copy-start.3
  12.4 8.5 %copy-start.1 = (bf16[8,128]{1,0:T(8,128)(2,1)S(1)}, bf16[8,128]{1,0:T(8,128)(2,1)}, u32[]{:S(2)}) copy-start(bf16[8,128]{1,0:T(8,128)(2,1)} %param.5) | copy-start | bytes 6148
  21.5 38.6 %all-to-all-start = ((bf16[64,8,128]{2,1,0:T(8,128)(2,1)}), bf16[64,8,128]{2,1,0:T(8,128)(2,1)S(1)}, u32[]{:S(2)}, u32[]{:S(2)}) async-start(bf16[64,8,128]{2,1,0:T(8,128)(2,1)} %broadcast_in_dim.4), calls=%async_computation | async-start | bytes 262144 | tf_op jit(solution)/shard_map/all_to_all | solution.py:8
  43.0 0.7 copy-start.4
  62.2 12.9 %all-to-all-start.1 = ((f32[16,8,128]{2,1,0:T(8,128)}), f32[16,8,128]{2,1,0:T(8,128)S(1)}, u32[]{:S(2)}, u32[]{:S(2)}) async-start(f32[16,8,128]{2,1,0:T(8,128)} %copy.6), calls=%async_computation.1 | async-start | bytes 131072 | tf_op jit(solution)/shard_map/all_to_all | solution.py:8
  75.1 27.9 %all-to-all-start.3 = ((f32[64,8,128]{2,1,0:T(8,128)}), f32[64,8,128]{2,1,0:T(8,128)S(1)}, u32[]{:S(2)}, u32[]{:S(2)}) async-start(f32[64,8,128]{2,1,0:T(8,128)} %copy.7), calls=%async_computation.3 | async-start | bytes 524288 | tf_op jit(solution)/shard_map/all_to_all | solution.py:8

commit v2 on v1

v2 whole, which is shorter than its diff:
```python
import jax
import jax.numpy as jnp
from jax import lax
from jax.experimental import pallas as pl
from jax.experimental.pallas import tpu as pltpu
from jax.sharding import PartitionSpec as P

SMEM = pl.BlockSpec(memory_space=pltpu.SMEM)
VMEM = pl.BlockSpec(memory_space=pltpu.VMEM)


def exchange(parts, axis):
    return lax.all_to_all(parts, axis, 0, 0, tiled=True)


def mirror_kernel(slots, place, vec, row_set, tiles, parts):
    my_row = place[0]
    own = vec[...].astype(jnp.float32)
    for r in range(parts.shape[0]):
        parts[r] = jnp.where(r > my_row, own, 0.0)
    for k in range(tiles.shape[0]):
        product = jnp.dot(row_set[slots[0, k]], tiles[k], preferred_element_type=jnp.float32)
        weight = slots[3, k].astype(jnp.float32)
        parts[slots[1, k]] += product * weight


def direct_kernel(slots, place, vec, arrived, tiles, parts):
    my_row = place[0]
    parts[...] = jnp.zeros_like(parts)
    for k in range(tiles.shape[0]):
        source = slots[1, k]
        values = jnp.where(source == my_row, vec[...], arrived[source].astype(jnp.bfloat16))
        product = lax.dot_general(
            values, tiles[k], (((1,), (1,)), ((), ())), preferred_element_type=jnp.float32
        )
        weight = slots[2, k].astype(jnp.float32)
        parts[slots[0, k]] += product * weight


def body(vectors, tiles, tile_rows, tile_cols, tile_live):
    nvec, seg = vectors.shape
    n_row = lax.axis_size("row")
    n_col = lax.axis_size("col")
    my_row = lax.axis_index("row")
    my_col = lax.axis_index("col")
    blocks = tiles.reshape(-1, 128, 128)
    rows_local = tile_rows.reshape(-1)
    cols_local = tile_cols.reshape(-1)
    grow = my_row * n_col + rows_local
    gcol = cols_local * n_col + my_col
    keep = tile_live.reshape(-1) == 1
    direct_weight = (keep & (grow >= gcol)).astype(jnp.int32)
    mirror_weight = (keep & (grow > gcol)).astype(jnp.int32)
    slots = jnp.stack([rows_local, cols_local, direct_weight, mirror_weight])
    place = my_row.reshape(1)

    row_set = exchange(jnp.broadcast_to(vectors[None], (n_col, nvec, seg)), "col")
    outgoing = pl.pallas_call(
        mirror_kernel,
        out_shape=jax.ShapeDtypeStruct((n_row, nvec, seg), jnp.float32),
        in_specs=[SMEM, SMEM, VMEM, VMEM, VMEM],
        out_specs=VMEM,
        name="mirror",
        compiler_params=pltpu.CompilerParams(vmem_limit_bytes=4 << 20),
    )(slots, place, vectors, row_set, blocks)
    arrived = exchange(outgoing, "row")
    direct = pl.pallas_call(
        direct_kernel,
        out_shape=jax.ShapeDtypeStruct((n_col, nvec, seg), jnp.float32),
        in_specs=[SMEM, SMEM, VMEM, VMEM, VMEM],
        out_specs=VMEM,
        name="direct",
        compiler_params=pltpu.CompilerParams(vmem_limit_bytes=4 << 20),
    )(slots, place, vectors, arrived, blocks)
    straight = exchange(direct, "col")
    senders = lax.broadcasted_iota(jnp.int32, (n_row, 1, 1), 0)
    mirrored = jnp.sum(jnp.where(senders >= my_row, arrived, 0.0), axis=0)
    return mirrored + jnp.sum(straight, axis=0)


def solution(mesh):
    return jax.shard_map(
        body,
        mesh=mesh,
        in_specs=(
            P(None, ("row", "col")),
            P("row", "col", None, None, None),
            P("row", "col", None),
            P("row", "col", None),
            P("row", "col", None),
        ),
        out_specs=P(None, ("row", "col")),
        check_vma=False,
    )
```

time: 104 us -> 83.2 us (0.80)
  the two profiles are of different devices: /device:TPU:1 before, /device:TPU:2 now
where the time goes in v2:
time: 83.2 us; the launch traced here: 82.9 us
  waiting for transfers between devices  42.3 us (51%)
  starting transfers between devices  33 us (40%)
  Pallas kernels  3.51 us (4%)
  local copies, waits for them, and re-layouts  3.18 us (4%)
    all_to_all x3, waiting for transfers between devices, exchange(): return lax.all_to_all(parts, axis, 0, 0, tiled=True)  42.3 us
    all_to_all x3, starting transfers between devices, exchange(): return lax.all_to_all(parts, axis, 0, 0, tiled=True)  33 us
    unnamed x12, local copies, waits for them, and re-layouts  1.89 us
    pallas_call x1, Pallas kernels, body(): pl.pallas_call(direct_kernel, out_shape=jax.ShapeDtypeStruct((n_col, nvec...  1.85 us
  transfers between devices with their start and end apart: 3, of which 3 were waited for; matrix products, arithmetic and copies ran while one was open for 0% of the time, Pallas kernels for 0%

profile of v2, /device:TPU:2, one launch (start us, length us, event | category | flops | bytes accessed | tf_op | source)
XLA Modules:
  0.0 82.9 jit_solution(10180929222717719568)
XLA Ops:
  0.0 1.3 %broadcast_in_dim.19 = bf16[16,8,128]{2,1,0:T(8,128)(2,1)} broadcast(bf16[8,128]{1,0:T(8,128)(2,1)} %vec.3), dimensions={1,2} | broadcast | bytes 34816 | tf_op jit(solution)/shard_map/broadcast_in_dim | solution.py:57
  1.3 8.8 %all-to-all-start = ((bf16[16,8,128]{2,1,0:T(8,128)(2,1)}), bf16[16,8,128]{2,1,0:T(8,128)(2,1)S(1)}, u32[]{:S(2)}, u32[]{:S(2)}) async-start(bf16[16,8,128]{2,1,0:T(8,128)(2,1)} %broadcast_in_dim.19), calls=%async_computation | async-start | bytes 65536 | tf_op jit(solution)/shard_map/all_to_all | solution.py:13
  10.1 0.0 copy-start.3
  10.1 0.0 copy-start.4
  10.1 0.0 copy-start.5
  10.1 0.6 copy-done.3
  10.7 0.0 copy-done.4
  10.7 0.0 copy-done.5
  10.8 0.0 copy-start.2
  10.8 9.6 %all-to-all-done.row_set = bf16[16,8,128]{2,1,0:T(8,128)(2,1)S(1)} async-done(((bf16[16,8,128]{2,1,0:T(8,128)(2,1)}), bf16[16,8,128]{2,1,0:T(8,128)(2,1)S(1)}, u32[]{:S(2)}, u32[]{:S(2)}) %all-to-all-start) | async-done | bytes 32800 | tf_op jit(solution)/shard_map/all_to_all | solution.py:13
  20.3 0.0 copy-done.2
  20.3 0.0 copy-start
  20.3 1.2 %copy-done = bf16[1,1,32,128,128]{4,3,2,1,0:T(8,128)(2,1)S(1)} copy-done((bf16[1,1,32,128,128]{4,3,2,1,0:T(8,128)(2,1)S(1)}, bf16[1,1,32,128,128]{4,3,2,1,0:T(8,128)(2,1)}, u32[]{:S(2)}) %copy-start) | copy-done | bytes 1048600
  21.6 0.0 copy-start.1
  21.6 1.7 %mirror.1 = f32[64,8,128]{2,1,0:T(8,128)} custom-call(s32[4,32]{1,0:T(4,128)S(1)} %pad_add_fusion.slots, s32[1]{0:T(128)} %bitcast.3.place, bf16[8,128]{1,0:T(8,128)(2,1)S(1)} %copy-done.2, bf16[16,8,128]{2,1,0:T(8,128)(2,1)S(1)} %all-to-all-done.row_set, bf16[32,128,128]{2,1,0:T(8,128)(2,1)S(1)} %bitcast.18), custom_call_target="tpu_custom_call" | custom-call | tf_op jit(solution)/shard_map/mirror/pallas_call | solution.py:58
  23.2 20.8 %all-to-all-start.1 = ((f32[64,8,128]{2,1,0:T(8,128)}), f32[64,8,128]{2,1,0:T(8,128)S(1)}, u32[]{:S(2)}, u32[]{:S(2)}) async-start(f32[64,8,128]{2,1,0:T(8,128)} %mirror.1), calls=%async_computation.1 | async-start | bytes 524288 | tf_op jit(solution)/shard_map/all_to_all | solution.py:13
  44.0 22.3 %all-to-all-done.1.arrived = f32[64,8,128]{2,1,0:T(8,128)S(1)} async-done(((f32[64,8,128]{2,1,0:T(8,128)}), f32[64,8,128]{2,1,0:T(8,128)S(1)}, u32[]{:S(2)}, u32[]{:S(2)}) %all-to-all-start.1) | async-done | bytes 262176 | tf_op jit(solution)/shard_map/all_to_all | solution.py:13
  66.3 0.0 copy-done.1
  66.3 1.9 %direct.1 = f32[16,8,128]{2,1,0:T(8,128)} custom-call(s32[4,32]{1,0:T(4,128)S(1)} %pad_add_fusion.slots, s32[1]{0:T(128)} %bitcast.3.place, bf16[8,128]{1,0:T(8,128)(2,1)S(1)} %copy-done.2, f32[64,8,128]{2,1,0:T(8,128)S(1)} %all-to-all-done.1.arrived, bf16[32,128,128]{2,1,0:T(8,128)(2,1)S(1)} %bitcast.19), custom_call_target="tpu_custom_call" | custom-call | tf_op jit(solution)/shard_map/direct/pallas_call | solution.py:67
  68.2 3.5 %all-to-all-start.2 = ((f32[16,8,128]{2,1,0:T(8,128)}), f32[16,8,128]{2,1,0:T(8,128)S(1)}, u32[]{:S(2)}, u32[]{:S(2)}) async-start(f32[16,8,128]{2,1,0:T(8,128)} %direct.1), calls=%async_computation.2 | async-start | bytes 131072 | tf_op jit(solution)/shard_map/all_to_all | solution.py:13
  71.7 0.1 select_reduce_fusion
  71.8 10.4 %all-to-all-done.2 = f32[16,8,128]{2,1,0:T(8,128)S(1)} async-done(((f32[16,8,128]{2,1,0:T(8,128)}), f32[16,8,128]{2,1,0:T(8,128)S(1)}, u32[]{:S(2)}, u32[]{:S(2)}) %all-to-all-start.2) | async-done | bytes 65568 | tf_op jit(solution)/shard_map/all_to_all | solution.py:13
  82.3 0.6 add.41
  (4 shorter events, 0.0 us)
Async XLA Ops:
  1.3 19.1 %all-to-all-start = ((bf16[16,8,128]{2,1,0:T(8,128)(2,1)}), bf16[16,8,128]{2,1,0:T(8,128)(2,1)S(1)}, u32[]{:S(2)}, u32[]{:S(2)}) async-start(bf16[16,8,128]{2,1,0:T(8,128)(2,1)} %broadcast_in_dim.19), calls=%async_computation | async-start | bytes 65536 | tf_op jit(solution)/shard_map/all_to_all | solution.py:13
  10.1 0.7 copy-start.3
  10.1 0.7 copy-start.4
  10.1 0.7 copy-start.5
  10.8 9.6 %copy-start.2 = (bf16[8,128]{1,0:T(8,128)(2,1)S(1)}, bf16[8,128]{1,0:T(8,128)(2,1)}, u32[]{:S(2)}) copy-start(bf16[8,128]{1,0:T(8,128)(2,1)} %vec.3) | copy-start | bytes 6148
  20.3 1.2 %copy-start = (bf16[1,1,32,128,128]{4,3,2,1,0:T(8,128)(2,1)S(1)}, bf16[1,1,32,128,128]{4,3,2,1,0:T(8,128)(2,1)}, u32[]{:S(2)}) copy-start(bf16[1,1,32,128,128]{4,3,2,1,0:T(8,128)(2,1)} %param.6) | copy-start | bytes 3145732
  21.6 44.8 %copy-start.1 = (bf16[1,1,32,128,128]{4,3,2,1,0:T(8,128)(2,1)S(1)}, bf16[1,1,32,128,128]{4,3,2,1,0:T(8,128)(2,1)}, u32[]{:S(2)}) copy-start(bf16[1,1,32,128,128]{4,3,2,1,0:T(8,128)(2,1)} %param.6) | copy-start | bytes 3145732
  23.2 43.1 %all-to-all-start.1 = ((f32[64,8,128]{2,1,0:T(8,128)}), f32[64,8,128]{2,1,0:T(8,128)S(1)}, u32[]{:S(2)}, u32[]{:S(2)}) async-start(f32[64,8,128]{2,1,0:T(8,128)} %mirror.1), calls=%async_computation.1 | async-start | bytes 524288 | tf_op jit(solution)/shard_map/all_to_all | solution.py:13
  68.2 14.1 %all-to-all-start.2 = ((f32[16,8,128]{2,1,0:T(8,128)}), f32[16,8,128]{2,1,0:T(8,128)S(1)}, u32[]{:S(2)}, u32[]{:S(2)}) async-start(f32[16,8,128]{2,1,0:T(8,128)} %direct.1), calls=%async_computation.2 | async-start | bytes 131072 | tf_op jit(solution)/shard_map/all_to_all | solution.py:13

commit v3 on v2

v3 whole, which is shorter than its diff:
```python
import jax
import jax.numpy as jnp
from jax import lax
from jax.experimental import pallas as pl
from jax.experimental.pallas import tpu as pltpu
from jax.sharding import PartitionSpec as P

SMEM = pl.BlockSpec(memory_space=pltpu.SMEM)
VMEM = pl.BlockSpec(memory_space=pltpu.VMEM)


def exchange(parts, axis):
    return lax.all_to_all(parts, axis, 0, 0, tiled=True)


def mirror_kernel(n_col, rows, cols, vec, row_set, tiles, parts):
    my_row, my_col = lax.axis_index("row"), lax.axis_index("col")
    own = vec[...].astype(jnp.float32)
    for r in range(parts.shape[0]):
        parts[r] = jnp.where(r > my_row, own, 0.0)
    for k in range(tiles.shape[0]):
        product = jnp.dot(row_set[rows[0, 0, k]], tiles[k], preferred_element_type=jnp.float32)
        below = my_row * n_col + rows[0, 0, k] > cols[0, 0, k] * n_col + my_col
        weight = jnp.where(below, 1.0, 0.0)
        parts[cols[0, 0, k]] += product * weight


def direct_kernel(n_col, rows, cols, vec, arrived, tiles, parts, mirrored):
    my_row, my_col = lax.axis_index("row"), lax.axis_index("col")
    total = jnp.zeros(mirrored.shape, jnp.float32)
    for r in range(arrived.shape[0]):
        total += jnp.where(r >= my_row, arrived[r], 0.0)
    mirrored[...] = total
    parts[...] = jnp.zeros_like(parts)
    for k in range(tiles.shape[0]):
        source = cols[0, 0, k]
        values = jnp.where(source == my_row, vec[...], arrived[source].astype(jnp.bfloat16))
        product = lax.dot_general(
            values, tiles[k], (((1,), (1,)), ((), ())), preferred_element_type=jnp.float32
        )
        below = my_row * n_col + rows[0, 0, k] >= source * n_col + my_col
        weight = jnp.where(below, 1.0, 0.0)
        parts[rows[0, 0, k]] += product * weight


def body(vectors, tiles, tile_rows, tile_cols, tile_live):
    nvec, seg = vectors.shape
    n_row = lax.axis_size("row")
    n_col = lax.axis_size("col")
    live = (tile_live.reshape(-1, 1, 1) == 1).astype(tiles.dtype)
    blocks = tiles.reshape(-1, 128, 128) * live
    params = pltpu.CompilerParams(vmem_limit_bytes=4 << 20)

    row_set = exchange(jnp.broadcast_to(vectors[None], (n_col, nvec, seg)), "col")
    outgoing = pl.pallas_call(
        lambda *refs: mirror_kernel(n_col, *refs),
        out_shape=jax.ShapeDtypeStruct((n_row, nvec, seg), jnp.float32),
        in_specs=[SMEM] * 2 + [VMEM] * 3,
        out_specs=VMEM,
        compiler_params=params,
        name="mirror",
    )(tile_rows, tile_cols, vectors, row_set, blocks)
    arrived = exchange(outgoing, "row")
    direct, mirrored = pl.pallas_call(
        lambda *refs: direct_kernel(n_col, *refs),
        out_shape=[
            jax.ShapeDtypeStruct((n_col, nvec, seg), jnp.float32),
            jax.ShapeDtypeStruct((nvec, seg), jnp.float32),
        ],
        in_specs=[SMEM] * 2 + [VMEM] * 3,
        out_specs=[VMEM, VMEM],
        compiler_params=params,
        name="direct",
    )(tile_rows, tile_cols, vectors, arrived, blocks)
    straight = exchange(direct, "col")
    return mirrored + jnp.sum(straight, axis=0)


def solution(mesh):
    return jax.shard_map(
        body,
        mesh=mesh,
        in_specs=(
            P(None, ("row", "col")),
            P("row", "col", None, None, None),
            P("row", "col", None),
            P("row", "col", None),
            P("row", "col", None),
        ),
        out_specs=P(None, ("row", "col")),
        check_vma=False,
    )
```

time: 83.2 us -> 79.6 us (0.957)
  blocking collectives: 0 us -> 56.1 us
  waiting for transfers between devices: 42.3 us -> 8.84 us
  starting transfers between devices: 33 us -> 8.9 us
  local copies, waits for them, and re-layouts: 3.18 us -> 1.31 us
  Pallas kernels: 3.51 us -> 2.17 us
  other arithmetic: 0.78 us -> 1.99 us
    all_to_all x0 -> x2, blocking collectives: none -> 56.1 us  [exchange(): return lax.all_to_all(parts, axis, 0, 0, tiled=True)]
    all_to_all x3 -> x1, waiting for transfers between devices: 42.3 us -> 8.84 us  [exchange(): return lax.all_to_all(parts, axis, 0, 0, tiled=True)]
    all_to_all x3 -> x1, starting transfers between devices: 33 us -> 8.9 us  [exchange(): return lax.all_to_all(parts, axis, 0, 0, tiled=True)]
    unnamed x12 -> x8, local copies, waits for them, and re-layouts: 1.89 us -> 0.02 us
    mul x0 -> x1, other arithmetic: none -> 1.37 us  [body(): blocks = tiles.reshape(-1, 128, 128) * live]
    pallas_call x2, Pallas kernels: 3.51 us -> 2.17 us  [the longest x1 1.23 us: body(): pl.pallas_call(lambda *refs: direct_kernel(n_col, *refs), out_shape=[jax....]
  transfers between devices with their start and end apart: 3 -> 1, of which waited for: 3 -> 1; matrix products, arithmetic and copies ran while one was open for 0% -> 2% of each run, Pallas kernels for 0% -> 0%
where the time goes in v3:
time: 79.6 us; the launch traced here: 79.3 us
  blocking collectives  56.1 us (70%)
  starting transfers between devices  8.9 us (11%)
  waiting for transfers between devices  8.84 us (11%)
  Pallas kernels  2.17 us (3%)
  other arithmetic  1.99 us (2%)
  local copies, waits for them, and re-layouts  1.31 us (2%)
    all_to_all x2, blocking collectives, exchange(): return lax.all_to_all(parts, axis, 0, 0, tiled=True)  56.1 us
    all_to_all x1, starting transfers between devices, exchange(): return lax.all_to_all(parts, axis, 0, 0, tiled=True)  8.9 us
    all_to_all x1, waiting for transfers between devices, exchange(): return lax.all_to_all(parts, axis, 0, 0, tiled=True)  8.84 us
  transfers between devices with their start and end apart: 1, of which 1 were waited for; matrix products, arithmetic and copies ran while one was open for 2% of the time, Pallas kernels for 0%

profile of v3, /device:TPU:2, one launch (start us, length us, event | category | flops | bytes accessed | tf_op | source)
XLA Modules:
  0.0 79.3 jit_solution(7018129978272660401)
XLA Ops:
  0.0 1.3 %broadcast_in_dim.2 = bf16[16,8,128]{2,1,0:T(8,128)(2,1)} broadcast(bf16[8,128]{1,0:T(8,128)(2,1)} %refs_2_.3), dimensions={1,2} | broadcast | bytes 34816 | tf_op jit(solution)/shard_map/broadcast_in_dim | solution.py:54
  1.3 0.0 copy-start.3
  1.3 8.9 %all-to-all-start = ((bf16[16,8,128]{2,1,0:T(8,128)(2,1)}), bf16[16,8,128]{2,1,0:T(8,128)(2,1)S(1)}, u32[]{:S(2)}, u32[]{:S(2)}) async-start(bf16[16,8,128]{2,1,0:T(8,128)(2,1)} %broadcast_in_dim.2), calls=%async_computation | async-start | bytes 65536 | tf_op jit(solution)/shard_map/all_to_all | solution.py:13
  10.2 0.0 copy-done.3
  10.2 0.0 copy-start
  10.2 0.0 copy-start.1
  10.2 0.0 copy-start.2
  10.3 1.4 %bitcast_multiply_fusion.refs_4_ = bf16[32,128,128]{2,1,0:T(8,128)(2,1)S(1)} fusion(bf16[1,1,32,128,128]{4,3,2,1,0:T(8,128)(2,1)} %param.6, bf16[32]{0:T(256)(128)(2,1)S(1)} %fusion), kind=kLoop, calls=%fused_computation | loop fusion | flops 524288 | bytes 2097216 | tf_op jit(solution)/shard_map/mul | solution.py:51
  11.6 8.8 %all-to-all-done.refs_3_ = bf16[16,8,128]{2,1,0:T(8,128)(2,1)S(1)} async-done(((bf16[16,8,128]{2,1,0:T(8,128)(2,1)}), bf16[16,8,128]{2,1,0:T(8,128)(2,1)S(1)}, u32[]{:S(2)}, u32[]{:S(2)}) %all-to-all-start) | async-done | bytes 32800 | tf_op jit(solution)/shard_map/all_to_all | solution.py:13
  20.5 0.0 copy-done
  20.5 0.0 copy-done.1
  20.5 0.0 copy-done.2
  20.5 0.9 %mirror.1 = f32[64,8,128]{2,1,0:T(8,128)S(1)} custom-call(s32[1,1,32]{2,1,0:T(1,128)S(1)} %copy-done.1, s32[1,1,32]{2,1,0:T(1,128)S(1)} %copy-done.2, bf16[8,128]{1,0:T(8,128)(2,1)S(1)} %copy-done, bf16[16,8,128]{2,1,0:T(8,128)(2,1)S(1)} %all-to-all-done.refs_3_, bf16[32,128,128]{2,1,0:T(8,128)(2,1)S(1)} %bitcast_multiply_fusion.refs_4_), custom_call_target="tpu_custom_call" | custom-call | tf_op jit(solution)/shard_map/mirror/pallas_call | solution.py:55
  21.4 42.9 %all_to_all.15.refs_3_ = f32[64,8,128]{2,1,0:T(8,128)S(1)} all-to-all(f32[64,8,128]{2,1,0:T(8,128)S(1)} %mirror.1), channel_id=1, replica_groups=mesh['row'=64,'col'=16] {'row'}, dimensions={0} | all-to-all | bytes 524288 | tf_op jit(solution)/shard_map/all_to_all | solution.py:13
  64.3 1.2 %direct.1 = (f32[16,8,128]{2,1,0:T(8,128)S(1)}, f32[8,128]{1,0:T(8,128)S(1)}) custom-call(s32[1,1,32]{2,1,0:T(1,128)S(1)} %copy-done.1, s32[1,1,32]{2,1,0:T(1,128)S(1)} %copy-done.2, bf16[8,128]{1,0:T(8,128)(2,1)S(1)} %copy-done, f32[64,8,128]{2,1,0:T(8,128)S(1)} %all_to_all.15.refs_3_, bf16[32,128,128]{2,1,0:T(8,128)(2,1)S(1)} %bitcast_multiply_fusion.refs_4_), custom_call_target="tpu_custom_call" | custom-call | tf_op jit(solution)/shard_map/direct/pallas_call | solution.py:64
  65.5 13.2 %all_to_all.16 = f32[16,8,128]{2,1,0:T(8,128)S(1)} all-to-all(f32[16,8,128]{2,1,0:T(8,128)S(1)} %get-tuple-element.8), channel_id=1, replica_groups=mesh['row'=64,'col'=16] {'col'}, dimensions={0} | all-to-all | bytes 131072 | tf_op jit(solution)/shard_map/all_to_all | solution.py:13
  78.7 0.6 add.3
  (2 shorter events, 0.0 us)
Async XLA Ops:
  1.3 8.9 %copy-start.3 = (s32[1,1,32]{2,1,0:T(1,128)S(1)}, s32[1,1,32]{2,1,0:T(1,128)}, u32[]{:S(2)}) copy-start(s32[1,1,32]{2,1,0:T(1,128)} %param.9) | copy-start | bytes 388
  1.3 19.2 %all-to-all-start = ((bf16[16,8,128]{2,1,0:T(8,128)(2,1)}), bf16[16,8,128]{2,1,0:T(8,128)(2,1)S(1)}, u32[]{:S(2)}, u32[]{:S(2)}) async-start(bf16[16,8,128]{2,1,0:T(8,128)(2,1)} %broadcast_in_dim.2), calls=%async_computation | async-start | bytes 65536 | tf_op jit(solution)/shard_map/all_to_all | solution.py:13
  10.2 10.3 %copy-start = (bf16[8,128]{1,0:T(8,128)(2,1)S(1)}, bf16[8,128]{1,0:T(8,128)(2,1)}, u32[]{:S(2)}) copy-start(bf16[8,128]{1,0:T(8,128)(2,1)} %refs_2_.3) | copy-start | bytes 6148
  10.2 10.2 %copy-start.1 = (s32[1,1,32]{2,1,0:T(1,128)S(1)}, s32[1,1,32]{2,1,0:T(1,128)}, u32[]{:S(2)}) copy-start(s32[1,1,32]{2,1,0:T(1,128)} %refs_0_.3) | copy-start | bytes 388
  10.2 10.2 %copy-start.2 = (s32[1,1,32]{2,1,0:T(1,128)S(1)}, s32[1,1,32]{2,1,0:T(1,128)}, u32[]{:S(2)}) copy-start(s32[1,1,32]{2,1,0:T(1,128)} %refs_1_.3) | copy-start | bytes 388

commit v4 on v3

--- a/solution.py
+++ b/solution.py
@@ -9,32 +9,35 @@
 VMEM = pl.BlockSpec(memory_space=pltpu.VMEM)
 
 
-def exchange(parts, axis):
-    return lax.all_to_all(parts, axis, 0, 0, tiled=True)
+def exchange(parts, axis, order=None):
+    groups = None if order is None else [order]
+    return lax.all_to_all(parts, axis, 0, 0, tiled=True, axis_index_groups=groups)
 
 
 def mirror_kernel(n_col, rows, cols, vec, row_set, tiles, parts):
     my_row, my_col = lax.axis_index("row"), lax.axis_index("col")
     own = vec[...].astype(jnp.float32)
+    last = parts.shape[0] - 1
     for r in range(parts.shape[0]):
-        parts[r] = jnp.where(r > my_row, own, 0.0)
+        parts[last - r] = jnp.where(r > my_row, own, 0.0)
     for k in range(tiles.shape[0]):
         product = jnp.dot(row_set[rows[0, 0, k]], tiles[k], preferred_element_type=jnp.float32)
         below = my_row * n_col + rows[0, 0, k] > cols[0, 0, k] * n_col + my_col
         weight = jnp.where(below, 1.0, 0.0)
-        parts[cols[0, 0, k]] += product * weight
+        parts[last - cols[0, 0, k]] += product * weight
 
 
 def direct_kernel(n_col, rows, cols, vec, arrived, tiles, parts, mirrored):
     my_row, my_col = lax.axis_index("row"), lax.axis_index("col")
+    last = arrived.shape[0] - 1
     total = jnp.zeros(mirrored.shape, jnp.float32)
     for r in range(arrived.shape[0]):
-        total += jnp.where(r >= my_row, arrived[r], 0.0)
+        total += jnp.where(r >= my_row, arrived[last - r], 0.0)
     mirrored[...] = total
     parts[...] = jnp.zeros_like(parts)
     for k in range(tiles.shape[0]):
         source = cols[0, 0, k]
-        values = jnp.where(source == my_row, vec[...], arrived[source].astype(jnp.bfloat16))
+        values = jnp.where(source == my_row, vec[...], arrived[last - source].astype(jnp.bfloat16))
         product = lax.dot_general(
             values, tiles[k], (((1,), (1,)), ((), ())), preferred_element_type=jnp.float32
         )
@@ -60,7 +63,7 @@
         compiler_params=params,
         name="mirror",
     )(tile_rows, tile_cols, vectors, row_set, blocks)
-    arrived = exchange(outgoing, "row")
+    arrived = exchange(outgoing, "row", list(range(n_row))[::-1])
     direct, mirrored = pl.pallas_call(
         lambda *refs: direct_kernel(n_col, *refs),
         out_shape=[

time: 79.6 us -> 76.3 us (0.959)
  the two profiles are of different devices: /device:TPU:2 before, /device:TPU:64 now
where the time goes in v4:
time: 76.3 us; the launch traced here: 76 us
  blocking collectives  51.8 us (68%)
  starting transfers between devices  9.8 us (13%)
  waiting for transfers between devices  8.84 us (12%)
  Pallas kernels  2.16 us (3%)
  other arithmetic  1.99 us (3%)
  local copies, waits for them, and re-layouts  1.31 us (2%)
    all_to_all x2, blocking collectives, exchange(): lax.all_to_all(parts, axis, 0, 0, tiled=True, axis_index_groups=groups)  51.8 us
    all_to_all x1, starting transfers between devices, exchange(): lax.all_to_all(parts, axis, 0, 0, tiled=True, axis_index_groups=groups)  9.8 us
    all_to_all x1, waiting for transfers between devices, exchange(): lax.all_to_all(parts, axis, 0, 0, tiled=True, axis_index_groups=groups)  8.84 us
  transfers between devices with their start and end apart: 1, of which 1 were waited for; matrix products, arithmetic and copies ran while one was open for 2% of the time, Pallas kernels for 0%

profile of v4, /device:TPU:64, one launch (start us, length us, event | category | flops | bytes accessed | tf_op | source)
XLA Modules:
  0.0 76.0 jit_solution(9549343746773165574)
XLA Ops:
  0.0 1.3 %broadcast_in_dim.2 = bf16[16,8,128]{2,1,0:T(8,128)(2,1)} broadcast(bf16[8,128]{1,0:T(8,128)(2,1)} %refs_2_.3), dimensions={1,2} | broadcast | bytes 34816 | tf_op jit(solution)/shard_map/broadcast_in_dim | solution.py:57
  1.3 0.0 copy-start.3
  1.3 9.8 %all-to-all-start = ((bf16[16,8,128]{2,1,0:T(8,128)(2,1)}), bf16[16,8,128]{2,1,0:T(8,128)(2,1)S(1)}, u32[]{:S(2)}, u32[]{:S(2)}) async-start(bf16[16,8,128]{2,1,0:T(8,128)(2,1)} %broadcast_in_dim.2), calls=%async_computation | async-start | bytes 65536 | tf_op jit(solution)/shard_map/all_to_all | solution.py:14
  11.1 0.0 copy-done.3
  11.1 0.0 copy-start
  11.1 0.0 copy-start.1
  11.1 0.0 copy-start.2
  11.2 1.4 %bitcast_multiply_fusion.refs_4_ = bf16[32,128,128]{2,1,0:T(8,128)(2,1)S(1)} fusion(bf16[1,1,32,128,128]{4,3,2,1,0:T(8,128)(2,1)} %param.6, bf16[32]{0:T(256)(128)(2,1)S(1)} %fusion), kind=kLoop, calls=%fused_computation | loop fusion | flops 524288 | bytes 2097216 | tf_op jit(solution)/shard_map/mul | solution.py:54
  12.5 8.8 %all-to-all-done.refs_3_ = bf16[16,8,128]{2,1,0:T(8,128)(2,1)S(1)} async-done(((bf16[16,8,128]{2,1,0:T(8,128)(2,1)}), bf16[16,8,128]{2,1,0:T(8,128)(2,1)S(1)}, u32[]{:S(2)}, u32[]{:S(2)}) %all-to-all-start) | async-done | bytes 32800 | tf_op jit(solution)/shard_map/all_to_all | solution.py:14
  21.4 0.0 copy-done
  21.4 0.0 copy-done.1
  21.4 0.0 copy-done.2
  21.4 0.9 %mirror.1 = f32[64,8,128]{2,1,0:T(8,128)S(1)} custom-call(s32[1,1,32]{2,1,0:T(1,128)S(1)} %copy-done.1, s32[1,1,32]{2,1,0:T(1,128)S(1)} %copy-done.2, bf16[8,128]{1,0:T(8,128)(2,1)S(1)} %copy-done, bf16[16,8,128]{2,1,0:T(8,128)(2,1)S(1)} %all-to-all-done.refs_3_, bf16[32,128,128]{2,1,0:T(8,128)(2,1)S(1)} %bitcast_multiply_fusion.refs_4_), custom_call_target="tpu_custom_call" | custom-call | tf_op jit(solution)/shard_map/mirror/pallas_call | solution.py:58
  22.3 38.6 %all_to_all.15.refs_3_ = f32[64,8,128]{2,1,0:T(8,128)S(1)} all-to-all(f32[64,8,128]{2,1,0:T(8,128)S(1)} %mirror.1), channel_id=1, replica_groups={{1008,992,976,960,944,928,912,896,880,864,848,832,816,800,784,768,752,7..., dimensions={0} | all-to-all | bytes 524288 | tf_op jit(solution)/shard_map/all_to_all | solution.py:14
  61.0 1.2 %direct.1 = (f32[16,8,128]{2,1,0:T(8,128)S(1)}, f32[8,128]{1,0:T(8,128)S(1)}) custom-call(s32[1,1,32]{2,1,0:T(1,128)S(1)} %copy-done.1, s32[1,1,32]{2,1,0:T(1,128)S(1)} %copy-done.2, bf16[8,128]{1,0:T(8,128)(2,1)S(1)} %copy-done, f32[64,8,128]{2,1,0:T(8,128)S(1)} %all_to_all.15.refs_3_, bf16[32,128,128]{2,1,0:T(8,128)(2,1)S(1)} %bitcast_multiply_fusion.refs_4_), custom_call_target="tpu_custom_call" | custom-call | tf_op jit(solution)/shard_map/direct/pallas_call | solution.py:67
  62.2 13.2 %all_to_all.16 = f32[16,8,128]{2,1,0:T(8,128)S(1)} all-to-all(f32[16,8,128]{2,1,0:T(8,128)S(1)} %get-tuple-element.8), channel_id=1, replica_groups=mesh['row'=64,'col'=16] {'col'}, dimensions={0} | all-to-all | bytes 131072 | tf_op jit(solution)/shard_map/all_to_all | solution.py:14
  75.4 0.6 add.3
  (2 shorter events, 0.0 us)
Async XLA Ops:
  1.3 9.8 %copy-start.3 = (s32[1,1,32]{2,1,0:T(1,128)S(1)}, s32[1,1,32]{2,1,0:T(1,128)}, u32[]{:S(2)}) copy-start(s32[1,1,32]{2,1,0:T(1,128)} %param.9) | copy-start | bytes 388
  1.3 20.1 %all-to-all-start = ((bf16[16,8,128]{2,1,0:T(8,128)(2,1)}), bf16[16,8,128]{2,1,0:T(8,128)(2,1)S(1)}, u32[]{:S(2)}, u32[]{:S(2)}) async-start(bf16[16,8,128]{2,1,0:T(8,128)(2,1)} %broadcast_in_dim.2), calls=%async_computation | async-start | bytes 65536 | tf_op jit(solution)/shard_map/all_to_all | solution.py:14
  11.1 10.3 %copy-start = (bf16[8,128]{1,0:T(8,128)(2,1)S(1)}, bf16[8,128]{1,0:T(8,128)(2,1)}, u32[]{:S(2)}) copy-start(bf16[8,128]{1,0:T(8,128)(2,1)} %refs_2_.3) | copy-start | bytes 6148
  11.1 10.2 %copy-start.1 = (s32[1,1,32]{2,1,0:T(1,128)S(1)}, s32[1,1,32]{2,1,0:T(1,128)}, u32[]{:S(2)}) copy-start(s32[1,1,32]{2,1,0:T(1,128)} %refs_0_.3) | copy-start | bytes 388
  11.1 10.2 %copy-start.2 = (s32[1,1,32]{2,1,0:T(1,128)S(1)}, s32[1,1,32]{2,1,0:T(1,128)}, u32[]{:S(2)}) copy-start(s32[1,1,32]{2,1,0:T(1,128)} %refs_1_.3) | copy-start | bytes 388

commit v5 on v3

v5 whole, which is shorter than its diff:
```python
import jax
import jax.numpy as jnp
from jax import lax
from jax.experimental import pallas as pl
from jax.experimental.pallas import tpu as pltpu
from jax.sharding import PartitionSpec as P

SMEM = pl.BlockSpec(memory_space=pltpu.SMEM)
VMEM = pl.BlockSpec(memory_space=pltpu.VMEM)


def row_sequence(n):
    planes = n // 4
    ring = [p + h for p in range(planes // 2) for h in (0, planes // 2)]
    return [4 * z + q for z in ring for q in range(4)]


def col_sequence(n):
    return [2 * y + x for p in range(n // 4) for y in (p, p + n // 4) for x in range(2)]


def exchange(parts, axis, order):
    return lax.all_to_all(parts, axis, 0, 0, tiled=True, axis_index_groups=[order])


def mirror_kernel(n_col, order, rows, cols, spot, seat, vec, row_set, tiles, parts):
    my_row, my_col = lax.axis_index("row"), lax.axis_index("col")
    own = vec[...].astype(jnp.float32)
    for at, r in enumerate(order):
        parts[at] = jnp.where(r > my_row, own, 0.0)
    for k in range(tiles.shape[0]):
        product = jnp.dot(row_set[seat[rows[0, 0, k]]], tiles[k], preferred_element_type=jnp.float32)
        below = my_row * n_col + rows[0, 0, k] > cols[0, 0, k] * n_col + my_col
        weight = jnp.where(below, 1.0, 0.0)
        parts[spot[cols[0, 0, k]]] += product * weight


def direct_kernel(n_col, order, rows, cols, spot, seat, vec, arrived, tiles, parts, mirrored):
    my_row, my_col = lax.axis_index("row"), lax.axis_index("col")
    total = jnp.zeros(mirrored.shape, jnp.float32)
    for at, r in enumerate(order):
        total += jnp.where(r >= my_row, arrived[at], 0.0)
    mirrored[...] = total
    parts[...] = jnp.zeros_like(parts)
    for k in range(tiles.shape[0]):
        source = cols[0, 0, k]
        values = jnp.where(source == my_row, vec[...], arrived[spot[source]].astype(jnp.bfloat16))
        product = lax.dot_general(
            values, tiles[k], (((1,), (1,)), ((), ())), preferred_element_type=jnp.float32
        )
        below = my_row * n_col + rows[0, 0, k] >= source * n_col + my_col
        weight = jnp.where(below, 1.0, 0.0)
        parts[seat[rows[0, 0, k]]] += product * weight


def body(vectors, tiles, tile_rows, tile_cols, tile_live):
    nvec, seg = vectors.shape
    n_row = lax.axis_size("row")
    n_col = lax.axis_size("col")
    row_order = row_sequence(n_row)
    row_spot = jnp.array([row_order.index(r) for r in range(n_row)], jnp.int32)
    col_order = col_sequence(n_col)
    col_spot = jnp.array([col_order.index(c) for c in range(n_col)], jnp.int32)
    live = (tile_live.reshape(-1, 1, 1) == 1).astype(tiles.dtype)
    blocks = tiles.reshape(-1, 128, 128) * live
    params = pltpu.CompilerParams(vmem_limit_bytes=4 << 20)

    row_set = exchange(jnp.broadcast_to(vectors[None], (n_col, nvec, seg)), "col", col_order)
    outgoing = pl.pallas_call(
        lambda *refs: mirror_kernel(n_col, row_order, *refs),
        out_shape=jax.ShapeDtypeStruct((n_row, nvec, seg), jnp.float32),
        in_specs=[SMEM] * 4 + [VMEM] * 3,
        out_specs=VMEM,
        compiler_params=params,
        name="mirror",
    )(tile_rows, tile_cols, row_spot, col_spot, vectors, row_set, blocks)
    arrived = exchange(outgoing, "row", row_order)
    direct, mirrored = pl.pallas_call(
        lambda *refs: direct_kernel(n_col, row_order, *refs),
        out_shape=[
            jax.ShapeDtypeStruct((n_col, nvec, seg), jnp.float32),
            jax.ShapeDtypeStruct((nvec, seg), jnp.float32),
        ],
        in_specs=[SMEM] * 4 + [VMEM] * 3,
        out_specs=[VMEM, VMEM],
        compiler_params=params,
        name="direct",
    )(tile_rows, tile_cols, row_spot, col_spot, vectors, arrived, blocks)
    straight = exchange(direct, "col", col_order)
    return mirrored + jnp.sum(straight, axis=0)


def solution(mesh):
    return jax.shard_map(
        body,
        mesh=mesh,
        in_specs=(
            P(None, ("row", "col")),
            P("row", "col", None, None, None),
            P("row", "col", None),
            P("row", "col", None),
            P("row", "col", None),
        ),
        out_specs=P(None, ("row", "col")),
        check_vma=False,
    )
```

time: 79.6 us -> 78.4 us (0.985)
  the two profiles are of different devices: /device:TPU:2 before, /device:TPU:64 now
where the time goes in v5:
time: 78.4 us; the launch traced here: 78.1 us
  blocking collectives  53.8 us (69%)
  starting transfers between devices  9.8 us (12%)
  waiting for transfers between devices  8.81 us (11%)
  Pallas kernels  2.2 us (3%)
  other arithmetic  2 us (3%)
  local copies, waits for them, and re-layouts  1.33 us (2%)
    all_to_all x2, blocking collectives, exchange(): lax.all_to_all(parts, axis, 0, 0, tiled=True, axis_index_groups=[order])  53.8 us
    all_to_all x1, starting transfers between devices, exchange(): lax.all_to_all(parts, axis, 0, 0, tiled=True, axis_index_groups=[order])  9.8 us
    all_to_all x1, waiting for transfers between devices, exchange(): lax.all_to_all(parts, axis, 0, 0, tiled=True, axis_index_groups=[order])  8.81 us
  transfers between devices with their start and end apart: 1, of which 1 were waited for; matrix products, arithmetic and copies ran while one was open for 2% of the time, Pallas kernels for 0%

profile of v5, /device:TPU:64, one launch (start us, length us, event | category | flops | bytes accessed | tf_op | source)
XLA Modules:
  0.0 78.1 jit_solution(18239922657612663399)
XLA Ops:
  0.0 1.3 %broadcast_in_dim.2 = bf16[16,8,128]{2,1,0:T(8,128)(2,1)} broadcast(bf16[8,128]{1,0:T(8,128)(2,1)} %refs_4_.3), dimensions={1,2} | broadcast | bytes 34816 | tf_op jit(solution)/shard_map/broadcast_in_dim | solution.py:68
  1.3 0.0 copy-start.5
  1.3 9.8 %all-to-all-start = ((bf16[16,8,128]{2,1,0:T(8,128)(2,1)}), bf16[16,8,128]{2,1,0:T(8,128)(2,1)S(1)}, u32[]{:S(2)}, u32[]{:S(2)}) async-start(bf16[16,8,128]{2,1,0:T(8,128)(2,1)} %broadcast_in_dim.2), calls=%async_computation | async-start | bytes 65536 | tf_op jit(solution)/shard_map/all_to_all | solution.py:23
  11.1 0.0 copy-done.5
  11.1 0.0 copy-start
  11.1 0.0 copy-start.1
  11.2 0.0 copy-start.2
  11.2 0.0 copy-start.3
  11.2 0.0 copy-start.4
  11.2 1.4 %bitcast_multiply_fusion.refs_6_ = bf16[32,128,128]{2,1,0:T(8,128)(2,1)S(1)} fusion(bf16[1,1,32,128,128]{4,3,2,1,0:T(8,128)(2,1)} %param.8, bf16[32]{0:T(256)(128)(2,1)S(1)} %fusion), kind=kLoop, calls=%fused_computation | loop fusion | flops 524288 | bytes 2097216 | tf_op jit(solution)/shard_map/mul | solution.py:65
  12.6 8.8 %all-to-all-done.refs_5_ = bf16[16,8,128]{2,1,0:T(8,128)(2,1)S(1)} async-done(((bf16[16,8,128]{2,1,0:T(8,128)(2,1)}), bf16[16,8,128]{2,1,0:T(8,128)(2,1)S(1)}, u32[]{:S(2)}, u32[]{:S(2)}) %all-to-all-start) | async-done | bytes 32800 | tf_op jit(solution)/shard_map/all_to_all | solution.py:23
  21.4 0.0 copy-done
  21.4 0.0 copy-done.1
  21.4 0.0 copy-done.2
  21.4 0.0 copy-done.3
  21.4 0.0 copy-done.4
  21.4 1.0 %mirror.1 = f32[64,8,128]{2,1,0:T(8,128)S(1)} custom-call(s32[1,1,32]{2,1,0:T(1,128)S(1)} %copy-done.1, s32[1,1,32]{2,1,0:T(1,128)S(1)} %copy-done.2, s32[64]{0:T(128)S(1)} %copy-done.4, s32[16]{0:T(128)S(1)} %copy-done.3, bf16[8,128]{1,0:T(8,128)(2,1)S(1)} %copy-done, bf16[16,8,128]{2,1,0:T(8,128)(2,1)S(1)} %all-to-all-done.refs_5_, ...), custom_call_target="tpu_custom_call" | custom-call | tf_op jit(solution)/shard_map/mirror/pallas_call | solution.py:69
  22.4 40.8 %all_to_all.15.refs_5_ = f32[64,8,128]{2,1,0:T(8,128)S(1)} all-to-all(f32[64,8,128]{2,1,0:T(8,128)S(1)} %mirror.1), channel_id=1, replica_groups={{0,16,32,48,512,528,544,560,64,80,96,112,576,592,608,624,128,144,160,17..., dimensions={0} | all-to-all | bytes 524288 | tf_op jit(solution)/shard_map/all_to_all | solution.py:23
  63.2 1.2 %direct.1 = (f32[16,8,128]{2,1,0:T(8,128)S(1)}, f32[8,128]{1,0:T(8,128)S(1)}) custom-call(s32[1,1,32]{2,1,0:T(1,128)S(1)} %copy-done.1, s32[1,1,32]{2,1,0:T(1,128)S(1)} %copy-done.2, s32[64]{0:T(128)S(1)} %copy-done.4, s32[16]{0:T(128)S(1)} %copy-done.3, bf16[8,128]{1,0:T(8,128)(2,1)S(1)} %copy-done, f32[64,8,128]{2,1,0:T(8,128)S(1)} %all_to_all.15.refs_5_, ...), custom_call_target="tpu_custom_call" | custom-call | tf_op jit(solution)/shard_map/direct/pallas_call | solution.py:78
  64.4 13.1 %all_to_all.16 = f32[16,8,128]{2,1,0:T(8,128)S(1)} all-to-all(f32[16,8,128]{2,1,0:T(8,128)S(1)} %get-tuple-element.8), channel_id=1, replica_groups={{0,1,8,9,2,3,10,11,4,5,12,13,6,7,14,15},{16,17,24,25,18,19,26,27,20,21,..., dimensions={0} | all-to-all | bytes 131072 | tf_op jit(solution)/shard_map/all_to_all | solution.py:23
  77.5 0.6 add.3
  (2 shorter events, 0.0 us)
Async XLA Ops:
  1.3 9.8 %copy-start.5 = (s32[1,1,32]{2,1,0:T(1,128)S(1)}, s32[1,1,32]{2,1,0:T(1,128)}, u32[]{:S(2)}) copy-start(s32[1,1,32]{2,1,0:T(1,128)} %param.11) | copy-start | bytes 388
  1.3 20.1 %all-to-all-start = ((bf16[16,8,128]{2,1,0:T(8,128)(2,1)}), bf16[16,8,128]{2,1,0:T(8,128)(2,1)S(1)}, u32[]{:S(2)}, u32[]{:S(2)}) async-start(bf16[16,8,128]{2,1,0:T(8,128)(2,1)} %broadcast_in_dim.2), calls=%async_computation | async-start | bytes 65536 | tf_op jit(solution)/shard_map/all_to_all | solution.py:23
  11.1 10.3 %copy-start = (bf16[8,128]{1,0:T(8,128)(2,1)S(1)}, bf16[8,128]{1,0:T(8,128)(2,1)}, u32[]{:S(2)}) copy-start(bf16[8,128]{1,0:T(8,128)(2,1)} %refs_4_.3) | copy-start | bytes 6148
  11.1 10.3 %copy-start.1 = (s32[1,1,32]{2,1,0:T(1,128)S(1)}, s32[1,1,32]{2,1,0:T(1,128)}, u32[]{:S(2)}) copy-start(s32[1,1,32]{2,1,0:T(1,128)} %refs_0_.3) | copy-start | bytes 388
  11.2 10.2 %copy-start.2 = (s32[1,1,32]{2,1,0:T(1,128)S(1)}, s32[1,1,32]{2,1,0:T(1,128)}, u32[]{:S(2)}) copy-start(s32[1,1,32]{2,1,0:T(1,128)} %refs_1_.3) | copy-start | bytes 388
  11.2 10.2 %copy-start.3 = (s32[16]{0:T(128)S(1)}, s32[16]{0:T(128)}, u32[]{:S(2)}) copy-start(s32[16]{0:T(128)} %constant.9.clone.refs_3_) | copy-start | bytes 196
  11.2 10.2 %copy-start.4 = (s32[64]{0:T(128)S(1)}, s32[64]{0:T(128)}, u32[]{:S(2)}) copy-start(s32[64]{0:T(128)} %constant.8.clone.refs_2_) | copy-start | bytes 772

commit v6 on v3

v6 whole, which is shorter than its diff:
```python
import jax
import jax.numpy as jnp
from jax import lax
from jax.experimental import pallas as pl
from jax.experimental.pallas import tpu as pltpu
from jax.sharding import PartitionSpec as P

SMEM = pl.BlockSpec(memory_space=pltpu.SMEM)
VMEM = pl.BlockSpec(memory_space=pltpu.VMEM)


def exchange(parts, axes, groups):
    return lax.all_to_all(parts, axes, 0, 0, tiled=True, axis_index_groups=groups)


def mirror_kernel(n_col, spots, lists, other_lists, row_sets, tiles, other_tiles, parts, sums):
    my_row, my_col = lax.axis_index("row"), lax.axis_index("col")
    pair, side = my_row // 2, my_row % 2
    pairs = parts.shape[0]
    sums[...] = jnp.zeros_like(sums)
    for k in range(tiles.shape[0]):
        for who, codes, blocks in ((side, lists, tiles), (1 - side, other_lists, other_tiles)):
            row, col = codes[0, k], codes[1, k]
            values = row_sets[who * n_col + row]
            product = jnp.dot(values, blocks[k], preferred_element_type=jnp.float32)
            below = (2 * pair + who) * n_col + row > col * n_col + my_col
            weight = jnp.where(below & (col % 2 == side) & (codes[2, k] == 1), 1.0, 0.0)
            sums[col // 2] += product * weight
    first, second = row_sets[my_col], row_sets[n_col + my_col]
    for p in range(pairs):
        high = sums[p].astype(jnp.bfloat16)
        low = (sums[p] - high.astype(jnp.float32)).astype(jnp.bfloat16)
        parts[spots[p], 0] = jnp.where(p > pair, first, high)
        parts[spots[p], 1] = jnp.where(p > pair, second, low)


def direct_kernel(n_col, spots, lists, row_sets, arrived, tiles, parts, mirrored):
    my_row, my_col = lax.axis_index("row"), lax.axis_index("col")
    pair = my_row // 2
    total = jnp.zeros(mirrored.shape, jnp.float32)
    for p in range(arrived.shape[0]):
        both = arrived[spots[p], 0].astype(jnp.float32) + arrived[spots[p], 1].astype(jnp.float32)
        total += jnp.where(p >= pair, both, 0.0)
    mirrored[...] = total
    parts[...] = jnp.zeros_like(parts)
    for k in range(tiles.shape[0]):
        row, col = lists[0, k], lists[1, k]
        here = row_sets[col % 2 * n_col + my_col]
        values = jnp.where(col // 2 == pair, here, arrived[spots[col // 2], col % 2])
        product = lax.dot_general(
            values, tiles[k], (((1,), (1,)), ((), ())), preferred_element_type=jnp.float32
        )
        below = my_row * n_col + row >= col * n_col + my_col
        parts[row] += product * jnp.where(below, 1.0, 0.0)


def body(vectors, tiles, tile_rows, tile_cols, tile_live):
    nvec, seg = vectors.shape
    n_row = lax.axis_size("row")
    n_col = lax.axis_size("col")
    pairs = n_row // 2
    sides = [(i, i ^ 1) for i in range(n_row)]
    order = list(range(pairs))[::-1]
    spots = jnp.array([order.index(p) for p in range(pairs)], jnp.int32)
    params = pltpu.CompilerParams(vmem_limit_bytes=4 << 20)

    near = [[p * 2 * n_col + i for i in range(2 * n_col)] for p in range(pairs)]
    row_sets = exchange(jnp.broadcast_to(vectors[None], (2 * n_col, nvec, seg)), ("row", "col"), near)
    lists = jnp.stack([tile_rows.reshape(-1), tile_cols.reshape(-1), tile_live.reshape(-1)])
    other_lists = lax.ppermute(lists, "row", sides)
    blocks = tiles.reshape(-1, 128, 128)
    other_blocks = lax.ppermute(blocks, "row", sides)
    live = (tile_live.reshape(-1, 1, 1) == 1).astype(tiles.dtype)
    blocks = blocks * live

    outgoing = pl.pallas_call(
        lambda *refs: mirror_kernel(n_col, *refs),
        out_shape=jax.ShapeDtypeStruct((pairs, 2, nvec, seg), jnp.bfloat16),
        in_specs=[SMEM] * 3 + [VMEM] * 3,
        out_specs=VMEM,
        scratch_shapes=[pltpu.VMEM((pairs, nvec, seg), jnp.float32)],
        compiler_params=params,
        name="mirror",
    )(spots, lists, other_lists, row_sets, blocks, other_blocks)
    far = [[2 * p + side for p in order] for side in range(2)]
    arrived = exchange(outgoing, "row", far)
    direct, mirrored = pl.pallas_call(
        lambda *refs: direct_kernel(n_col, *refs),
        out_shape=[
            jax.ShapeDtypeStruct((n_col, nvec, seg), jnp.float32),
            jax.ShapeDtypeStruct((nvec, seg), jnp.float32),
        ],
        in_specs=[SMEM] * 2 + [VMEM] * 3,
        out_specs=[VMEM, VMEM],
        compiler_params=params,
        name="direct",
    )(spots, lists, row_sets, arrived, blocks)
    straight = exchange(direct, "col", None)
    return mirrored + jnp.sum(straight, axis=0)


def solution(mesh):
    return jax.shard_map(
        body,
        mesh=mesh,
        in_specs=(
            P(None, ("row", "col")),
            P("row", "col", None, None, None),
            P("row", "col", None),
            P("row", "col", None),
            P("row", "col", None),
        ),
        out_specs=P(None, ("row", "col")),
        check_vma=False,
    )
```

time: 79.6 us -> 75.9 us (0.954)
  blocking collectives: 56.1 us -> 47.2 us
  starting transfers between devices: 8.9 us -> 13.4 us
    all_to_all x2, blocking collectives: 56.1 us -> 47.2 us  [exchange(): lax.all_to_all(parts, axes, 0, 0, tiled=True, axis_index_groups=groups)]
    ppermute x0 -> x2, starting transfers between devices: none -> 4.32 us  [the longest x1 2.41 us: body(): other_lists = lax.ppermute(lists, 'row', sides)]
  transfers between devices with their start and end apart: 1 -> 3, of which waited for: 1 -> 1; matrix products, arithmetic and copies ran while one was open for 2% -> 3% of each run, Pallas kernels for 0% -> 0%
where the time goes in v6:
time: 75.9 us; the launch traced here: 75.5 us
  blocking collectives  47.2 us (62%)
  starting transfers between devices  13.4 us (18%)
  waiting for transfers between devices  8.93 us (12%)
  Pallas kernels  2.66 us (4%)
  other arithmetic  2 us (3%)
  local copies, waits for them, and re-layouts  1.3 us (2%)
    all_to_all x2, blocking collectives, exchange(): lax.all_to_all(parts, axes, 0, 0, tiled=True, axis_index_groups=groups)  47.2 us
    all_to_all x1, starting transfers between devices, exchange(): lax.all_to_all(parts, axes, 0, 0, tiled=True, axis_index_groups=groups)  9.05 us
    all_to_all x1, waiting for transfers between devices, exchange(): lax.all_to_all(parts, axes, 0, 0, tiled=True, axis_index_groups=groups)  8.92 us
    ppermute x1, starting transfers between devices, body(): other_lists = lax.ppermute(lists, 'row', sides)  2.41 us
    ppermute x1, starting transfers between devices, body(): other_blocks = lax.ppermute(blocks, 'row', sides)  1.91 us
  transfers between devices with their start and end apart: 3, of which 1 were waited for; matrix products, arithmetic and copies ran while one was open for 3% of the time, Pallas kernels for 0%

profile of v6, /device:TPU:2, one launch (start us, length us, event | category | flops | bytes accessed | tf_op | source)
XLA Modules:
  0.0 75.5 jit_solution(3213447714965724208)
XLA Ops:
  0.0 1.9 %collective-permute-start.1 = (bf16[32,128,128]{2,1,0:T(8,128)(2,1)}, bf16[32,128,128]{2,1,0:T(8,128)(2,1)S(1)}, u32[]{:S(2)}, u32[]{:S(2)}) collective-permute-start(bf16[32,128,128]{2,1,0:T(8,128)(2,1)} %bitcast.7), channel_id=1, source_target_pairs={{0,16},{16,0},{32,48},{48,32},{64,80},{80,64},{96,112},{112,96},{1... | collective-permute-start | bytes 3145736 | tf_op jit(solution)/shard_map/ppermute | solution.py:72
  1.9 0.0 copy-start.2
  1.9 0.0 copy-start.3
  1.9 0.0 copy-start.4
  1.9 0.6 copy-done.2
  2.6 0.0 copy-done.3
  2.6 0.0 copy-done.4
  2.6 0.0 copy-start.1
  2.6 2.4 %collective-permute-start = (s32[3,32]{1,0:T(4,128)S(1)}, s32[3,32]{1,0:T(4,128)S(1)}, u32[]{:S(2)}, u32[]{:S(2)}) collective-permute-start(s32[3,32]{1,0:T(4,128)S(1)} %pad_add_fusion.refs_1_), channel_id=1, source_target_pairs={{0,16},{16,0},{32,48},{48,32},{64,80},{80,64},{96,112},{112,96},{1... | collective-permute-start | bytes 1160 | tf_op jit(solution)/shard_map/ppermute | solution.py:70
  5.0 0.0 copy-done.1
  5.0 0.6 broadcast_in_dim.2
  5.7 9.1 %all-to-all-start = ((bf16[32,8,128]{2,1,0:T(8,128)(2,1)}), bf16[32,8,128]{2,1,0:T(8,128)(2,1)S(1)}, u32[]{:S(2)}, u32[]{:S(2)}) async-start(bf16[32,8,128]{2,1,0:T(8,128)(2,1)} %broadcast_in_dim.2), calls=%async_computation | async-start | bytes 131072 | tf_op jit(solution)/shard_map/all_to_all | solution.py:13
  14.7 0.0 copy-start
  14.8 1.4 %broadcast_multiply_fusion.refs_4_ = bf16[32,128,128]{2,1,0:T(8,128)(2,1)S(1)} fusion(bf16[32]{0:T(256)(128)(2,1)S(1)} %fusion, bf16[1,1,32,128,128]{4,3,2,1,0:T(8,128)(2,1)} %param.7), kind=kLoop, calls=%fused_computation | loop fusion | flops 524288 | bytes 2097216 | tf_op jit(solution)/shard_map/mul | solution.py:74
  16.1 0.0 collective-permute-done.refs_2_
  16.1 8.9 %all-to-all-done.refs_3_.refs_2_ = bf16[32,8,128]{2,1,0:T(8,128)(2,1)S(1)} async-done(((bf16[32,8,128]{2,1,0:T(8,128)(2,1)}), bf16[32,8,128]{2,1,0:T(8,128)(2,1)S(1)}, u32[]{:S(2)}, u32[]{:S(2)}) %all-to-all-start) | async-done | bytes 65568 | tf_op jit(solution)/shard_map/all_to_all | solution.py:13
  25.1 0.0 collective-permute-done.1.refs_5_
  25.1 0.0 copy-done
  25.1 1.4 %mirror.1 = bf16[32,2,8,128]{3,2,1,0:T(8,128)(2,1)S(1)} custom-call(s32[32]{0:T(128)S(1)} %copy-done, s32[3,32]{1,0:T(4,128)S(1)} %pad_add_fusion.refs_1_, s32[3,32]{1,0:T(4,128)S(1)} %collective-permute-done.refs_2_, bf16[32,8,128]{2,1,0:T(8,128)(2,1)S(1)} %all-to-all-done.refs_3_.refs_2_, bf16[32,128,128]{2,1,0:T(8,128)(2,1)S(1)} %broadcast_multiply_fusion.refs_4_, ...), custom_call_target="tpu_custom_call" | custom-call | tf_op jit(solution)/shard_map/mirror/pallas_call | solution.py:76
  26.5 34.0 %all_to_all.15.refs_3_ = bf16[32,2,8,128]{3,2,1,0:T(8,128)(2,1)S(1)} all-to-all(bf16[32,2,8,128]{3,2,1,0:T(8,128)(2,1)S(1)} %mirror.1), channel_id=1, replica_groups={{992,960,928,896,864,832,800,768,736,704,672,640,608,576,544,512,480,44..., dimensions={0} | all-to-all | bytes 262144 | tf_op jit(solution)/shard_map/all_to_all | solution.py:13
  60.5 1.3 %direct.1 = (f32[16,8,128]{2,1,0:T(8,128)S(1)}, f32[8,128]{1,0:T(8,128)S(1)}) custom-call(s32[32]{0:T(128)S(1)} %copy-done, s32[3,32]{1,0:T(4,128)S(1)} %pad_add_fusion.refs_1_, bf16[32,8,128]{2,1,0:T(8,128)(2,1)S(1)} %all-to-all-done.refs_3_.refs_2_, bf16[32,2,8,128]{3,2,1,0:T(8,128)(2,1)S(1)} %all_to_all.15.refs_3_, ...), custom_call_target="tpu_custom_call" | custom-call | tf_op jit(solution)/shard_map/direct/pallas_call | solution.py:87
  61.7 13.2 %all_to_all.16 = f32[16,8,128]{2,1,0:T(8,128)S(1)} all-to-all(f32[16,8,128]{2,1,0:T(8,128)S(1)} %get-tuple-element.8), channel_id=1, replica_groups=mesh['row'=64,'col'=16] {'col'}, dimensions={0} | all-to-all | bytes 131072 | tf_op jit(solution)/shard_map/all_to_all | solution.py:13
  74.9 0.6 add.3
  (3 shorter events, 0.0 us)
Async XLA Ops:
  0.0 25.1 %collective-permute-start.1 = (bf16[32,128,128]{2,1,0:T(8,128)(2,1)}, bf16[32,128,128]{2,1,0:T(8,128)(2,1)S(1)}, u32[]{:S(2)}, u32[]{:S(2)}) collective-permute-start(bf16[32,128,128]{2,1,0:T(8,128)(2,1)} %bitcast.7), channel_id=1, source_target_pairs={{0,16},{16,0},{32,48},{48,32},{64,80},{80,64},{96,112},{112,96},{1... | collective-permute-start | bytes 3145736 | tf_op jit(solution)/shard_map/ppermute | solution.py:72
  1.9 0.7 copy-start.2
  1.9 0.7 copy-start.3
  1.9 0.7 copy-start.4
  2.6 2.4 %copy-start.1 = (bf16[8,128]{1,0:T(8,128)(2,1)S(1)}, bf16[8,128]{1,0:T(8,128)(2,1)}, u32[]{:S(2)}) copy-start(bf16[8,128]{1,0:T(8,128)(2,1)} %param.6) | copy-start | bytes 6148
  2.6 13.5 %collective-permute-start = (s32[3,32]{1,0:T(4,128)S(1)}, s32[3,32]{1,0:T(4,128)S(1)}, u32[]{:S(2)}, u32[]{:S(2)}) collective-permute-start(s32[3,32]{1,0:T(4,128)S(1)} %pad_add_fusion.refs_1_), channel_id=1, source_target_pairs={{0,16},{16,0},{32,48},{48,32},{64,80},{80,64},{96,112},{112,96},{1... | collective-permute-start | bytes 1160 | tf_op jit(solution)/shard_map/ppermute | solution.py:70
  5.7 19.4 %all-to-all-start = ((bf16[32,8,128]{2,1,0:T(8,128)(2,1)}), bf16[32,8,128]{2,1,0:T(8,128)(2,1)S(1)}, u32[]{:S(2)}, u32[]{:S(2)}) async-start(bf16[32,8,128]{2,1,0:T(8,128)(2,1)} %broadcast_in_dim.2), calls=%async_computation | async-start | bytes 131072 | tf_op jit(solution)/shard_map/all_to_all | solution.py:13
  14.7 10.3 %copy-start = (s32[32]{0:T(128)S(1)}, s32[32]{0:T(128)}, u32[]{:S(2)}) copy-start(s32[32]{0:T(128)} %constant.6.clone.refs_0_) | copy-start | bytes 388

commit v7 on v6

--- a/solution.py
+++ b/solution.py
@@ -13,33 +13,46 @@
     return lax.all_to_all(parts, axes, 0, 0, tiled=True, axis_index_groups=groups)
 
 
-def mirror_kernel(n_col, spots, lists, other_lists, row_sets, tiles, other_tiles, parts, sums):
+def stage_kernel(live, tiles, out):
+    for k in range(tiles.shape[0]):
+        out[k] = jnp.where(live[0, 0, k] == 1, tiles[k], jnp.zeros_like(tiles[k]))
+
+
+def add_mirror(n_col, who, codes, row_sets, tiles, sums):
     my_row, my_col = lax.axis_index("row"), lax.axis_index("col")
     pair, side = my_row // 2, my_row % 2
-    pairs = parts.shape[0]
+    for k in range(tiles.shape[0]):
+        row, col = codes[0, k], codes[1, k]
+        product = jnp.dot(row_sets[who * n_col + row], tiles[k], preferred_element_type=jnp.float32)
+        below = (2 * pair + who) * n_col + row > col * n_col + my_col
+        weight = jnp.where(below & (col % 2 == side) & (codes[2, k] == 1), 1.0, 0.0)
+        sums[col // 2] += product * weight
+
+
+def own_kernel(n_col, lists, row_sets, tiles, sums):
     sums[...] = jnp.zeros_like(sums)
-    for k in range(tiles.shape[0]):
-        for who, codes, blocks in ((side, lists, tiles), (1 - side, other_lists, other_tiles)):
-            row, col = codes[0, k], codes[1, k]
-            values = row_sets[who * n_col + row]
-            product = jnp.dot(values, blocks[k], preferred_element_type=jnp.float32)
-            below = (2 * pair + who) * n_col + row > col * n_col + my_col
-            weight = jnp.where(below & (col % 2 == side) & (codes[2, k] == 1), 1.0, 0.0)
-            sums[col // 2] += product * weight
+    add_mirror(n_col, lax.axis_index("row") % 2, lists, row_sets, tiles, sums)
+
+
+def pair_kernel(n_col, order, other_lists, row_sets, other_tiles, own_sums, parts, sums):
+    my_row, my_col = lax.axis_index("row"), lax.axis_index("col")
+    pair = my_row // 2
+    sums[...] = own_sums[...]
+    add_mirror(n_col, 1 - my_row % 2, other_lists, row_sets, other_tiles, sums)
     first, second = row_sets[my_col], row_sets[n_col + my_col]
-    for p in range(pairs):
+    for at, p in enumerate(order):
         high = sums[p].astype(jnp.bfloat16)
         low = (sums[p] - high.astype(jnp.float32)).astype(jnp.bfloat16)
-        parts[spots[p], 0] = jnp.where(p > pair, first, high)
-        parts[spots[p], 1] = jnp.where(p > pair, second, low)
+        parts[at, 0] = jnp.where(p > pair, first, high)
+        parts[at, 1] = jnp.where(p > pair, second, low)
 
 
-def direct_kernel(n_col, spots, lists, row_sets, arrived, tiles, parts, mirrored):
+def direct_kernel(n_col, order, spots, lists, row_sets, arrived, tiles, parts, mirrored):
     my_row, my_col = lax.axis_index("row"), lax.axis_index("col")
     pair = my_row // 2
     total = jnp.zeros(mirrored.shape, jnp.float32)
-    for p in range(arrived.shape[0]):
-        both = arrived[spots[p], 0].astype(jnp.float32) + arrived[spots[p], 1].astype(jnp.float32)
+    for at, p in enumerate(order):
+        both = arrived[at, 0].astype(jnp.float32) + arrived[at, 1].astype(jnp.float32)
         total += jnp.where(p >= pair, both, 0.0)
     mirrored[...] = total
     parts[...] = jnp.zeros_like(parts)
@@ -70,22 +83,38 @@
     other_lists = lax.ppermute(lists, "row", sides)
     blocks = tiles.reshape(-1, 128, 128)
     other_blocks = lax.ppermute(blocks, "row", sides)
-    live = (tile_live.reshape(-1, 1, 1) == 1).astype(tiles.dtype)
-    blocks = blocks * live
+    blocks = pl.pallas_call(
+        stage_kernel,
+        out_shape=jax.ShapeDtypeStruct(blocks.shape, blocks.dtype),
+        in_specs=[SMEM, VMEM],
+        out_specs=VMEM,
+        compiler_params=params,
+        cost_estimate=pl.CostEstimate(flops=0, bytes_accessed=4 * blocks.size, transcendentals=0),
+        name="stage",
+    )(tile_live, blocks)
 
+    own_sums = pl.pallas_call(
+        lambda *refs: own_kernel(n_col, *refs),
+        out_shape=jax.ShapeDtypeStruct((pairs, nvec, seg), jnp.float32),
+        in_specs=[SMEM, VMEM, VMEM],
+        out_specs=VMEM,
+        compiler_params=params,
+        cost_estimate=pl.CostEstimate(flops=10**10, bytes_accessed=2 * blocks.size, transcendentals=0),
+        name="own",
+    )(lists, row_sets, blocks)
     outgoing = pl.pallas_call(
-        lambda *refs: mirror_kernel(n_col, *refs),
+        lambda *refs: pair_kernel(n_col, order, *refs),
         out_shape=jax.ShapeDtypeStruct((pairs, 2, nvec, seg), jnp.bfloat16),
-        in_specs=[SMEM] * 3 + [VMEM] * 3,
+        in_specs=[SMEM] + [VMEM] * 3,
         out_specs=VMEM,
         scratch_shapes=[pltpu.VMEM((pairs, nvec, seg), jnp.float32)],
         compiler_params=params,
-        name="mirror",
-    )(spots, lists, other_lists, row_sets, blocks, other_blocks)
+        name="pair",
+    )(other_lists, row_sets, other_blocks, own_sums)
     far = [[2 * p + side for p in order] for side in range(2)]
     arrived = exchange(outgoing, "row", far)
     direct, mirrored = pl.pallas_call(
-        lambda *refs: direct_kernel(n_col, *refs),
+        lambda *refs: direct_kernel(n_col, order, *refs),
         out_shape=[
             jax.ShapeDtypeStruct((n_col, nvec, seg), jnp.float32),
             jax.ShapeDtypeStruct((nvec, seg), jnp.float32),

time: 75.9 us -> 75.3 us (level)
  waiting for transfers between devices: 8.93 us -> 3.28 us
  blocking collectives: 47.2 us -> 50.3 us
  local copies, waits for them, and re-layouts: 1.3 us -> 3.2 us
  other arithmetic: 2 us -> 0.63 us
  Pallas kernels: 2.66 us -> 4 us
    all_to_all x1, waiting for transfers between devices: 8.92 us -> 3.27 us  [exchange(): lax.all_to_all(parts, axes, 0, 0, tiled=True, axis_index_groups=groups)]
    all_to_all x2, blocking collectives: 47.2 us -> 50.3 us  [exchange(): lax.all_to_all(parts, axes, 0, 0, tiled=True, axis_index_groups=groups)]
    mul x1 -> x0, other arithmetic: 1.36 us -> none  [body(): blocks = blocks * live]
    pallas_call x2 -> x4, Pallas kernels: 2.66 us -> 4 us  [the longest x1 1.25 us: body(): pl.pallas_call(lambda *refs: direct_kernel(n_col, order, *refs), out_shap...]
    unnamed x10, local copies, waits for them, and re-layouts: 0.67 us -> 1.89 us
  transfers between devices with their start and end apart: 3 -> 3, of which waited for: 1 -> 1; matrix products, arithmetic and copies ran while one was open for 3% -> 0% of each run, Pallas kernels for 0% -> 2%
where the time goes in v7:
time: 75.3 us; the launch traced here: 74.9 us
  blocking collectives  50.3 us (67%)
  starting transfers between devices  13.4 us (18%)
  Pallas kernels  4 us (5%)
  waiting for transfers between devices  3.28 us (4%)
  local copies, waits for them, and re-layouts  3.2 us (4%)
    all_to_all x2, blocking collectives, exchange(): lax.all_to_all(parts, axes, 0, 0, tiled=True, axis_index_groups=groups)  50.3 us
    all_to_all x1, starting transfers between devices, exchange(): lax.all_to_all(parts, axes, 0, 0, tiled=True, axis_index_groups=groups)  9.05 us
    all_to_all x1, waiting for transfers between devices, exchange(): lax.all_to_all(parts, axes, 0, 0, tiled=True, axis_index_groups=groups)  3.27 us
    ppermute x1, starting transfers between devices, body(): other_blocks = lax.ppermute(blocks, 'row', sides)  2.19 us
    ppermute x1, starting transfers between devices, body(): other_lists = lax.ppermute(lists, 'row', sides)  2.14 us
    unnamed x10, local copies, waits for them, and re-layouts  1.89 us
  transfers between devices with their start and end apart: 3, of which 1 were waited for; matrix products, arithmetic and copies ran while one was open for 0% of the time, Pallas kernels for 2%

profile of v7, /device:TPU:2, one launch (start us, length us, event | category | flops | bytes accessed | tf_op | source)
XLA Modules:
  0.0 74.9 jit_solution(5015069149433836482)
XLA Ops:
  0.0 1.3 %broadcast_in_dim.2 = bf16[32,8,128]{2,1,0:T(8,128)(2,1)} broadcast(bf16[8,128]{1,0:T(8,128)(2,1)} %param.6), dimensions={1,2} | broadcast | bytes 67584 | tf_op jit(solution)/shard_map/broadcast_in_dim | solution.py:81
  1.3 9.1 %all-to-all-start = ((bf16[32,8,128]{2,1,0:T(8,128)(2,1)}), bf16[32,8,128]{2,1,0:T(8,128)(2,1)S(1)}, u32[]{:S(2)}, u32[]{:S(2)}) async-start(bf16[32,8,128]{2,1,0:T(8,128)(2,1)} %broadcast_in_dim.2), calls=%async_computation | async-start | bytes 131072 | tf_op jit(solution)/shard_map/all_to_all | solution.py:13
  10.4 2.2 %collective-permute-start.1 = (bf16[32,128,128]{2,1,0:T(8,128)(2,1)}, bf16[32,128,128]{2,1,0:T(8,128)(2,1)S(1)}, u32[]{:S(2)}, u32[]{:S(2)}) collective-permute-start(bf16[32,128,128]{2,1,0:T(8,128)(2,1)} %bitcast.4), channel_id=1, source_target_pairs={{0,16},{16,0},{32,48},{48,32},{64,80},{80,64},{96,112},{112,96},{1... | collective-permute-start | bytes 3145736 | tf_op jit(solution)/shard_map/ppermute | solution.py:85
  12.6 0.0 copy-start.1
  12.6 0.0 copy-start.3
  12.6 0.0 copy-start.4
  12.6 0.6 copy-done.1
  13.2 0.0 copy-done.3
  13.2 0.0 copy-done.4
  13.3 2.1 %collective-permute-start = (s32[3,32]{1,0:T(4,128)S(1)}, s32[3,32]{1,0:T(4,128)S(1)}, u32[]{:S(2)}, u32[]{:S(2)}) collective-permute-start(s32[3,32]{1,0:T(4,128)S(1)} %pad_add_fusion.refs_0_.refs_1_), channel_id=1, source_target_pairs={{0,16},{16,0},{32,48},{48,32},{64,80},{80,64},{96,112},{112,96},{1... | collective-permute-start | bytes 1160 | tf_op jit(solution)/shard_map/ppermute | solution.py:83
  15.4 0.0 copy-start
  15.4 1.2 %copy-done = bf16[1,1,32,128,128]{4,3,2,1,0:T(8,128)(2,1)S(1)} copy-done((bf16[1,1,32,128,128]{4,3,2,1,0:T(8,128)(2,1)S(1)}, bf16[1,1,32,128,128]{4,3,2,1,0:T(8,128)(2,1)}, u32[]{:S(2)}) %copy-start) | copy-done | bytes 1048600
  16.6 0.8 %stage.1.refs_2_.refs_4_ = bf16[32,128,128]{2,1,0:T(8,128)(2,1)S(1)} custom-call(s32[1,1,32]{2,1,0:T(1,128)S(1)} %copy-done.1, bf16[32,128,128]{2,1,0:T(8,128)(2,1)S(1)} %bitcast.5), custom_call_target="tpu_custom_call" | custom-call | bytes 2097152 | tf_op jit(solution)/shard_map/stage/pallas_call | solution.py:86
  17.4 3.3 %all-to-all-done.refs_1_.refs_2_ = bf16[32,8,128]{2,1,0:T(8,128)(2,1)S(1)} async-done(((bf16[32,8,128]{2,1,0:T(8,128)(2,1)}), bf16[32,8,128]{2,1,0:T(8,128)(2,1)S(1)}, u32[]{:S(2)}, u32[]{:S(2)}) %all-to-all-start) | async-done | bytes 65568 | tf_op jit(solution)/shard_map/all_to_all | solution.py:13
  20.7 1.0 %own.1.refs_3_ = f32[32,8,128]{2,1,0:T(8,128)S(1)} custom-call(s32[3,32]{1,0:T(4,128)S(1)} %pad_add_fusion.refs_0_.refs_1_, bf16[32,8,128]{2,1,0:T(8,128)(2,1)S(1)} %all-to-all-done.refs_1_.refs_2_, bf16[32,128,128]{2,1,0:T(8,128)(2,1)S(1)} %stage.1.refs_2_.refs_4_), custom_call_target="tpu_custom_call" | custom-call | flops 10000000000 | bytes 1048576 | tf_op jit(solution)/shard_map/own/pallas_call | solution.py:96
  21.7 0.0 collective-permute-done.refs_0_
  21.7 0.0 collective-permute-done.1.refs_2_
  21.7 1.0 %pair.1 = bf16[32,2,8,128]{3,2,1,0:T(8,128)(2,1)S(1)} custom-call(s32[3,32]{1,0:T(4,128)S(1)} %collective-permute-done.refs_0_, bf16[32,8,128]{2,1,0:T(8,128)(2,1)S(1)} %all-to-all-done.refs_1_.refs_2_, bf16[32,128,128]{2,1,0:T(8,128)(2,1)S(1)} %collective-permute-done.1.refs_2_, f32[32,8,128]{2,1,0:T(8,128)S(1)} %own.1.refs_3_), custom_call_target="tpu_custom_call" | custom-call | tf_op jit(solution)/shard_map/pair/pallas_call | solution.py:105
  22.7 0.0 copy-start.2
  22.7 34.0 %all_to_all.15.refs_3_ = bf16[32,2,8,128]{3,2,1,0:T(8,128)(2,1)S(1)} all-to-all(bf16[32,2,8,128]{3,2,1,0:T(8,128)(2,1)S(1)} %pair.1), channel_id=1, replica_groups={{992,960,928,896,864,832,800,768,736,704,672,640,608,576,544,512,480,44..., dimensions={0} | all-to-all | bytes 262144 | tf_op jit(solution)/shard_map/all_to_all | solution.py:13
  56.7 0.0 copy-done.2
  56.7 1.2 %direct.1 = (f32[16,8,128]{2,1,0:T(8,128)S(1)}, f32[8,128]{1,0:T(8,128)S(1)}) custom-call(s32[32]{0:T(128)S(1)} %copy-done.2, s32[3,32]{1,0:T(4,128)S(1)} %pad_add_fusion.refs_0_.refs_1_, bf16[32,8,128]{2,1,0:T(8,128)(2,1)S(1)} %all-to-all-done.refs_1_.refs_2_, bf16[32,2,8,128]{3,2,1,0:T(8,128)(2,1)S(1)} %all_to_all.15.refs_3_, ...), custom_call_target="tpu_custom_call" | custom-call | tf_op jit(solution)/shard_map/direct/pallas_call | solution.py:116
  57.9 16.4 %all_to_all.16 = f32[16,8,128]{2,1,0:T(8,128)S(1)} all-to-all(f32[16,8,128]{2,1,0:T(8,128)S(1)} %get-tuple-element.8), channel_id=1, replica_groups=mesh['row'=64,'col'=16] {'col'}, dimensions={0} | all-to-all | bytes 131072 | tf_op jit(solution)/shard_map/all_to_all | solution.py:13
  74.3 0.6 add.3
  (2 shorter events, 0.0 us)
Async XLA Ops:
  1.3 19.4 %all-to-all-start = ((bf16[32,8,128]{2,1,0:T(8,128)(2,1)}), bf16[32,8,128]{2,1,0:T(8,128)(2,1)S(1)}, u32[]{:S(2)}, u32[]{:S(2)}) async-start(bf16[32,8,128]{2,1,0:T(8,128)(2,1)} %broadcast_in_dim.2), calls=%async_computation | async-start | bytes 131072 | tf_op jit(solution)/shard_map/all_to_all | solution.py:13
  10.4 11.3 %collective-permute-start.1 = (bf16[32,128,128]{2,1,0:T(8,128)(2,1)}, bf16[32,128,128]{2,1,0:T(8,128)(2,1)S(1)}, u32[]{:S(2)}, u32[]{:S(2)}) collective-permute-start(bf16[32,128,128]{2,1,0:T(8,128)(2,1)} %bitcast.4), channel_id=1, source_target_pairs={{0,16},{16,0},{32,48},{48,32},{64,80},{80,64},{96,112},{112,96},{1... | collective-permute-start | bytes 3145736 | tf_op jit(solution)/shard_map/ppermute | solution.py:85
  12.6 0.7 copy-start.1
  12.6 0.7 copy-start.3
  12.6 0.7 copy-start.4
  13.3 8.4 %collective-permute-start = (s32[3,32]{1,0:T(4,128)S(1)}, s32[3,32]{1,0:T(4,128)S(1)}, u32[]{:S(2)}, u32[]{:S(2)}) collective-permute-start(s32[3,32]{1,0:T(4,128)S(1)} %pad_add_fusion.refs_0_.refs_1_), channel_id=1, source_target_pairs={{0,16},{16,0},{32,48},{48,32},{64,80},{80,64},{96,112},{112,96},{1... | collective-permute-start | bytes 1160 | tf_op jit(solution)/shard_map/ppermute | solution.py:83
  15.4 1.2 %copy-start = (bf16[1,1,32,128,128]{4,3,2,1,0:T(8,128)(2,1)S(1)}, bf16[1,1,32,128,128]{4,3,2,1,0:T(8,128)(2,1)}, u32[]{:S(2)}) copy-start(bf16[1,1,32,128,128]{4,3,2,1,0:T(8,128)(2,1)} %param.7) | copy-start | bytes 3145732
  22.7 34.0 %copy-start.2 = (s32[32]{0:T(128)S(1)}, s32[32]{0:T(128)}, u32[]{:S(2)}) copy-start(s32[32]{0:T(128)} %constant.4.clone.refs_0_) | copy-start | bytes 388

commit v8 on v7

v8 whole, which is shorter than its diff:
```python
import jax
import jax.numpy as jnp
from jax import lax
from jax.experimental import pallas as pl
from jax.experimental.pallas import tpu as pltpu
from jax.sharding import PartitionSpec as P

SMEM = pl.BlockSpec(memory_space=pltpu.SMEM)
VMEM = pl.BlockSpec(memory_space=pltpu.VMEM)


def exchange(parts, axes, groups):
    return lax.all_to_all(parts, axes, 0, 0, tiled=True, axis_index_groups=groups)


def stage_kernel(lists, tiles, out, notes, sem):
    count = tiles.shape[0]
    notes[...] = jnp.zeros_like(notes)
    notes[pl.ds(0, lists.shape[0]), pl.ds(0, count)] = lists[...].astype(jnp.float32)
    out[count] = notes[...].astype(out.dtype)
    copy = pltpu.make_async_copy(tiles, out.at[pl.ds(0, count)], sem)
    copy.start()
    copy.wait()


def add_mirror(n_col, who, slot, count, row_sets, tiles, sums):
    my_row, my_col = lax.axis_index("row"), lax.axis_index("col")
    pair, side = my_row // 2, my_row % 2
    for k in range(count):
        row, col, live = slot(k)
        product = jnp.dot(row_sets[who * n_col + row], tiles[k], preferred_element_type=jnp.float32)
        below = (2 * pair + who) * n_col + row > col * n_col + my_col
        weight = jnp.where(below & (col % 2 == side) & (live == 1), 1.0, 0.0)
        sums[col // 2] += product * weight


def own_kernel(n_col, lists, row_sets, staged, sums):
    sums[...] = jnp.zeros_like(sums)
    slot = lambda k: (lists[0, k], lists[1, k], lists[2, k])
    add_mirror(n_col, lax.axis_index("row") % 2, slot, lists.shape[1], row_sets, staged, sums)


def pair_kernel(n_col, order, row_sets, other, own_sums, parts, sums, page, notes, sem):
    count = other.shape[0] - 1
    page[...] = other[count, pl.ds(0, page.shape[0]), :].astype(jnp.float32).astype(jnp.int32)
    copy = pltpu.make_async_copy(page, notes, sem)
    copy.start()
    my_row, my_col = lax.axis_index("row"), lax.axis_index("col")
    pair = my_row // 2
    sums[...] = own_sums[...]
    copy.wait()
    slot = lambda k: (notes[0, k], notes[1, k], notes[2, k])
    add_mirror(n_col, 1 - my_row % 2, slot, count, row_sets, other, sums)
    first, second = row_sets[my_col], row_sets[n_col + my_col]
    for at, p in enumerate(order):
        high = sums[p].astype(jnp.bfloat16)
        low = (sums[p] - high.astype(jnp.float32)).astype(jnp.bfloat16)
        parts[at, 0] = jnp.where(p > pair, first, high)
        parts[at, 1] = jnp.where(p > pair, second, low)


def direct_kernel(n_col, order, spots, lists, row_sets, arrived, staged, parts, mirrored):
    my_row, my_col = lax.axis_index("row"), lax.axis_index("col")
    pair = my_row // 2
    total = jnp.zeros(mirrored.shape, jnp.float32)
    for at, p in enumerate(order):
        both = arrived[at, 0].astype(jnp.float32) + arrived[at, 1].astype(jnp.float32)
        total += jnp.where(p >= pair, both, 0.0)
    mirrored[...] = total
    parts[...] = jnp.zeros_like(parts)
    for k in range(lists.shape[1]):
        row, col = lists[0, k], lists[1, k]
        here = row_sets[col % 2 * n_col + my_col]
        values = jnp.where(col // 2 == pair, here, arrived[spots[col // 2], col % 2])
        product = lax.dot_general(
            values, staged[k], (((1,), (1,)), ((), ())), preferred_element_type=jnp.float32
        )
        below = my_row * n_col + row >= col * n_col + my_col
        parts[row] += product * jnp.where(below & (lists[2, k] == 1), 1.0, 0.0)


def body(vectors, tiles, tile_rows, tile_cols, tile_live):
    nvec, seg = vectors.shape
    n_row = lax.axis_size("row")
    n_col = lax.axis_size("col")
    pairs = n_row // 2
    sides = [(i, i ^ 1) for i in range(n_row)]
    order = list(range(pairs))[::-1]
    spots = jnp.array([order.index(p) for p in range(pairs)], jnp.int32)
    params = pltpu.CompilerParams(vmem_limit_bytes=4 << 20)

    near = [[p * 2 * n_col + i for i in range(2 * n_col)] for p in range(pairs)]
    row_sets = exchange(jnp.broadcast_to(vectors[None], (2 * n_col, nvec, seg)), ("row", "col"), near)
    blocks = tiles.reshape(-1, 128, 128)
    count = blocks.shape[0]
    lists = jnp.stack([slots.reshape(-1) for slots in (tile_rows, tile_cols, tile_live)])
    staged = pl.pallas_call(
        stage_kernel,
        out_shape=jax.ShapeDtypeStruct((count + 1, 128, 128), blocks.dtype),
        in_specs=[VMEM] * 2,
        out_specs=VMEM,
        scratch_shapes=[pltpu.VMEM((128, 128), jnp.float32), pltpu.SemaphoreType.DMA],
        compiler_params=params,
        cost_estimate=pl.CostEstimate(flops=0, bytes_accessed=4 * blocks.size, transcendentals=0),
        name="stage",
    )(lists, blocks)
    other = lax.ppermute(staged, "row", sides)

    own_sums = pl.pallas_call(
        lambda *refs: own_kernel(n_col, *refs),
        out_shape=jax.ShapeDtypeStruct((pairs, nvec, seg), jnp.float32),
        in_specs=[SMEM] + [VMEM] * 2,
        out_specs=VMEM,
        compiler_params=params,
        cost_estimate=pl.CostEstimate(flops=10**11, bytes_accessed=2 * blocks.size, transcendentals=0),
        name="own",
    )(lists, row_sets, staged)
    outgoing = pl.pallas_call(
        lambda *refs: pair_kernel(n_col, order, *refs),
        out_shape=jax.ShapeDtypeStruct((pairs, 2, nvec, seg), jnp.bfloat16),
        in_specs=[VMEM] * 3,
        out_specs=VMEM,
        scratch_shapes=[
            pltpu.VMEM((pairs, nvec, seg), jnp.float32),
            pltpu.VMEM((16, 128), jnp.int32),
            pltpu.SMEM((16, 128), jnp.int32),
            pltpu.SemaphoreType.DMA,
        ],
        compiler_params=params,
        name="pair",
    )(row_sets, other, own_sums)
    far = [[2 * p + side for p in order] for side in range(2)]
    arrived = exchange(outgoing, "row", far)
    direct, mirrored = pl.pallas_call(
        lambda *refs: direct_kernel(n_col, order, *refs),
        out_shape=[
            jax.ShapeDtypeStruct((n_col, nvec, seg), jnp.float32),
            jax.ShapeDtypeStruct((nvec, seg), jnp.float32),
        ],
        in_specs=[SMEM] * 2 + [VMEM] * 3,
        out_specs=[VMEM, VMEM],
        compiler_params=params,
        name="direct",
    )(spots, lists, row_sets, arrived, staged)
    straight = exchange(direct, "col", None)
    return mirrored + jnp.sum(straight, axis=0)


def solution(mesh):
    return jax.shard_map(
        body,
        mesh=mesh,
        in_specs=(
            P(None, ("row", "col")),
            P("row", "col", None, None, None),
            P("row", "col", None),
            P("row", "col", None),
            P("row", "col", None),
        ),
        out_specs=P(None, ("row", "col")),
        check_vma=False,
    )
```

time: 75.3 us -> 73.9 us (0.981)
  waiting for transfers between devices: 3.28 us -> 6.11 us
  starting transfers between devices: 13.4 us -> 11.2 us
  blocking collectives: 50.3 us -> 48.9 us
    all_to_all x1, waiting for transfers between devices: 3.27 us -> 6.11 us  [exchange(): lax.all_to_all(parts, axes, 0, 0, tiled=True, axis_index_groups=groups)]
    ppermute x2 -> x1, starting transfers between devices: 4.33 us -> 2.19 us  [body(): other = lax.ppermute(staged, 'row', sides)]
    all_to_all x2, blocking collectives: 50.3 us -> 48.9 us  [exchange(): lax.all_to_all(parts, axes, 0, 0, tiled=True, axis_index_groups=groups)]
    unnamed x10 -> x4, local copies, waits for them, and re-layouts: 1.89 us -> 1.23 us
  transfers between devices with their start and end apart: 3 -> 2, of which waited for: 1 -> 1; matrix products, arithmetic and copies ran while one was open for 0% -> 1% of each run, Pallas kernels for 2% -> 1%
where the time goes in v8:
time: 73.9 us; the launch traced here: 73.6 us
  blocking collectives  48.9 us (66%)
  starting transfers between devices  11.2 us (15%)
  waiting for transfers between devices  6.11 us (8%)
  Pallas kernels  3.45 us (5%)
  local copies, waits for them, and re-layouts  2.53 us (3%)
  other arithmetic  1.32 us (2%)
    all_to_all x2, blocking collectives, exchange(): lax.all_to_all(parts, axes, 0, 0, tiled=True, axis_index_groups=groups)  48.9 us
    all_to_all x1, starting transfers between devices, exchange(): lax.all_to_all(parts, axes, 0, 0, tiled=True, axis_index_groups=groups)  9.05 us
    all_to_all x1, waiting for transfers between devices, exchange(): lax.all_to_all(parts, axes, 0, 0, tiled=True, axis_index_groups=groups)  6.11 us
    ppermute x1, starting transfers between devices, body(): other = lax.ppermute(staged, 'row', sides)  2.19 us
  transfers between devices with their start and end apart: 2, of which 1 were waited for; matrix products, arithmetic and copies ran while one was open for 1% of the time, Pallas kernels for 1%

profile of v8, /device:TPU:2, one launch (start us, length us, event | category | flops | bytes accessed | tf_op | source)
XLA Modules:
  0.0 73.6 jit_solution(13492381121101772293)
XLA Ops:
  0.0 1.3 %broadcast_in_dim.2 = bf16[32,8,128]{2,1,0:T(8,128)(2,1)} broadcast(bf16[8,128]{1,0:T(8,128)(2,1)} %param.6), dimensions={1,2} | broadcast | bytes 67584 | tf_op jit(solution)/shard_map/broadcast_in_dim | solution.py:93
  1.3 9.1 %all-to-all-start = ((bf16[32,8,128]{2,1,0:T(8,128)(2,1)}), bf16[32,8,128]{2,1,0:T(8,128)(2,1)S(1)}, u32[]{:S(2)}, u32[]{:S(2)}) async-start(bf16[32,8,128]{2,1,0:T(8,128)(2,1)} %broadcast_in_dim.2), calls=%async_computation | async-start | bytes 131072 | tf_op jit(solution)/shard_map/all_to_all | solution.py:13
  10.4 0.7 pad_add_fusion.lists.refs_0_.refs_1_
  11.1 0.0 copy-start
  11.1 1.2 %copy-done = bf16[1,1,32,128,128]{4,3,2,1,0:T(8,128)(2,1)S(1)} copy-done((bf16[1,1,32,128,128]{4,3,2,1,0:T(8,128)(2,1)S(1)}, bf16[1,1,32,128,128]{4,3,2,1,0:T(8,128)(2,1)}, u32[]{:S(2)}) %copy-start) | copy-done | bytes 1048600
  12.3 0.1 stage.1.refs_2_.refs_4_
  12.4 2.2 %collective-permute-start = (bf16[33,128,128]{2,1,0:T(8,128)(2,1)S(1)}, bf16[33,128,128]{2,1,0:T(8,128)(2,1)S(1)}, u32[]{:S(2)}, u32[]{:S(2)}) collective-permute-start(bf16[33,128,128]{2,1,0:T(8,128)(2,1)S(1)} %stage.1.refs_2_.refs_4_), channel_id=1, source_target_pairs={{0,16},{16,0},{32,48},{48,32},{64,80},{80,64},{96,112},{112,96},{1... | collective-permute-start | bytes 3244040 | tf_op jit(solution)/shard_map/ppermute | solution.py:107
  14.6 6.1 %all-to-all-done.refs_1_.refs_0_.refs_2_ = bf16[32,8,128]{2,1,0:T(8,128)(2,1)S(1)} async-done(((bf16[32,8,128]{2,1,0:T(8,128)(2,1)}), bf16[32,8,128]{2,1,0:T(8,128)(2,1)S(1)}, u32[]{:S(2)}, u32[]{:S(2)}) %all-to-all-start) | async-done | bytes 65568 | tf_op jit(solution)/shard_map/all_to_all | solution.py:13
  20.7 1.0 %own.1.refs_2_ = f32[32,8,128]{2,1,0:T(8,128)S(1)} custom-call(s32[3,32]{1,0:T(4,128)S(1)} %pad_add_fusion.lists.refs_0_.refs_1_, bf16[32,8,128]{2,1,0:T(8,128)(2,1)S(1)} %all-to-all-done.refs_1_.refs_0_.refs_2_, bf16[33,128,128]{2,1,0:T(8,128)(2,1)S(1)} %stage.1.refs_2_.refs_4_), custom_call_target="tpu_custom_call" | custom-call | flops 99999997952 | bytes 1048576 | tf_op jit(solution)/shard_map/own/pallas_call | solution.py:109
  21.7 0.0 copy-start.1
  21.7 0.0 collective-permute-done.refs_1_
  21.7 1.1 %pair.1 = bf16[32,2,8,128]{3,2,1,0:T(8,128)(2,1)S(1)} custom-call(bf16[32,8,128]{2,1,0:T(8,128)(2,1)S(1)} %all-to-all-done.refs_1_.refs_0_.refs_2_, bf16[33,128,128]{2,1,0:T(8,128)(2,1)S(1)} %collective-permute-done.refs_1_, f32[32,8,128]{2,1,0:T(8,128)S(1)} %own.1.refs_2_), custom_call_target="tpu_custom_call" | custom-call | tf_op jit(solution)/shard_map/pair/pallas_call | solution.py:118
  22.8 34.0 %all_to_all.15.refs_3_ = bf16[32,2,8,128]{3,2,1,0:T(8,128)(2,1)S(1)} all-to-all(bf16[32,2,8,128]{3,2,1,0:T(8,128)(2,1)S(1)} %pair.1), channel_id=1, replica_groups={{992,960,928,896,864,832,800,768,736,704,672,640,608,576,544,512,480,44..., dimensions={0} | all-to-all | bytes 262144 | tf_op jit(solution)/shard_map/all_to_all | solution.py:13
  56.8 0.0 copy-done.1
  56.8 1.2 %direct.1 = (f32[16,8,128]{2,1,0:T(8,128)S(1)}, f32[8,128]{1,0:T(8,128)S(1)}) custom-call(s32[32]{0:T(128)S(1)} %copy-done.1, s32[3,32]{1,0:T(4,128)S(1)} %pad_add_fusion.lists.refs_0_.refs_1_, bf16[32,8,128]{2,1,0:T(8,128)(2,1)S(1)} %all-to-all-done.refs_1_.refs_0_.refs_2_, bf16[32,2,8,128]{3,2,1,0:T(8,128)(2,1)S(1)} %all_to_all.15.refs_3_, ...), custom_call_target="tpu_custom_call" | custom-call | tf_op jit(solution)/shard_map/direct/pallas_call | solution.py:134
  58.1 14.9 %all_to_all.16 = f32[16,8,128]{2,1,0:T(8,128)S(1)} all-to-all(f32[16,8,128]{2,1,0:T(8,128)S(1)} %get-tuple-element.8), channel_id=1, replica_groups=mesh['row'=64,'col'=16] {'col'}, dimensions={0} | all-to-all | bytes 131072 | tf_op jit(solution)/shard_map/all_to_all | solution.py:13
  73.0 0.6 add.3
  (1 shorter events, 0.0 us)
Async XLA Ops:
  1.3 19.4 %all-to-all-start = ((bf16[32,8,128]{2,1,0:T(8,128)(2,1)}), bf16[32,8,128]{2,1,0:T(8,128)(2,1)S(1)}, u32[]{:S(2)}, u32[]{:S(2)}) async-start(bf16[32,8,128]{2,1,0:T(8,128)(2,1)} %broadcast_in_dim.2), calls=%async_computation | async-start | bytes 131072 | tf_op jit(solution)/shard_map/all_to_all | solution.py:13
  11.1 1.2 %copy-start = (bf16[1,1,32,128,128]{4,3,2,1,0:T(8,128)(2,1)S(1)}, bf16[1,1,32,128,128]{4,3,2,1,0:T(8,128)(2,1)}, u32[]{:S(2)}) copy-start(bf16[1,1,32,128,128]{4,3,2,1,0:T(8,128)(2,1)} %param.7) | copy-start | bytes 3145732
  12.4 9.3 %collective-permute-start = (bf16[33,128,128]{2,1,0:T(8,128)(2,1)S(1)}, bf16[33,128,128]{2,1,0:T(8,128)(2,1)S(1)}, u32[]{:S(2)}, u32[]{:S(2)}) collective-permute-start(bf16[33,128,128]{2,1,0:T(8,128)(2,1)S(1)} %stage.1.refs_2_.refs_4_), channel_id=1, source_target_pairs={{0,16},{16,0},{32,48},{48,32},{64,80},{80,64},{96,112},{112,96},{1... | collective-permute-start | bytes 3244040 | tf_op jit(solution)/shard_map/ppermute | solution.py:107
  21.7 35.1 %copy-start.1 = (s32[32]{0:T(128)S(1)}, s32[32]{0:T(128)}, u32[]{:S(2)}) copy-start(s32[32]{0:T(128)} %constant.4.clone.refs_0_) | copy-start | bytes 388

commit v9 on v8

--- a/solution.py
+++ b/solution.py
@@ -11,6 +11,17 @@
 
 def exchange(parts, axes, groups):
     return lax.all_to_all(parts, axes, 0, 0, tiled=True, axis_index_groups=groups)
+
+
+def seat(col, n_col):
+    y, half = col // 2, n_col // 4
+    return y % half * 4 + y // half * 2 + col % 2
+
+
+def plane_order(planes):
+    anchor = planes * 3 // 4
+    apart = lambda z: min((z - anchor) % planes, (anchor - z) % planes)
+    return [1, 0] + sorted(range(2, planes), key=apart)
 
 
 def stage_kernel(lists, tiles, out, notes, sem):
@@ -28,7 +39,7 @@
     pair, side = my_row // 2, my_row % 2
     for k in range(count):
         row, col, live = slot(k)
-        product = jnp.dot(row_sets[who * n_col + row], tiles[k], preferred_element_type=jnp.float32)
+        product = jnp.dot(row_sets[seat(row, n_col) * 2 + who], tiles[k], preferred_element_type=jnp.float32)
         below = (2 * pair + who) * n_col + row > col * n_col + my_col
         weight = jnp.where(below & (col % 2 == side) & (live == 1), 1.0, 0.0)
         sums[col // 2] += product * weight
@@ -51,7 +62,7 @@
     copy.wait()
     slot = lambda k: (notes[0, k], notes[1, k], notes[2, k])
     add_mirror(n_col, 1 - my_row % 2, slot, count, row_sets, other, sums)
-    first, second = row_sets[my_col], row_sets[n_col + my_col]
+    first, second = row_sets[seat(my_col, n_col) * 2], row_sets[seat(my_col, n_col) * 2 + 1]
     for at, p in enumerate(order):
         high = sums[p].astype(jnp.bfloat16)
         low = (sums[p] - high.astype(jnp.float32)).astype(jnp.bfloat16)
@@ -70,13 +81,13 @@
     parts[...] = jnp.zeros_like(parts)
     for k in range(lists.shape[1]):
         row, col = lists[0, k], lists[1, k]
-        here = row_sets[col % 2 * n_col + my_col]
+        here = row_sets[seat(my_col, n_col) * 2 + col % 2]
         values = jnp.where(col // 2 == pair, here, arrived[spots[col // 2], col % 2])
         product = lax.dot_general(
             values, staged[k], (((1,), (1,)), ((), ())), preferred_element_type=jnp.float32
         )
         below = my_row * n_col + row >= col * n_col + my_col
-        parts[row] += product * jnp.where(below & (lists[2, k] == 1), 1.0, 0.0)
+        parts[seat(row, n_col)] += product * jnp.where(below & (lists[2, k] == 1), 1.0, 0.0)
 
 
 def body(vectors, tiles, tile_rows, tile_cols, tile_live):
@@ -85,11 +96,12 @@
     n_col = lax.axis_size("col")
     pairs = n_row // 2
     sides = [(i, i ^ 1) for i in range(n_row)]
-    order = list(range(pairs))[::-1]
+    order = [2 * z + half for z in plane_order(pairs // 2) for half in (1, 0)]
     spots = jnp.array([order.index(p) for p in range(pairs)], jnp.int32)
     params = pltpu.CompilerParams(vmem_limit_bytes=4 << 20)
 
-    near = [[p * 2 * n_col + i for i in range(2 * n_col)] for p in range(pairs)]
+    columns = sorted(range(n_col), key=lambda c: seat(c, n_col))
+    near = [[(2 * p + side) * n_col + c for c in columns for side in range(2)] for p in range(pairs)]
     row_sets = exchange(jnp.broadcast_to(vectors[None], (2 * n_col, nvec, seg)), ("row", "col"), near)
     blocks = tiles.reshape(-1, 128, 128)
     count = blocks.shape[0]
@@ -142,7 +154,7 @@
         compiler_params=params,
         name="direct",
     )(spots, lists, row_sets, arrived, staged)
-    straight = exchange(direct, "col", None)
+    straight = exchange(direct, "col", [columns])
     return mirrored + jnp.sum(straight, axis=0)
 
 

time: 73.9 us -> 77 us (1.042)
  blocking collectives: 48.9 us -> 50.7 us
    all_to_all x2, blocking collectives: 48.9 us -> 50.7 us  [exchange(): lax.all_to_all(parts, axes, 0, 0, tiled=True, axis_index_groups=groups)]
  transfers between devices with their start and end apart: 2 -> 2, of which waited for: 1 -> 1; matrix products, arithmetic and copies ran while one was open for 1% -> 1% of each run, Pallas kernels for 1% -> 2%
where the time goes in v9:
time: 77 us; the launch traced here: 76.2 us
  blocking collectives  50.7 us (66%)
  starting transfers between devices  11.2 us (15%)
  waiting for transfers between devices  6.15 us (8%)
  Pallas kernels  4.17 us (5%)
  local copies, waits for them, and re-layouts  2.54 us (3%)
  other arithmetic  1.32 us (2%)
    all_to_all x2, blocking collectives, exchange(): lax.all_to_all(parts, axes, 0, 0, tiled=True, axis_index_groups=groups)  50.7 us
    all_to_all x1, starting transfers between devices, exchange(): lax.all_to_all(parts, axes, 0, 0, tiled=True, axis_index_groups=groups)  9.05 us
    all_to_all x1, waiting for transfers between devices, exchange(): lax.all_to_all(parts, axes, 0, 0, tiled=True, axis_index_groups=groups)  6.15 us
    ppermute x1, starting transfers between devices, body(): other = lax.ppermute(staged, 'row', sides)  2.18 us
  transfers between devices with their start and end apart: 2, of which 1 were waited for; matrix products, arithmetic and copies ran while one was open for 1% of the time, Pallas kernels for 2%

profile of v9, /device:TPU:2, one launch (start us, length us, event | category | flops | bytes accessed | tf_op | source)
XLA Modules:
  0.0 76.2 jit_solution(18103331297893946821)
XLA Ops:
  0.0 1.3 %broadcast_in_dim.2 = bf16[32,8,128]{2,1,0:T(8,128)(2,1)} broadcast(bf16[8,128]{1,0:T(8,128)(2,1)} %param.6), dimensions={1,2} | broadcast | bytes 67584 | tf_op jit(solution)/shard_map/broadcast_in_dim | solution.py:105
  1.3 9.1 %all-to-all-start = ((bf16[32,8,128]{2,1,0:T(8,128)(2,1)}), bf16[32,8,128]{2,1,0:T(8,128)(2,1)S(1)}, u32[]{:S(2)}, u32[]{:S(2)}) async-start(bf16[32,8,128]{2,1,0:T(8,128)(2,1)} %broadcast_in_dim.2), calls=%async_computation | async-start | bytes 131072 | tf_op jit(solution)/shard_map/all_to_all | solution.py:13
  10.4 0.7 pad_add_fusion.lists.refs_0_.refs_1_
  11.1 0.0 copy-start
  11.1 1.2 %copy-done = bf16[1,1,32,128,128]{4,3,2,1,0:T(8,128)(2,1)S(1)} copy-done((bf16[1,1,32,128,128]{4,3,2,1,0:T(8,128)(2,1)S(1)}, bf16[1,1,32,128,128]{4,3,2,1,0:T(8,128)(2,1)}, u32[]{:S(2)}) %copy-start) | copy-done | bytes 1048600
  12.3 0.1 stage.1.refs_2_.refs_4_
  12.4 2.2 %collective-permute-start = (bf16[33,128,128]{2,1,0:T(8,128)(2,1)S(1)}, bf16[33,128,128]{2,1,0:T(8,128)(2,1)S(1)}, u32[]{:S(2)}, u32[]{:S(2)}) collective-permute-start(bf16[33,128,128]{2,1,0:T(8,128)(2,1)S(1)} %stage.1.refs_2_.refs_4_), channel_id=1, source_target_pairs={{0,16},{16,0},{32,48},{48,32},{64,80},{80,64},{96,112},{112,96},{1... | collective-permute-start | bytes 3244040 | tf_op jit(solution)/shard_map/ppermute | solution.py:119
  14.6 6.1 %all-to-all-done.refs_1_.refs_0_.refs_2_ = bf16[32,8,128]{2,1,0:T(8,128)(2,1)S(1)} async-done(((bf16[32,8,128]{2,1,0:T(8,128)(2,1)}), bf16[32,8,128]{2,1,0:T(8,128)(2,1)S(1)}, u32[]{:S(2)}, u32[]{:S(2)}) %all-to-all-start) | async-done | bytes 65568 | tf_op jit(solution)/shard_map/all_to_all | solution.py:13
  20.7 1.3 %own.1.refs_2_ = f32[32,8,128]{2,1,0:T(8,128)S(1)} custom-call(s32[3,32]{1,0:T(4,128)S(1)} %pad_add_fusion.lists.refs_0_.refs_1_, bf16[32,8,128]{2,1,0:T(8,128)(2,1)S(1)} %all-to-all-done.refs_1_.refs_0_.refs_2_, bf16[33,128,128]{2,1,0:T(8,128)(2,1)S(1)} %stage.1.refs_2_.refs_4_), custom_call_target="tpu_custom_call" | custom-call | flops 99999997952 | bytes 1048576 | tf_op jit(solution)/shard_map/own/pallas_call | solution.py:121
  22.0 0.0 copy-start.1
  22.0 0.0 collective-permute-done.refs_1_
  22.0 1.4 %pair.1 = bf16[32,2,8,128]{3,2,1,0:T(8,128)(2,1)S(1)} custom-call(bf16[32,8,128]{2,1,0:T(8,128)(2,1)S(1)} %all-to-all-done.refs_1_.refs_0_.refs_2_, bf16[33,128,128]{2,1,0:T(8,128)(2,1)S(1)} %collective-permute-done.refs_1_, f32[32,8,128]{2,1,0:T(8,128)S(1)} %own.1.refs_2_), custom_call_target="tpu_custom_call" | custom-call | tf_op jit(solution)/shard_map/pair/pallas_call | solution.py:130
  23.5 35.8 %all_to_all.15.refs_3_ = bf16[32,2,8,128]{3,2,1,0:T(8,128)(2,1)S(1)} all-to-all(bf16[32,2,8,128]{3,2,1,0:T(8,128)(2,1)S(1)} %pair.1), channel_id=1, replica_groups={{96,64,32,0,800,768,736,704,864,832,672,640,928,896,608,576,992,960,544..., dimensions={0} | all-to-all | bytes 262144 | tf_op jit(solution)/shard_map/all_to_all | solution.py:13
  59.2 0.0 copy-done.1
  59.2 1.4 %direct.1 = (f32[16,8,128]{2,1,0:T(8,128)S(1)}, f32[8,128]{1,0:T(8,128)S(1)}) custom-call(s32[32]{0:T(128)S(1)} %copy-done.1, s32[3,32]{1,0:T(4,128)S(1)} %pad_add_fusion.lists.refs_0_.refs_1_, bf16[32,8,128]{2,1,0:T(8,128)(2,1)S(1)} %all-to-all-done.refs_1_.refs_0_.refs_2_, bf16[32,2,8,128]{3,2,1,0:T(8,128)(2,1)S(1)} %all_to_all.15.refs_3_, ...), custom_call_target="tpu_custom_call" | custom-call | tf_op jit(solution)/shard_map/direct/pallas_call | solution.py:146
  60.6 14.9 %all_to_all.16 = f32[16,8,128]{2,1,0:T(8,128)S(1)} all-to-all(f32[16,8,128]{2,1,0:T(8,128)S(1)} %get-tuple-element.8), channel_id=1, replica_groups={{0,1,8,9,2,3,10,11,4,5,12,13,6,7,14,15},{16,17,24,25,18,19,26,27,20,21,..., dimensions={0} | all-to-all | bytes 131072 | tf_op jit(solution)/shard_map/all_to_all | solution.py:13
  75.6 0.6 add.3
  (1 shorter events, 0.0 us)
Async XLA Ops:
  1.3 19.4 %all-to-all-start = ((bf16[32,8,128]{2,1,0:T(8,128)(2,1)}), bf16[32,8,128]{2,1,0:T(8,128)(2,1)S(1)}, u32[]{:S(2)}, u32[]{:S(2)}) async-start(bf16[32,8,128]{2,1,0:T(8,128)(2,1)} %broadcast_in_dim.2), calls=%async_computation | async-start | bytes 131072 | tf_op jit(solution)/shard_map/all_to_all | solution.py:13
  11.1 1.2 %copy-start = (bf16[1,1,32,128,128]{4,3,2,1,0:T(8,128)(2,1)S(1)}, bf16[1,1,32,128,128]{4,3,2,1,0:T(8,128)(2,1)}, u32[]{:S(2)}) copy-start(bf16[1,1,32,128,128]{4,3,2,1,0:T(8,128)(2,1)} %param.7) | copy-start | bytes 3145732
  12.4 9.6 %collective-permute-start = (bf16[33,128,128]{2,1,0:T(8,128)(2,1)S(1)}, bf16[33,128,128]{2,1,0:T(8,128)(2,1)S(1)}, u32[]{:S(2)}, u32[]{:S(2)}) collective-permute-start(bf16[33,128,128]{2,1,0:T(8,128)(2,1)S(1)} %stage.1.refs_2_.refs_4_), channel_id=1, source_target_pairs={{0,16},{16,0},{32,48},{48,32},{64,80},{80,64},{96,112},{112,96},{1... | collective-permute-start | bytes 3244040 | tf_op jit(solution)/shard_map/ppermute | solution.py:119
  22.0 37.2 %copy-start.1 = (s32[32]{0:T(128)S(1)}, s32[32]{0:T(128)}, u32[]{:S(2)}) copy-start(s32[32]{0:T(128)} %constant.4.clone.refs_0_) | copy-start | bytes 388

commit v10 on v8

--- a/solution.py
+++ b/solution.py
@@ -85,7 +85,8 @@
     n_col = lax.axis_size("col")
     pairs = n_row // 2
     sides = [(i, i ^ 1) for i in range(n_row)]
-    order = list(range(pairs))[::-1]
+    planes = pairs // 2
+    order = [2 * (i * (planes // 2 + 1) % planes) + half for i in range(planes) for half in range(2)]
     spots = jnp.array([order.index(p) for p in range(pairs)], jnp.int32)
     params = pltpu.CompilerParams(vmem_limit_bytes=4 << 20)
 

time: 73.9 us -> 76.6 us (1.037)
  blocking collectives: 48.9 us -> 51.5 us
    all_to_all x2, blocking collectives: 48.9 us -> 51.5 us  [exchange(): lax.all_to_all(parts, axes, 0, 0, tiled=True, axis_index_groups=groups)]
where the time goes in v10:
time: 76.6 us; the launch traced here: 76.2 us
  blocking collectives  51.5 us (67%)
  starting transfers between devices  11.2 us (15%)
  waiting for transfers between devices  6.11 us (8%)
  Pallas kernels  3.44 us (4%)
  local copies, waits for them, and re-layouts  2.53 us (3%)
  other arithmetic  1.32 us (2%)
    all_to_all x2, blocking collectives, exchange(): lax.all_to_all(parts, axes, 0, 0, tiled=True, axis_index_groups=groups)  51.5 us
    all_to_all x1, starting transfers between devices, exchange(): lax.all_to_all(parts, axes, 0, 0, tiled=True, axis_index_groups=groups)  9.05 us
    all_to_all x1, waiting for transfers between devices, exchange(): lax.all_to_all(parts, axes, 0, 0, tiled=True, axis_index_groups=groups)  6.11 us
    ppermute x1, starting transfers between devices, body(): other = lax.ppermute(staged, 'row', sides)  2.19 us
  transfers between devices with their start and end apart: 2, of which 1 were waited for; matrix products, arithmetic and copies ran while one was open for 1% of the time, Pallas kernels for 1%

profile of v10, /device:TPU:2, one launch (start us, length us, event | category | flops | bytes accessed | tf_op | source)
XLA Modules:
  0.0 76.2 jit_solution(6609327677439307295)
XLA Ops:
  0.0 1.3 %broadcast_in_dim.2 = bf16[32,8,128]{2,1,0:T(8,128)(2,1)} broadcast(bf16[8,128]{1,0:T(8,128)(2,1)} %param.6), dimensions={1,2} | broadcast | bytes 67584 | tf_op jit(solution)/shard_map/broadcast_in_dim | solution.py:94
  1.3 9.1 %all-to-all-start = ((bf16[32,8,128]{2,1,0:T(8,128)(2,1)}), bf16[32,8,128]{2,1,0:T(8,128)(2,1)S(1)}, u32[]{:S(2)}, u32[]{:S(2)}) async-start(bf16[32,8,128]{2,1,0:T(8,128)(2,1)} %broadcast_in_dim.2), calls=%async_computation | async-start | bytes 131072 | tf_op jit(solution)/shard_map/all_to_all | solution.py:13
  10.4 0.7 pad_add_fusion.lists.refs_0_.refs_1_
  11.1 0.0 copy-start
  11.1 1.2 %copy-done = bf16[1,1,32,128,128]{4,3,2,1,0:T(8,128)(2,1)S(1)} copy-done((bf16[1,1,32,128,128]{4,3,2,1,0:T(8,128)(2,1)S(1)}, bf16[1,1,32,128,128]{4,3,2,1,0:T(8,128)(2,1)}, u32[]{:S(2)}) %copy-start) | copy-done | bytes 1048600
  12.3 0.1 stage.1.refs_2_.refs_4_
  12.4 2.2 %collective-permute-start = (bf16[33,128,128]{2,1,0:T(8,128)(2,1)S(1)}, bf16[33,128,128]{2,1,0:T(8,128)(2,1)S(1)}, u32[]{:S(2)}, u32[]{:S(2)}) collective-permute-start(bf16[33,128,128]{2,1,0:T(8,128)(2,1)S(1)} %stage.1.refs_2_.refs_4_), channel_id=1, source_target_pairs={{0,16},{16,0},{32,48},{48,32},{64,80},{80,64},{96,112},{112,96},{1... | collective-permute-start | bytes 3244040 | tf_op jit(solution)/shard_map/ppermute | solution.py:108
  14.6 6.1 %all-to-all-done.refs_1_.refs_0_.refs_2_ = bf16[32,8,128]{2,1,0:T(8,128)(2,1)S(1)} async-done(((bf16[32,8,128]{2,1,0:T(8,128)(2,1)}), bf16[32,8,128]{2,1,0:T(8,128)(2,1)S(1)}, u32[]{:S(2)}, u32[]{:S(2)}) %all-to-all-start) | async-done | bytes 65568 | tf_op jit(solution)/shard_map/all_to_all | solution.py:13
  20.7 1.0 %own.1.refs_2_ = f32[32,8,128]{2,1,0:T(8,128)S(1)} custom-call(s32[3,32]{1,0:T(4,128)S(1)} %pad_add_fusion.lists.refs_0_.refs_1_, bf16[32,8,128]{2,1,0:T(8,128)(2,1)S(1)} %all-to-all-done.refs_1_.refs_0_.refs_2_, bf16[33,128,128]{2,1,0:T(8,128)(2,1)S(1)} %stage.1.refs_2_.refs_4_), custom_call_target="tpu_custom_call" | custom-call | flops 99999997952 | bytes 1048576 | tf_op jit(solution)/shard_map/own/pallas_call | solution.py:110
  21.7 0.0 copy-start.1
  21.7 0.0 collective-permute-done.refs_1_
  21.7 1.1 %pair.1 = bf16[32,2,8,128]{3,2,1,0:T(8,128)(2,1)S(1)} custom-call(bf16[32,8,128]{2,1,0:T(8,128)(2,1)S(1)} %all-to-all-done.refs_1_.refs_0_.refs_2_, bf16[33,128,128]{2,1,0:T(8,128)(2,1)S(1)} %collective-permute-done.refs_1_, f32[32,8,128]{2,1,0:T(8,128)S(1)} %own.1.refs_2_), custom_call_target="tpu_custom_call" | custom-call | tf_op jit(solution)/shard_map/pair/pallas_call | solution.py:119
  22.8 35.9 %all_to_all.15.refs_3_ = bf16[32,2,8,128]{3,2,1,0:T(8,128)(2,1)S(1)} all-to-all(bf16[32,2,8,128]{3,2,1,0:T(8,128)(2,1)S(1)} %pair.1), channel_id=1, replica_groups={{0,32,576,608,128,160,704,736,256,288,832,864,384,416,960,992,512,544,6..., dimensions={0} | all-to-all | bytes 262144 | tf_op jit(solution)/shard_map/all_to_all | solution.py:13
  58.8 0.0 copy-done.1
  58.8 1.2 %direct.1 = (f32[16,8,128]{2,1,0:T(8,128)S(1)}, f32[8,128]{1,0:T(8,128)S(1)}) custom-call(s32[32]{0:T(128)S(1)} %copy-done.1, s32[3,32]{1,0:T(4,128)S(1)} %pad_add_fusion.lists.refs_0_.refs_1_, bf16[32,8,128]{2,1,0:T(8,128)(2,1)S(1)} %all-to-all-done.refs_1_.refs_0_.refs_2_, bf16[32,2,8,128]{3,2,1,0:T(8,128)(2,1)S(1)} %all_to_all.15.refs_3_, ...), custom_call_target="tpu_custom_call" | custom-call | tf_op jit(solution)/shard_map/direct/pallas_call | solution.py:135
  60.0 15.6 %all_to_all.16 = f32[16,8,128]{2,1,0:T(8,128)S(1)} all-to-all(f32[16,8,128]{2,1,0:T(8,128)S(1)} %get-tuple-element.8), channel_id=1, replica_groups=mesh['row'=64,'col'=16] {'col'}, dimensions={0} | all-to-all | bytes 131072 | tf_op jit(solution)/shard_map/all_to_all | solution.py:13
  75.6 0.6 add.3
  (1 shorter events, 0.0 us)
Async XLA Ops:
  1.3 19.4 %all-to-all-start = ((bf16[32,8,128]{2,1,0:T(8,128)(2,1)}), bf16[32,8,128]{2,1,0:T(8,128)(2,1)S(1)}, u32[]{:S(2)}, u32[]{:S(2)}) async-start(bf16[32,8,128]{2,1,0:T(8,128)(2,1)} %broadcast_in_dim.2), calls=%async_computation | async-start | bytes 131072 | tf_op jit(solution)/shard_map/all_to_all | solution.py:13
  11.1 1.2 %copy-start = (bf16[1,1,32,128,128]{4,3,2,1,0:T(8,128)(2,1)S(1)}, bf16[1,1,32,128,128]{4,3,2,1,0:T(8,128)(2,1)}, u32[]{:S(2)}) copy-start(bf16[1,1,32,128,128]{4,3,2,1,0:T(8,128)(2,1)} %param.7) | copy-start | bytes 3145732
  12.4 9.3 %collective-permute-start = (bf16[33,128,128]{2,1,0:T(8,128)(2,1)S(1)}, bf16[33,128,128]{2,1,0:T(8,128)(2,1)S(1)}, u32[]{:S(2)}, u32[]{:S(2)}) collective-permute-start(bf16[33,128,128]{2,1,0:T(8,128)(2,1)S(1)} %stage.1.refs_2_.refs_4_), channel_id=1, source_target_pairs={{0,16},{16,0},{32,48},{48,32},{64,80},{80,64},{96,112},{112,96},{1... | collective-permute-start | bytes 3244040 | tf_op jit(solution)/shard_map/ppermute | solution.py:108
  21.7 37.1 %copy-start.1 = (s32[32]{0:T(128)S(1)}, s32[32]{0:T(128)}, u32[]{:S(2)}) copy-start(s32[32]{0:T(128)} %constant.4.clone.refs_0_) | copy-start | bytes 388

commit v11 on v10

--- a/solution.py
+++ b/solution.py
@@ -86,7 +86,7 @@
     pairs = n_row // 2
     sides = [(i, i ^ 1) for i in range(n_row)]
     planes = pairs // 2
-    order = [2 * (i * (planes // 2 + 1) % planes) + half for i in range(planes) for half in range(2)]
+    order = [2 * (i * (planes // 2 - 1) % planes) + half for i in range(planes) for half in (1, 0)]
     spots = jnp.array([order.index(p) for p in range(pairs)], jnp.int32)
     params = pltpu.CompilerParams(vmem_limit_bytes=4 << 20)
 

time: 76.6 us -> 76.4 us (level)
  the two profiles are of different devices: /device:TPU:2 before, /device:TPU:8 now
where the time goes in v11:
time: 76.4 us; the launch traced here: 76 us
  blocking collectives  44.6 us (58%)
  starting transfers between devices  18.7 us (24%)
  waiting for transfers between devices  5.28 us (7%)
  Pallas kernels  3.46 us (5%)
  local copies, waits for them, and re-layouts  2.53 us (3%)
  other arithmetic  1.32 us (2%)
    all_to_all x2, blocking collectives, exchange(): lax.all_to_all(parts, axes, 0, 0, tiled=True, axis_index_groups=groups)  44.6 us
    all_to_all x1, starting transfers between devices, exchange(): lax.all_to_all(parts, axes, 0, 0, tiled=True, axis_index_groups=groups)  16.6 us
    all_to_all x1, waiting for transfers between devices, exchange(): lax.all_to_all(parts, axes, 0, 0, tiled=True, axis_index_groups=groups)  5.28 us
    ppermute x1, starting transfers between devices, body(): other = lax.ppermute(staged, 'row', sides)  2.13 us
  transfers between devices with their start and end apart: 2, of which 1 were waited for; matrix products, arithmetic and copies ran while one was open for 1% of the time, Pallas kernels for 1%

profile of v11, /device:TPU:8, one launch (start us, length us, event | category | flops | bytes accessed | tf_op | source)
XLA Modules:
  0.0 76.0 jit_solution(6173994302850872494)
XLA Ops:
  0.0 1.3 %broadcast_in_dim.2 = bf16[32,8,128]{2,1,0:T(8,128)(2,1)} broadcast(bf16[8,128]{1,0:T(8,128)(2,1)} %param.6), dimensions={1,2} | broadcast | bytes 67584 | tf_op jit(solution)/shard_map/broadcast_in_dim | solution.py:94
  1.3 16.6 %all-to-all-start = ((bf16[32,8,128]{2,1,0:T(8,128)(2,1)}), bf16[32,8,128]{2,1,0:T(8,128)(2,1)S(1)}, u32[]{:S(2)}, u32[]{:S(2)}) async-start(bf16[32,8,128]{2,1,0:T(8,128)(2,1)} %broadcast_in_dim.2), calls=%async_computation | async-start | bytes 131072 | tf_op jit(solution)/shard_map/all_to_all | solution.py:13
  17.9 0.7 pad_add_fusion.lists.refs_0_.refs_1_
  18.6 0.0 copy-start
  18.6 1.2 %copy-done = bf16[1,1,32,128,128]{4,3,2,1,0:T(8,128)(2,1)S(1)} copy-done((bf16[1,1,32,128,128]{4,3,2,1,0:T(8,128)(2,1)S(1)}, bf16[1,1,32,128,128]{4,3,2,1,0:T(8,128)(2,1)}, u32[]{:S(2)}) %copy-start) | copy-done | bytes 1048600
  19.8 0.1 stage.1.refs_2_.refs_4_
  19.9 2.1 %collective-permute-start = (bf16[33,128,128]{2,1,0:T(8,128)(2,1)S(1)}, bf16[33,128,128]{2,1,0:T(8,128)(2,1)S(1)}, u32[]{:S(2)}, u32[]{:S(2)}) collective-permute-start(bf16[33,128,128]{2,1,0:T(8,128)(2,1)S(1)} %stage.1.refs_2_.refs_4_), channel_id=1, source_target_pairs={{0,16},{16,0},{32,48},{48,32},{64,80},{80,64},{96,112},{112,96},{1... | collective-permute-start | bytes 3244040 | tf_op jit(solution)/shard_map/ppermute | solution.py:108
  22.1 5.3 %all-to-all-done.refs_1_.refs_0_.refs_2_ = bf16[32,8,128]{2,1,0:T(8,128)(2,1)S(1)} async-done(((bf16[32,8,128]{2,1,0:T(8,128)(2,1)}), bf16[32,8,128]{2,1,0:T(8,128)(2,1)S(1)}, u32[]{:S(2)}, u32[]{:S(2)}) %all-to-all-start) | async-done | bytes 65568 | tf_op jit(solution)/shard_map/all_to_all | solution.py:13
  27.3 1.0 %own.1.refs_2_ = f32[32,8,128]{2,1,0:T(8,128)S(1)} custom-call(s32[3,32]{1,0:T(4,128)S(1)} %pad_add_fusion.lists.refs_0_.refs_1_, bf16[32,8,128]{2,1,0:T(8,128)(2,1)S(1)} %all-to-all-done.refs_1_.refs_0_.refs_2_, bf16[33,128,128]{2,1,0:T(8,128)(2,1)S(1)} %stage.1.refs_2_.refs_4_), custom_call_target="tpu_custom_call" | custom-call | flops 99999997952 | bytes 1048576 | tf_op jit(solution)/shard_map/own/pallas_call | solution.py:110
  28.3 0.0 copy-start.1
  28.3 0.0 collective-permute-done.refs_1_
  28.4 1.1 %pair.1 = bf16[32,2,8,128]{3,2,1,0:T(8,128)(2,1)S(1)} custom-call(bf16[32,8,128]{2,1,0:T(8,128)(2,1)S(1)} %all-to-all-done.refs_1_.refs_0_.refs_2_, bf16[33,128,128]{2,1,0:T(8,128)(2,1)S(1)} %collective-permute-done.refs_1_, f32[32,8,128]{2,1,0:T(8,128)S(1)} %own.1.refs_2_), custom_call_target="tpu_custom_call" | custom-call | tf_op jit(solution)/shard_map/pair/pallas_call | solution.py:119
  29.5 29.4 %all_to_all.15.refs_3_ = bf16[32,2,8,128]{3,2,1,0:T(8,128)(2,1)S(1)} all-to-all(bf16[32,2,8,128]{3,2,1,0:T(8,128)(2,1)S(1)} %pair.1), channel_id=1, replica_groups={{32,0,480,448,928,896,352,320,800,768,224,192,672,640,96,64,544,512,992..., dimensions={0} | all-to-all | bytes 262144 | tf_op jit(solution)/shard_map/all_to_all | solution.py:13
  58.9 0.0 copy-done.1
  58.9 1.2 %direct.1 = (f32[16,8,128]{2,1,0:T(8,128)S(1)}, f32[8,128]{1,0:T(8,128)S(1)}) custom-call(s32[32]{0:T(128)S(1)} %copy-done.1, s32[3,32]{1,0:T(4,128)S(1)} %pad_add_fusion.lists.refs_0_.refs_1_, bf16[32,8,128]{2,1,0:T(8,128)(2,1)S(1)} %all-to-all-done.refs_1_.refs_0_.refs_2_, bf16[32,2,8,128]{3,2,1,0:T(8,128)(2,1)S(1)} %all_to_all.15.refs_3_, ...), custom_call_target="tpu_custom_call" | custom-call | tf_op jit(solution)/shard_map/direct/pallas_call | solution.py:135
  60.1 15.3 %all_to_all.16 = f32[16,8,128]{2,1,0:T(8,128)S(1)} all-to-all(f32[16,8,128]{2,1,0:T(8,128)S(1)} %get-tuple-element.8), channel_id=1, replica_groups=mesh['row'=64,'col'=16] {'col'}, dimensions={0} | all-to-all | bytes 131072 | tf_op jit(solution)/shard_map/all_to_all | solution.py:13
  75.4 0.6 add.3
  (1 shorter events, 0.0 us)
Async XLA Ops:
  1.3 26.0 %all-to-all-start = ((bf16[32,8,128]{2,1,0:T(8,128)(2,1)}), bf16[32,8,128]{2,1,0:T(8,128)(2,1)S(1)}, u32[]{:S(2)}, u32[]{:S(2)}) async-start(bf16[32,8,128]{2,1,0:T(8,128)(2,1)} %broadcast_in_dim.2), calls=%async_computation | async-start | bytes 131072 | tf_op jit(solution)/shard_map/all_to_all | solution.py:13
  18.6 1.2 %copy-start = (bf16[1,1,32,128,128]{4,3,2,1,0:T(8,128)(2,1)S(1)}, bf16[1,1,32,128,128]{4,3,2,1,0:T(8,128)(2,1)}, u32[]{:S(2)}) copy-start(bf16[1,1,32,128,128]{4,3,2,1,0:T(8,128)(2,1)} %param.7) | copy-start | bytes 3145732
  19.9 8.4 %collective-permute-start = (bf16[33,128,128]{2,1,0:T(8,128)(2,1)S(1)}, bf16[33,128,128]{2,1,0:T(8,128)(2,1)S(1)}, u32[]{:S(2)}, u32[]{:S(2)}) collective-permute-start(bf16[33,128,128]{2,1,0:T(8,128)(2,1)S(1)} %stage.1.refs_2_.refs_4_), channel_id=1, source_target_pairs={{0,16},{16,0},{32,48},{48,32},{64,80},{80,64},{96,112},{112,96},{1... | collective-permute-start | bytes 3244040 | tf_op jit(solution)/shard_map/ppermute | solution.py:108
  28.3 30.5 %copy-start.1 = (s32[32]{0:T(128)S(1)}, s32[32]{0:T(128)}, u32[]{:S(2)}) copy-start(s32[32]{0:T(128)} %constant.4.clone.refs_0_) | copy-start | bytes 388

commit v12 on v8

--- a/solution.py
+++ b/solution.py
@@ -13,6 +13,12 @@
     return lax.all_to_all(parts, axes, 0, 0, tiled=True, axis_index_groups=groups)
 
 
+def seat(col, n_col):
+    half = n_col // 4
+    y = col >> 1
+    return ((y & (half - 1)) << 2) | ((y >> (half.bit_length() - 1)) << 1) | (col & 1)
+
+
 def stage_kernel(lists, tiles, out, notes, sem):
     count = tiles.shape[0]
     notes[...] = jnp.zeros_like(notes)
@@ -25,19 +31,19 @@
 
 def add_mirror(n_col, who, slot, count, row_sets, tiles, sums):
     my_row, my_col = lax.axis_index("row"), lax.axis_index("col")
-    pair, side = my_row // 2, my_row % 2
+    pair, side = my_row >> 1, my_row & 1
     for k in range(count):
         row, col, live = slot(k)
-        product = jnp.dot(row_sets[who * n_col + row], tiles[k], preferred_element_type=jnp.float32)
+        product = jnp.dot(row_sets[(seat(row, n_col) << 1) | who], tiles[k], preferred_element_type=jnp.float32)
         below = (2 * pair + who) * n_col + row > col * n_col + my_col
-        weight = jnp.where(below & (col % 2 == side) & (live == 1), 1.0, 0.0)
-        sums[col // 2] += product * weight
+        weight = jnp.where(below & ((col & 1) == side) & (live == 1), 1.0, 0.0)
+        sums[col >> 1] += product * weight
 
 
 def own_kernel(n_col, lists, row_sets, staged, sums):
     sums[...] = jnp.zeros_like(sums)
     slot = lambda k: (lists[0, k], lists[1, k], lists[2, k])
-    add_mirror(n_col, lax.axis_index("row") % 2, slot, lists.shape[1], row_sets, staged, sums)
+    add_mirror(n_col, lax.axis_index("row") & 1, slot, lists.shape[1], row_sets, staged, sums)
 
 
 def pair_kernel(n_col, order, row_sets, other, own_sums, parts, sums, page, notes, sem):
@@ -46,12 +52,12 @@
     copy = pltpu.make_async_copy(page, notes, sem)
     copy.start()
     my_row, my_col = lax.axis_index("row"), lax.axis_index("col")
-    pair = my_row // 2
+    pair = my_row >> 1
     sums[...] = own_sums[...]
     copy.wait()
     slot = lambda k: (notes[0, k], notes[1, k], notes[2, k])
-    add_mirror(n_col, 1 - my_row % 2, slot, count, row_sets, other, sums)
-    first, second = row_sets[my_col], row_sets[n_col + my_col]
+    add_mirror(n_col, 1 - (my_row & 1), slot, count, row_sets, other, sums)
+    first, second = row_sets[seat(my_col, n_col) << 1], row_sets[(seat(my_col, n_col) << 1) | 1]
     for at, p in enumerate(order):
         high = sums[p].astype(jnp.bfloat16)
         low = (sums[p] - high.astype(jnp.float32)).astype(jnp.bfloat16)
@@ -61,17 +67,18 @@
 
 def direct_kernel(n_col, order, spots, lists, row_sets, arrived, staged, parts, mirrored):
     my_row, my_col = lax.axis_index("row"), lax.axis_index("col")
-    pair = my_row // 2
+    pair = my_row >> 1
     total = jnp.zeros(mirrored.shape, jnp.float32)
     for at, p in enumerate(order):
         both = arrived[at, 0].astype(jnp.float32) + arrived[at, 1].astype(jnp.float32)
         total += jnp.where(p >= pair, both, 0.0)
     mirrored[...] = total
     parts[...] = jnp.zeros_like(parts)
+    base = seat(my_col, n_col) << 1
     for k in range(lists.shape[1]):
         row, col = lists[0, k], lists[1, k]
-        here = row_sets[col % 2 * n_col + my_col]
-        values = jnp.where(col // 2 == pair, here, arrived[spots[col // 2], col % 2])
+        here = row_sets[base + (col & 1)]
+        values = jnp.where((col >> 1) == pair, here, arrived[spots[col >> 1], col & 1])
         product = lax.dot_general(
             values, staged[k], (((1,), (1,)), ((), ())), preferred_element_type=jnp.float32
         )
@@ -89,7 +96,8 @@
     spots = jnp.array([order.index(p) for p in range(pairs)], jnp.int32)
     params = pltpu.CompilerParams(vmem_limit_bytes=4 << 20)
 
-    near = [[p * 2 * n_col + i for i in range(2 * n_col)] for p in range(pairs)]
+    columns = sorted(range(n_col), key=lambda c: seat(c, n_col))
+    near = [[(2 * p + side) * n_col + c for c in columns for side in range(2)] for p in range(pairs)]
     row_sets = exchange(jnp.broadcast_to(vectors[None], (2 * n_col, nvec, seg)), ("row", "col"), near)
     blocks = tiles.reshape(-1, 128, 128)
     count = blocks.shape[0]

time: 73.9 us -> 73.9 us (level)
  no operation moved by 1% of the time
where the time goes in v12:
time: 73.9 us; the launch traced here: 73.6 us
  blocking collectives  48.9 us (66%)
  starting transfers between devices  11.2 us (15%)
  waiting for transfers between devices  6.15 us (8%)
  Pallas kernels  3.42 us (5%)
  local copies, waits for them, and re-layouts  2.53 us (3%)
  other arithmetic  1.32 us (2%)
    all_to_all x2, blocking collectives, exchange(): lax.all_to_all(parts, axes, 0, 0, tiled=True, axis_index_groups=groups)  48.9 us
    all_to_all x1, starting transfers between devices, exchange(): lax.all_to_all(parts, axes, 0, 0, tiled=True, axis_index_groups=groups)  9.05 us
    all_to_all x1, waiting for transfers between devices, exchange(): lax.all_to_all(parts, axes, 0, 0, tiled=True, axis_index_groups=groups)  6.15 us
    ppermute x1, starting transfers between devices, body(): other = lax.ppermute(staged, 'row', sides)  2.18 us
  transfers between devices with their start and end apart: 2, of which 1 were waited for; matrix products, arithmetic and copies ran while one was open for 1% of the time, Pallas kernels for 1%

profile of v12, /device:TPU:2, one launch (start us, length us, event | category | flops | bytes accessed | tf_op | source)
XLA Modules:
  0.0 73.6 jit_solution(1367295137528795711)
XLA Ops:
  0.0 1.3 %broadcast_in_dim.2 = bf16[32,8,128]{2,1,0:T(8,128)(2,1)} broadcast(bf16[8,128]{1,0:T(8,128)(2,1)} %param.6), dimensions={1,2} | broadcast | bytes 67584 | tf_op jit(solution)/shard_map/broadcast_in_dim | solution.py:101
  1.3 9.1 %all-to-all-start = ((bf16[32,8,128]{2,1,0:T(8,128)(2,1)}), bf16[32,8,128]{2,1,0:T(8,128)(2,1)S(1)}, u32[]{:S(2)}, u32[]{:S(2)}) async-start(bf16[32,8,128]{2,1,0:T(8,128)(2,1)} %broadcast_in_dim.2), calls=%async_computation | async-start | bytes 131072 | tf_op jit(solution)/shard_map/all_to_all | solution.py:13
  10.4 0.7 pad_add_fusion.lists.refs_0_.refs_1_
  11.1 0.0 copy-start
  11.1 1.2 %copy-done = bf16[1,1,32,128,128]{4,3,2,1,0:T(8,128)(2,1)S(1)} copy-done((bf16[1,1,32,128,128]{4,3,2,1,0:T(8,128)(2,1)S(1)}, bf16[1,1,32,128,128]{4,3,2,1,0:T(8,128)(2,1)}, u32[]{:S(2)}) %copy-start) | copy-done | bytes 1048600
  12.3 0.1 stage.1.refs_2_.refs_4_
  12.4 2.2 %collective-permute-start = (bf16[33,128,128]{2,1,0:T(8,128)(2,1)S(1)}, bf16[33,128,128]{2,1,0:T(8,128)(2,1)S(1)}, u32[]{:S(2)}, u32[]{:S(2)}) collective-permute-start(bf16[33,128,128]{2,1,0:T(8,128)(2,1)S(1)} %stage.1.refs_2_.refs_4_), channel_id=1, source_target_pairs={{0,16},{16,0},{32,48},{48,32},{64,80},{80,64},{96,112},{112,96},{1... | collective-permute-start | bytes 3244040 | tf_op jit(solution)/shard_map/ppermute | solution.py:115
  14.6 6.1 %all-to-all-done.refs_1_.refs_0_.refs_2_ = bf16[32,8,128]{2,1,0:T(8,128)(2,1)S(1)} async-done(((bf16[32,8,128]{2,1,0:T(8,128)(2,1)}), bf16[32,8,128]{2,1,0:T(8,128)(2,1)S(1)}, u32[]{:S(2)}, u32[]{:S(2)}) %all-to-all-start) | async-done | bytes 65568 | tf_op jit(solution)/shard_map/all_to_all | solution.py:13
  20.7 1.0 %own.1.refs_2_ = f32[32,8,128]{2,1,0:T(8,128)S(1)} custom-call(s32[3,32]{1,0:T(4,128)S(1)} %pad_add_fusion.lists.refs_0_.refs_1_, bf16[32,8,128]{2,1,0:T(8,128)(2,1)S(1)} %all-to-all-done.refs_1_.refs_0_.refs_2_, bf16[33,128,128]{2,1,0:T(8,128)(2,1)S(1)} %stage.1.refs_2_.refs_4_), custom_call_target="tpu_custom_call" | custom-call | flops 99999997952 | bytes 1048576 | tf_op jit(solution)/shard_map/own/pallas_call | solution.py:117
  21.7 0.0 copy-start.1
  21.7 0.0 collective-permute-done.refs_1_
  21.7 1.1 %pair.1 = bf16[32,2,8,128]{3,2,1,0:T(8,128)(2,1)S(1)} custom-call(bf16[32,8,128]{2,1,0:T(8,128)(2,1)S(1)} %all-to-all-done.refs_1_.refs_0_.refs_2_, bf16[33,128,128]{2,1,0:T(8,128)(2,1)S(1)} %collective-permute-done.refs_1_, f32[32,8,128]{2,1,0:T(8,128)S(1)} %own.1.refs_2_), custom_call_target="tpu_custom_call" | custom-call | tf_op jit(solution)/shard_map/pair/pallas_call | solution.py:126
  22.8 33.7 %all_to_all.15.refs_3_ = bf16[32,2,8,128]{3,2,1,0:T(8,128)(2,1)S(1)} all-to-all(bf16[32,2,8,128]{3,2,1,0:T(8,128)(2,1)S(1)} %pair.1), channel_id=1, replica_groups={{992,960,928,896,864,832,800,768,736,704,672,640,608,576,544,512,480,44..., dimensions={0} | all-to-all | bytes 262144 | tf_op jit(solution)/shard_map/all_to_all | solution.py:13
  56.6 0.0 copy-done.1
  56.6 1.2 %direct.1 = (f32[16,8,128]{2,1,0:T(8,128)S(1)}, f32[8,128]{1,0:T(8,128)S(1)}) custom-call(s32[32]{0:T(128)S(1)} %copy-done.1, s32[3,32]{1,0:T(4,128)S(1)} %pad_add_fusion.lists.refs_0_.refs_1_, bf16[32,8,128]{2,1,0:T(8,128)(2,1)S(1)} %all-to-all-done.refs_1_.refs_0_.refs_2_, bf16[32,2,8,128]{3,2,1,0:T(8,128)(2,1)S(1)} %all_to_all.15.refs_3_, ...), custom_call_target="tpu_custom_call" | custom-call | tf_op jit(solution)/shard_map/direct/pallas_call | solution.py:142
  57.8 15.1 %all_to_all.16 = f32[16,8,128]{2,1,0:T(8,128)S(1)} all-to-all(f32[16,8,128]{2,1,0:T(8,128)S(1)} %get-tuple-element.8), channel_id=1, replica_groups=mesh['row'=64,'col'=16] {'col'}, dimensions={0} | all-to-all | bytes 131072 | tf_op jit(solution)/shard_map/all_to_all | solution.py:13
  73.0 0.6 add.3
  (1 shorter events, 0.0 us)
Async XLA Ops:
  1.3 19.4 %all-to-all-start = ((bf16[32,8,128]{2,1,0:T(8,128)(2,1)}), bf16[32,8,128]{2,1,0:T(8,128)(2,1)S(1)}, u32[]{:S(2)}, u32[]{:S(2)}) async-start(bf16[32,8,128]{2,1,0:T(8,128)(2,1)} %broadcast_in_dim.2), calls=%async_computation | async-start | bytes 131072 | tf_op jit(solution)/shard_map/all_to_all | solution.py:13
  11.1 1.2 %copy-start = (bf16[1,1,32,128,128]{4,3,2,1,0:T(8,128)(2,1)S(1)}, bf16[1,1,32,128,128]{4,3,2,1,0:T(8,128)(2,1)}, u32[]{:S(2)}) copy-start(bf16[1,1,32,128,128]{4,3,2,1,0:T(8,128)(2,1)} %param.7) | copy-start | bytes 3145732
  12.4 9.3 %collective-permute-start = (bf16[33,128,128]{2,1,0:T(8,128)(2,1)S(1)}, bf16[33,128,128]{2,1,0:T(8,128)(2,1)S(1)}, u32[]{:S(2)}, u32[]{:S(2)}) collective-permute-start(bf16[33,128,128]{2,1,0:T(8,128)(2,1)S(1)} %stage.1.refs_2_.refs_4_), channel_id=1, source_target_pairs={{0,16},{16,0},{32,48},{48,32},{64,80},{80,64},{96,112},{112,96},{1... | collective-permute-start | bytes 3244040 | tf_op jit(solution)/shard_map/ppermute | solution.py:115
  21.7 34.9 %copy-start.1 = (s32[32]{0:T(128)S(1)}, s32[32]{0:T(128)}, u32[]{:S(2)}) copy-start(s32[32]{0:T(128)} %constant.4.clone.refs_0_) | copy-start | bytes 388

commit v13 on v12

--- a/solution.py
+++ b/solution.py
@@ -19,14 +19,23 @@
     return ((y & (half - 1)) << 2) | ((y >> (half.bit_length() - 1)) << 1) | (col & 1)
 
 
-def stage_kernel(lists, tiles, out, notes, sem):
-    count = tiles.shape[0]
+def stage_kernel(rows, cols, live, tiles, out, page, notes, sems):
+    count, pieces = tiles.shape[0], sems.shape[0] - 1
+    step = count // pieces
+    copies = [
+        pltpu.make_async_copy(tiles.at[pl.ds(i * step, step)], out.at[pl.ds(i * step, step)], sems.at[i])
+        for i in range(pieces)
+    ]
+    for copy in copies:
+        copy.start()
     notes[...] = jnp.zeros_like(notes)
-    notes[pl.ds(0, lists.shape[0]), pl.ds(0, count)] = lists[...].astype(jnp.float32)
-    out[count] = notes[...].astype(out.dtype)
-    copy = pltpu.make_async_copy(tiles, out.at[pl.ds(0, count)], sem)
-    copy.start()
-    copy.wait()
+    for at, slots in enumerate((rows, cols, live)):
+        notes[pl.ds(at, 1), pl.ds(0, count)] = slots[0].astype(jnp.float32)
+    page[0] = notes[...].astype(page.dtype)
+    copies.append(pltpu.make_async_copy(page, out.at[pl.ds(count, 1)], sems.at[pieces]))
+    copies[-1].start()
+    for copy in copies:
+        copy.wait()
 
 
 def add_mirror(n_col, who, slot, count, row_sets, tiles, sums):
@@ -40,10 +49,10 @@
         sums[col >> 1] += product * weight
 
 
-def own_kernel(n_col, lists, row_sets, staged, sums):
+def own_kernel(n_col, rows, cols, live, row_sets, staged, sums):
     sums[...] = jnp.zeros_like(sums)
-    slot = lambda k: (lists[0, k], lists[1, k], lists[2, k])
-    add_mirror(n_col, lax.axis_index("row") & 1, slot, lists.shape[1], row_sets, staged, sums)
+    slot = lambda k: (rows[0, 0, k], cols[0, 0, k], live[0, 0, k])
+    add_mirror(n_col, lax.axis_index("row") & 1, slot, rows.shape[2], row_sets, staged, sums)
 
 
 def pair_kernel(n_col, order, row_sets, other, own_sums, parts, sums, page, notes, sem):
@@ -65,7 +74,7 @@
         parts[at, 1] = jnp.where(p > pair, second, low)
 
 
-def direct_kernel(n_col, order, spots, lists, row_sets, arrived, staged, parts, mirrored):
+def direct_kernel(n_col, order, spots, rows, cols, live, row_sets, arrived, staged, parts, mirrored):
     my_row, my_col = lax.axis_index("row"), lax.axis_index("col")
     pair = my_row >> 1
     total = jnp.zeros(mirrored.shape, jnp.float32)
@@ -75,15 +84,15 @@
     mirrored[...] = total
     parts[...] = jnp.zeros_like(parts)
     base = seat(my_col, n_col) << 1
-    for k in range(lists.shape[1]):
-        row, col = lists[0, k], lists[1, k]
+    for k in range(rows.shape[2]):
+        row, col = rows[0, 0, k], cols[0, 0, k]
         here = row_sets[base + (col & 1)]
         values = jnp.where((col >> 1) == pair, here, arrived[spots[col >> 1], col & 1])
         product = lax.dot_general(
             values, staged[k], (((1,), (1,)), ((), ())), preferred_element_type=jnp.float32
         )
         below = my_row * n_col + row >= col * n_col + my_col
-        parts[row] += product * jnp.where(below & (lists[2, k] == 1), 1.0, 0.0)
+        parts[row] += product * jnp.where(below & (live[0, 0, k] == 1), 1.0, 0.0)
 
 
 def body(vectors, tiles, tile_rows, tile_cols, tile_live):
@@ -101,28 +110,31 @@
     row_sets = exchange(jnp.broadcast_to(vectors[None], (2 * n_col, nvec, seg)), ("row", "col"), near)
     blocks = tiles.reshape(-1, 128, 128)
     count = blocks.shape[0]
-    lists = jnp.stack([slots.reshape(-1) for slots in (tile_rows, tile_cols, tile_live)])
+    slots = (tile_rows, tile_cols, tile_live)
     staged = pl.pallas_call(
         stage_kernel,
         out_shape=jax.ShapeDtypeStruct((count + 1, 128, 128), blocks.dtype),
-        in_specs=[VMEM] * 2,
-        out_specs=VMEM,
-        scratch_shapes=[pltpu.VMEM((128, 128), jnp.float32), pltpu.SemaphoreType.DMA],
-        compiler_params=params,
+        in_specs=[VMEM] * 3 + [pl.BlockSpec(memory_space=pl.ANY)],
+        out_specs=pl.BlockSpec(memory_space=pl.ANY),
+        scratch_shapes=[
+            pltpu.VMEM((1, 128, 128), blocks.dtype),
+            pltpu.VMEM((128, 128), jnp.float32),
+            pltpu.SemaphoreType.DMA((9,)),
+        ],
         cost_estimate=pl.CostEstimate(flops=0, bytes_accessed=4 * blocks.size, transcendentals=0),
         name="stage",
-    )(lists, blocks)
+    )(*slots, blocks)
     other = lax.ppermute(staged, "row", sides)
 
     own_sums = pl.pallas_call(
         lambda *refs: own_kernel(n_col, *refs),
         out_shape=jax.ShapeDtypeStruct((pairs, nvec, seg), jnp.float32),
-        in_specs=[SMEM] + [VMEM] * 2,
+        in_specs=[SMEM] * 3 + [VMEM] * 2,
         out_specs=VMEM,
         compiler_params=params,
         cost_estimate=pl.CostEstimate(flops=10**11, bytes_accessed=2 * blocks.size, transcendentals=0),
         name="own",
-    )(lists, row_sets, staged)
+    )(*slots, row_sets, staged)
     outgoing = pl.pallas_call(
         lambda *refs: pair_kernel(n_col, order, *refs),
         out_shape=jax.ShapeDtypeStruct((pairs, 2, nvec, seg), jnp.bfloat16),
@@ -145,11 +157,11 @@
             jax.ShapeDtypeStruct((n_col, nvec, seg), jnp.float32),
             jax.ShapeDtypeStruct((nvec, seg), jnp.float32),
         ],
-        in_specs=[SMEM] * 2 + [VMEM] * 3,
+        in_specs=[SMEM] * 4 + [VMEM] * 3,
         out_specs=[VMEM, VMEM],
         compiler_params=params,
         name="direct",
-    )(spots, lists, row_sets, arrived, staged)
+    )(spots, *slots, row_sets, arrived, staged)
     straight = exchange(direct, "col", None)
     return mirrored + jnp.sum(straight, axis=0)
 

time: 73.9 us -> 106 us (1.43)
  Pallas kernels: 3.42 us -> 37 us
  waiting for transfers between devices: 6.15 us -> 0.38 us
  blocking collectives: 48.9 us -> 53.6 us
    pallas_call x1, Pallas kernels: 0.09 us -> 33.7 us  [body(): pl.pallas_call(stage_kernel, out_shape=jax.ShapeDtypeStruct((count + 1, 1...]
    all_to_all x1, waiting for transfers between devices: 6.15 us -> 0.01 us  [exchange(): lax.all_to_all(parts, axes, 0, 0, tiled=True, axis_index_groups=groups)]
    all_to_all x2, blocking collectives: 48.9 us -> 53.6 us  [exchange(): lax.all_to_all(parts, axes, 0, 0, tiled=True, axis_index_groups=groups)]
  transfers between devices with their start and end apart: 2 -> 2, of which waited for: 1 -> 1; matrix products, arithmetic and copies ran while one was open for 1% -> 0% of each run, Pallas kernels for 1% -> 33%
where the time goes in v13:
time: 106 us; the launch traced here: 105 us
  blocking collectives  53.6 us (51%)
  Pallas kernels  37 us (35%)
  starting transfers between devices  11.2 us (11%)
  local copies, waits for them, and re-layouts  2.56 us (2%)
    all_to_all x2, blocking collectives, exchange(): lax.all_to_all(parts, axes, 0, 0, tiled=True, axis_index_groups=groups)  53.6 us
    pallas_call x1, Pallas kernels, body(): pl.pallas_call(stage_kernel, out_shape=jax.ShapeDtypeStruct((count + 1, 1...  33.7 us
    all_to_all x1, starting transfers between devices, exchange(): lax.all_to_all(parts, axes, 0, 0, tiled=True, axis_index_groups=groups)  9.05 us
    ppermute x1, starting transfers between devices, body(): other = lax.ppermute(staged, 'row', sides)  2.18 us
  transfers between devices with their start and end apart: 2, of which 1 were waited for; matrix products, arithmetic and copies ran while one was open for 0% of the time, Pallas kernels for 33%

profile of v13, /device:TPU:2, one launch (start us, length us, event | category | flops | bytes accessed | tf_op | source)
XLA Modules:
  0.0 105.4 jit_solution(17987813344684321395)
XLA Ops:
  0.0 1.3 %broadcast_in_dim.2 = bf16[32,8,128]{2,1,0:T(8,128)(2,1)} broadcast(bf16[8,128]{1,0:T(8,128)(2,1)} %param.6), dimensions={1,2} | broadcast | bytes 67584 | tf_op jit(solution)/shard_map/broadcast_in_dim | solution.py:110
  1.3 9.1 %all-to-all-start = ((bf16[32,8,128]{2,1,0:T(8,128)(2,1)}), bf16[32,8,128]{2,1,0:T(8,128)(2,1)S(1)}, u32[]{:S(2)}, u32[]{:S(2)}) async-start(bf16[32,8,128]{2,1,0:T(8,128)(2,1)} %broadcast_in_dim.2), calls=%async_computation | async-start | bytes 131072 | tf_op jit(solution)/shard_map/all_to_all | solution.py:13
  10.4 0.0 copy-start.2
  10.4 0.0 copy-start.3
  10.4 0.0 copy-start.4
  10.4 33.7 %stage.1.refs_4_.refs_6_ = bf16[33,128,128]{2,1,0:T(8,128)(2,1)} custom-call(s32[1,1,32]{2,1,0:T(1,128)} %refs_1_.3, s32[1,1,32]{2,1,0:T(1,128)} %refs_2_.3, s32[1,1,32]{2,1,0:T(1,128)} %refs_3_.1, bf16[32,128,128]{2,1,0:T(8,128)(2,1)} %bitcast.1), custom_call_target="tpu_custom_call" | custom-call | bytes 2097152 | tf_op jit(solution)/shard_map/stage/pallas_call | solution.py:114
  44.1 2.2 %collective-permute-start = (bf16[33,128,128]{2,1,0:T(8,128)(2,1)}, bf16[33,128,128]{2,1,0:T(8,128)(2,1)S(1)}, u32[]{:S(2)}, u32[]{:S(2)}) collective-permute-start(bf16[33,128,128]{2,1,0:T(8,128)(2,1)} %stage.1.refs_4_.refs_6_), channel_id=1, source_target_pairs={{0,16},{16,0},{32,48},{48,32},{64,80},{80,64},{96,112},{112,96},{1... | collective-permute-start | bytes 3244040 | tf_op jit(solution)/shard_map/ppermute | solution.py:127
  46.3 0.0 all-to-all-done.refs_3_.refs_0_.refs_4_
  46.3 0.0 copy-done.2
  46.3 0.0 copy-done.3
  46.3 0.0 copy-done.4
  46.3 0.0 copy-start
  46.3 1.2 %copy-done = bf16[33,128,128]{2,1,0:T(8,128)(2,1)S(1)} copy-done((bf16[33,128,128]{2,1,0:T(8,128)(2,1)S(1)}, bf16[33,128,128]{2,1,0:T(8,128)(2,1)}, u32[]{:S(2)}) %copy-start) | copy-done | bytes 1081368
  47.5 1.0 own.1.refs_2_
  48.5 0.0 copy-start.1
  48.5 0.0 copy-start.5
  48.5 0.4 collective-permute-done.refs_1_
  48.9 1.1 %pair.1 = bf16[32,2,8,128]{3,2,1,0:T(8,128)(2,1)S(1)} custom-call(bf16[32,8,128]{2,1,0:T(8,128)(2,1)S(1)} %all-to-all-done.refs_3_.refs_0_.refs_4_, bf16[33,128,128]{2,1,0:T(8,128)(2,1)S(1)} %collective-permute-done.refs_1_, f32[32,8,128]{2,1,0:T(8,128)S(1)} %own.1.refs_2_), custom_call_target="tpu_custom_call" | custom-call | tf_op jit(solution)/shard_map/pair/pallas_call | solution.py:138
  50.0 34.6 %all_to_all.15.refs_5_ = bf16[32,2,8,128]{3,2,1,0:T(8,128)(2,1)S(1)} all-to-all(bf16[32,2,8,128]{3,2,1,0:T(8,128)(2,1)S(1)} %pair.1), channel_id=1, replica_groups={{992,960,928,896,864,832,800,768,736,704,672,640,608,576,544,512,480,44..., dimensions={0} | all-to-all | bytes 262144 | tf_op jit(solution)/shard_map/all_to_all | solution.py:13
  84.6 0.0 copy-done.1
  84.6 0.0 copy-done.5
  84.6 1.2 %direct.1 = (f32[16,8,128]{2,1,0:T(8,128)S(1)}, f32[8,128]{1,0:T(8,128)S(1)}) custom-call(s32[32]{0:T(128)S(1)} %copy-done.5, s32[1,1,32]{2,1,0:T(1,128)S(1)} %copy-done.2, s32[1,1,32]{2,1,0:T(1,128)S(1)} %copy-done.3, s32[1,1,32]{2,1,0:T(1,128)S(1)} %copy-done.4, bf16[32,8,128]{2,1,0:T(8,128)(2,1)S(1)} %all-to-all-done.refs_3_.refs_0_.refs_4_, ...), custom_call_target="tpu_custom_call" | custom-call | tf_op jit(solution)/shard_map/direct/pallas_call | solution.py:154
  85.8 19.0 %all_to_all.16 = f32[16,8,128]{2,1,0:T(8,128)S(1)} all-to-all(f32[16,8,128]{2,1,0:T(8,128)S(1)} %get-tuple-element.8), channel_id=1, replica_groups=mesh['row'=64,'col'=16] {'col'}, dimensions={0} | all-to-all | bytes 131072 | tf_op jit(solution)/shard_map/all_to_all | solution.py:13
  104.9 0.6 add.3
  (1 shorter events, 0.0 us)
Async XLA Ops:
  1.3 45.0 %all-to-all-start = ((bf16[32,8,128]{2,1,0:T(8,128)(2,1)}), bf16[32,8,128]{2,1,0:T(8,128)(2,1)S(1)}, u32[]{:S(2)}, u32[]{:S(2)}) async-start(bf16[32,8,128]{2,1,0:T(8,128)(2,1)} %broadcast_in_dim.2), calls=%async_computation | async-start | bytes 131072 | tf_op jit(solution)/shard_map/all_to_all | solution.py:13
  10.4 35.9 %copy-start.2 = (s32[1,1,32]{2,1,0:T(1,128)S(1)}, s32[1,1,32]{2,1,0:T(1,128)}, u32[]{:S(2)}) copy-start(s32[1,1,32]{2,1,0:T(1,128)} %refs_1_.3) | copy-start | bytes 388
  10.4 35.9 %copy-start.3 = (s32[1,1,32]{2,1,0:T(1,128)S(1)}, s32[1,1,32]{2,1,0:T(1,128)}, u32[]{:S(2)}) copy-start(s32[1,1,32]{2,1,0:T(1,128)} %refs_2_.3) | copy-start | bytes 388
  10.4 35.9 %copy-start.4 = (s32[1,1,32]{2,1,0:T(1,128)S(1)}, s32[1,1,32]{2,1,0:T(1,128)}, u32[]{:S(2)}) copy-start(s32[1,1,32]{2,1,0:T(1,128)} %refs_3_.1) | copy-start | bytes 388
  44.1 4.8 %collective-permute-start = (bf16[33,128,128]{2,1,0:T(8,128)(2,1)}, bf16[33,128,128]{2,1,0:T(8,128)(2,1)S(1)}, u32[]{:S(2)}, u32[]{:S(2)}) collective-permute-start(bf16[33,128,128]{2,1,0:T(8,128)(2,1)} %stage.1.refs_4_.refs_6_), channel_id=1, source_target_pairs={{0,16},{16,0},{32,48},{48,32},{64,80},{80,64},{96,112},{112,96},{1... | collective-permute-start | bytes 3244040 | tf_op jit(solution)/shard_map/ppermute | solution.py:127
  46.3 1.2 %copy-start = (bf16[33,128,128]{2,1,0:T(8,128)(2,1)S(1)}, bf16[33,128,128]{2,1,0:T(8,128)(2,1)}, u32[]{:S(2)}) copy-start(bf16[33,128,128]{2,1,0:T(8,128)(2,1)} %stage.1.refs_4_.refs_6_) | copy-start | bytes 3244036
  48.5 36.1 %copy-start.1 = (bf16[33,128,128]{2,1,0:T(8,128)(2,1)S(1)}, bf16[33,128,128]{2,1,0:T(8,128)(2,1)}, u32[]{:S(2)}) copy-start(bf16[33,128,128]{2,1,0:T(8,128)(2,1)} %stage.1.refs_4_.refs_6_) | copy-start | bytes 3244036
  48.5 36.1 %copy-start.5 = (s32[32]{0:T(128)S(1)}, s32[32]{0:T(128)}, u32[]{:S(2)}) copy-start(s32[32]{0:T(128)} %constant.4.clone.refs_0_) | copy-start | bytes 388

commit v14 on v12

--- a/solution.py
+++ b/solution.py
@@ -34,7 +34,7 @@
     pair, side = my_row >> 1, my_row & 1
     for k in range(count):
         row, col, live = slot(k)
-        product = jnp.dot(row_sets[(seat(row, n_col) << 1) | who], tiles[k], preferred_element_type=jnp.float32)
+        product = jnp.dot(row_sets[2 * n_col - 1 - ((seat(row, n_col) << 1) | who)], tiles[k], preferred_element_type=jnp.float32)
         below = (2 * pair + who) * n_col + row > col * n_col + my_col
         weight = jnp.where(below & ((col & 1) == side) & (live == 1), 1.0, 0.0)
         sums[col >> 1] += product * weight
@@ -57,7 +57,8 @@
     copy.wait()
     slot = lambda k: (notes[0, k], notes[1, k], notes[2, k])
     add_mirror(n_col, 1 - (my_row & 1), slot, count, row_sets, other, sums)
-    first, second = row_sets[seat(my_col, n_col) << 1], row_sets[(seat(my_col, n_col) << 1) | 1]
+    base = 2 * n_col - 1 - (seat(my_col, n_col) << 1)
+    first, second = row_sets[base], row_sets[base - 1]
     for at, p in enumerate(order):
         high = sums[p].astype(jnp.bfloat16)
         low = (sums[p] - high.astype(jnp.float32)).astype(jnp.bfloat16)
@@ -74,16 +75,16 @@
         total += jnp.where(p >= pair, both, 0.0)
     mirrored[...] = total
     parts[...] = jnp.zeros_like(parts)
-    base = seat(my_col, n_col) << 1
+    base = 2 * n_col - 1 - (seat(my_col, n_col) << 1)
     for k in range(lists.shape[1]):
         row, col = lists[0, k], lists[1, k]
-        here = row_sets[base + (col & 1)]
+        here = row_sets[base - (col & 1)]
         values = jnp.where((col >> 1) == pair, here, arrived[spots[col >> 1], col & 1])
         product = lax.dot_general(
             values, staged[k], (((1,), (1,)), ((), ())), preferred_element_type=jnp.float32
         )
         below = my_row * n_col + row >= col * n_col + my_col
-        parts[row] += product * jnp.where(below & (lists[2, k] == 1), 1.0, 0.0)
+        parts[n_col - 1 - row] += product * jnp.where(below & (lists[2, k] == 1), 1.0, 0.0)
 
 
 def body(vectors, tiles, tile_rows, tile_cols, tile_live):
@@ -97,7 +98,7 @@
     params = pltpu.CompilerParams(vmem_limit_bytes=4 << 20)
 
     columns = sorted(range(n_col), key=lambda c: seat(c, n_col))
-    near = [[(2 * p + side) * n_col + c for c in columns for side in range(2)] for p in range(pairs)]
+    near = [[(2 * p + side) * n_col + c for c in columns[::-1] for side in (1, 0)] for p in range(pairs)]
     row_sets = exchange(jnp.broadcast_to(vectors[None], (2 * n_col, nvec, seg)), ("row", "col"), near)
     blocks = tiles.reshape(-1, 128, 128)
     count = blocks.shape[0]
@@ -150,7 +151,7 @@
         compiler_params=params,
         name="direct",
     )(spots, lists, row_sets, arrived, staged)
-    straight = exchange(direct, "col", None)
+    straight = exchange(direct, "col", [list(range(n_col))[::-1]])
     return mirrored + jnp.sum(straight, axis=0)
 
 

time: 73.9 us -> 70.5 us (0.954)
  the two profiles are of different devices: /device:TPU:2 before, /device:TPU:6 now
where the time goes in v14:
time: 70.5 us; the launch traced here: 70.2 us
  blocking collectives  48.9 us (69%)
  starting transfers between devices  10.5 us (15%)
  waiting for transfers between devices  3.45 us (5%)
  Pallas kernels  3.42 us (5%)
  local copies, waits for them, and re-layouts  2.53 us (4%)
  other arithmetic  1.32 us (2%)
    all_to_all x2, blocking collectives, exchange(): lax.all_to_all(parts, axes, 0, 0, tiled=True, axis_index_groups=groups)  48.9 us
    all_to_all x1, starting transfers between devices, exchange(): lax.all_to_all(parts, axes, 0, 0, tiled=True, axis_index_groups=groups)  8.49 us
    all_to_all x1, waiting for transfers between devices, exchange(): lax.all_to_all(parts, axes, 0, 0, tiled=True, axis_index_groups=groups)  3.45 us
    ppermute x1, starting transfers between devices, body(): other = lax.ppermute(staged, 'row', sides)  1.99 us
  transfers between devices with their start and end apart: 2, of which 1 were waited for; matrix products, arithmetic and copies ran while one was open for 1% of the time, Pallas kernels for 2%

profile of v14, /device:TPU:6, one launch (start us, length us, event | category | flops | bytes accessed | tf_op | source)
XLA Modules:
  0.0 70.2 jit_solution(11116914617277280357)
XLA Ops:
  0.0 1.3 %broadcast_in_dim.2 = bf16[32,8,128]{2,1,0:T(8,128)(2,1)} broadcast(bf16[8,128]{1,0:T(8,128)(2,1)} %param.6), dimensions={1,2} | broadcast | bytes 67584 | tf_op jit(solution)/shard_map/broadcast_in_dim | solution.py:102
  1.3 8.5 %all-to-all-start = ((bf16[32,8,128]{2,1,0:T(8,128)(2,1)}), bf16[32,8,128]{2,1,0:T(8,128)(2,1)S(1)}, u32[]{:S(2)}, u32[]{:S(2)}) async-start(bf16[32,8,128]{2,1,0:T(8,128)(2,1)} %broadcast_in_dim.2), calls=%async_computation | async-start | bytes 131072 | tf_op jit(solution)/shard_map/all_to_all | solution.py:13
  9.8 0.7 pad_add_fusion.lists.refs_0_.refs_1_
  10.5 0.0 copy-start
  10.5 1.2 %copy-done = bf16[1,1,32,128,128]{4,3,2,1,0:T(8,128)(2,1)S(1)} copy-done((bf16[1,1,32,128,128]{4,3,2,1,0:T(8,128)(2,1)S(1)}, bf16[1,1,32,128,128]{4,3,2,1,0:T(8,128)(2,1)}, u32[]{:S(2)}) %copy-start) | copy-done | bytes 1048600
  11.7 0.1 stage.1.refs_2_.refs_4_
  11.8 2.0 %collective-permute-start = (bf16[33,128,128]{2,1,0:T(8,128)(2,1)S(1)}, bf16[33,128,128]{2,1,0:T(8,128)(2,1)S(1)}, u32[]{:S(2)}, u32[]{:S(2)}) collective-permute-start(bf16[33,128,128]{2,1,0:T(8,128)(2,1)S(1)} %stage.1.refs_2_.refs_4_), channel_id=1, source_target_pairs={{0,16},{16,0},{32,48},{48,32},{64,80},{80,64},{96,112},{112,96},{1... | collective-permute-start | bytes 3244040 | tf_op jit(solution)/shard_map/ppermute | solution.py:116
  13.8 3.4 %all-to-all-done.refs_1_.refs_0_.refs_2_ = bf16[32,8,128]{2,1,0:T(8,128)(2,1)S(1)} async-done(((bf16[32,8,128]{2,1,0:T(8,128)(2,1)}), bf16[32,8,128]{2,1,0:T(8,128)(2,1)S(1)}, u32[]{:S(2)}, u32[]{:S(2)}) %all-to-all-start) | async-done | bytes 65568 | tf_op jit(solution)/shard_map/all_to_all | solution.py:13
  17.3 1.0 %own.1.refs_2_ = f32[32,8,128]{2,1,0:T(8,128)S(1)} custom-call(s32[3,32]{1,0:T(4,128)S(1)} %pad_add_fusion.lists.refs_0_.refs_1_, bf16[32,8,128]{2,1,0:T(8,128)(2,1)S(1)} %all-to-all-done.refs_1_.refs_0_.refs_2_, bf16[33,128,128]{2,1,0:T(8,128)(2,1)S(1)} %stage.1.refs_2_.refs_4_), custom_call_target="tpu_custom_call" | custom-call | flops 99999997952 | bytes 1048576 | tf_op jit(solution)/shard_map/own/pallas_call | solution.py:118
  18.2 0.0 copy-start.1
  18.2 0.0 collective-permute-done.refs_1_
  18.3 1.1 %pair.1 = bf16[32,2,8,128]{3,2,1,0:T(8,128)(2,1)S(1)} custom-call(bf16[32,8,128]{2,1,0:T(8,128)(2,1)S(1)} %all-to-all-done.refs_1_.refs_0_.refs_2_, bf16[33,128,128]{2,1,0:T(8,128)(2,1)S(1)} %collective-permute-done.refs_1_, f32[32,8,128]{2,1,0:T(8,128)S(1)} %own.1.refs_2_), custom_call_target="tpu_custom_call" | custom-call | tf_op jit(solution)/shard_map/pair/pallas_call | solution.py:127
  19.4 33.6 %all_to_all.15.refs_3_ = bf16[32,2,8,128]{3,2,1,0:T(8,128)(2,1)S(1)} all-to-all(bf16[32,2,8,128]{3,2,1,0:T(8,128)(2,1)S(1)} %pair.1), channel_id=1, replica_groups={{992,960,928,896,864,832,800,768,736,704,672,640,608,576,544,512,480,44..., dimensions={0} | all-to-all | bytes 262144 | tf_op jit(solution)/shard_map/all_to_all | solution.py:13
  53.0 0.0 copy-done.1
  53.0 1.2 %direct.1 = (f32[16,8,128]{2,1,0:T(8,128)S(1)}, f32[8,128]{1,0:T(8,128)S(1)}) custom-call(s32[32]{0:T(128)S(1)} %copy-done.1, s32[3,32]{1,0:T(4,128)S(1)} %pad_add_fusion.lists.refs_0_.refs_1_, bf16[32,8,128]{2,1,0:T(8,128)(2,1)S(1)} %all-to-all-done.refs_1_.refs_0_.refs_2_, bf16[32,2,8,128]{3,2,1,0:T(8,128)(2,1)S(1)} %all_to_all.15.refs_3_, ...), custom_call_target="tpu_custom_call" | custom-call | tf_op jit(solution)/shard_map/direct/pallas_call | solution.py:143
  54.3 15.3 %all_to_all.16 = f32[16,8,128]{2,1,0:T(8,128)S(1)} all-to-all(f32[16,8,128]{2,1,0:T(8,128)S(1)} %get-tuple-element.8), channel_id=1, replica_groups={{15,14,13,12,11,10,9,8,7,6,5,4,3,2,1,0},{31,30,29,28,27,26,25,24,23,22,..., dimensions={0} | all-to-all | bytes 131072 | tf_op jit(solution)/shard_map/all_to_all | solution.py:13
  69.6 0.6 add.3
  (1 shorter events, 0.0 us)
Async XLA Ops:
  1.3 16.0 %all-to-all-start = ((bf16[32,8,128]{2,1,0:T(8,128)(2,1)}), bf16[32,8,128]{2,1,0:T(8,128)(2,1)S(1)}, u32[]{:S(2)}, u32[]{:S(2)}) async-start(bf16[32,8,128]{2,1,0:T(8,128)(2,1)} %broadcast_in_dim.2), calls=%async_computation | async-start | bytes 131072 | tf_op jit(solution)/shard_map/all_to_all | solution.py:13
  10.5 1.2 %copy-start = (bf16[1,1,32,128,128]{4,3,2,1,0:T(8,128)(2,1)S(1)}, bf16[1,1,32,128,128]{4,3,2,1,0:T(8,128)(2,1)}, u32[]{:S(2)}) copy-start(bf16[1,1,32,128,128]{4,3,2,1,0:T(8,128)(2,1)} %param.7) | copy-start | bytes 3145732
  11.8 6.4 %collective-permute-start = (bf16[33,128,128]{2,1,0:T(8,128)(2,1)S(1)}, bf16[33,128,128]{2,1,0:T(8,128)(2,1)S(1)}, u32[]{:S(2)}, u32[]{:S(2)}) collective-permute-start(bf16[33,128,128]{2,1,0:T(8,128)(2,1)S(1)} %stage.1.refs_2_.refs_4_), channel_id=1, source_target_pairs={{0,16},{16,0},{32,48},{48,32},{64,80},{80,64},{96,112},{112,96},{1... | collective-permute-start | bytes 3244040 | tf_op jit(solution)/shard_map/ppermute | solution.py:116
  18.2 34.8 %copy-start.1 = (s32[32]{0:T(128)S(1)}, s32[32]{0:T(128)}, u32[]{:S(2)}) copy-start(s32[32]{0:T(128)} %constant.4.clone.refs_0_) | copy-start | bytes 388

commit v15 on v14

--- a/solution.py
+++ b/solution.py
@@ -11,12 +11,6 @@
 
 def exchange(parts, axes, groups):
     return lax.all_to_all(parts, axes, 0, 0, tiled=True, axis_index_groups=groups)
-
-
-def seat(col, n_col):
-    half = n_col // 4
-    y = col >> 1
-    return ((y & (half - 1)) << 2) | ((y >> (half.bit_length() - 1)) << 1) | (col & 1)
 
 
 def stage_kernel(lists, tiles, out, notes, sem):
@@ -34,7 +28,7 @@
     pair, side = my_row >> 1, my_row & 1
     for k in range(count):
         row, col, live = slot(k)
-        product = jnp.dot(row_sets[2 * n_col - 1 - ((seat(row, n_col) << 1) | who)], tiles[k], preferred_element_type=jnp.float32)
+        product = jnp.dot(row_sets[2 * n_col - 1 - ((row << 1) | who)], tiles[k], preferred_element_type=jnp.float32)
         below = (2 * pair + who) * n_col + row > col * n_col + my_col
         weight = jnp.where(below & ((col & 1) == side) & (live == 1), 1.0, 0.0)
         sums[col >> 1] += product * weight
@@ -57,7 +51,7 @@
     copy.wait()
     slot = lambda k: (notes[0, k], notes[1, k], notes[2, k])
     add_mirror(n_col, 1 - (my_row & 1), slot, count, row_sets, other, sums)
-    base = 2 * n_col - 1 - (seat(my_col, n_col) << 1)
+    base = 2 * n_col - 1 - (my_col << 1)
     first, second = row_sets[base], row_sets[base - 1]
     for at, p in enumerate(order):
         high = sums[p].astype(jnp.bfloat16)
@@ -75,7 +69,7 @@
         total += jnp.where(p >= pair, both, 0.0)
     mirrored[...] = total
     parts[...] = jnp.zeros_like(parts)
-    base = 2 * n_col - 1 - (seat(my_col, n_col) << 1)
+    base = 2 * n_col - 1 - (my_col << 1)
     for k in range(lists.shape[1]):
         row, col = lists[0, k], lists[1, k]
         here = row_sets[base - (col & 1)]
@@ -97,7 +91,7 @@
     spots = jnp.array([order.index(p) for p in range(pairs)], jnp.int32)
     params = pltpu.CompilerParams(vmem_limit_bytes=4 << 20)
 
-    columns = sorted(range(n_col), key=lambda c: seat(c, n_col))
+    columns = list(range(n_col))
     near = [[(2 * p + side) * n_col + c for c in columns[::-1] for side in (1, 0)] for p in range(pairs)]
     row_sets = exchange(jnp.broadcast_to(vectors[None], (2 * n_col, nvec, seg)), ("row", "col"), near)
     blocks = tiles.reshape(-1, 128, 128)
@@ -151,7 +145,7 @@
         compiler_params=params,
         name="direct",
     )(spots, lists, row_sets, arrived, staged)
-    straight = exchange(direct, "col", [list(range(n_col))[::-1]])
+    straight = exchange(direct, "col", [columns[::-1]])
     return mirrored + jnp.sum(straight, axis=0)
 
 

time: 70.5 us -> 70.5 us (level)
  no operation moved by 1% of the time
where the time goes in v15:
time: 70.5 us; the launch traced here: 70.2 us
  blocking collectives  48.7 us (69%)
  starting transfers between devices  10.5 us (15%)
  waiting for transfers between devices  3.67 us (5%)
  Pallas kernels  3.42 us (5%)
  local copies, waits for them, and re-layouts  2.53 us (4%)
  other arithmetic  1.32 us (2%)
    all_to_all x2, blocking collectives, exchange(): lax.all_to_all(parts, axes, 0, 0, tiled=True, axis_index_groups=groups)  48.7 us
    all_to_all x1, starting transfers between devices, exchange(): lax.all_to_all(parts, axes, 0, 0, tiled=True, axis_index_groups=groups)  8.49 us
    all_to_all x1, waiting for transfers between devices, exchange(): lax.all_to_all(parts, axes, 0, 0, tiled=True, axis_index_groups=groups)  3.67 us
    ppermute x1, starting transfers between devices, body(): other = lax.ppermute(staged, 'row', sides)  1.99 us
  transfers between devices with their start and end apart: 2, of which 1 were waited for; matrix products, arithmetic and copies ran while one was open for 1% of the time, Pallas kernels for 2%

profile of v15, /device:TPU:6, one launch (start us, length us, event | category | flops | bytes accessed | tf_op | source)
XLA Modules:
  0.0 70.2 jit_solution(17463340680517554379)
XLA Ops:
  0.0 1.3 %broadcast_in_dim.2 = bf16[32,8,128]{2,1,0:T(8,128)(2,1)} broadcast(bf16[8,128]{1,0:T(8,128)(2,1)} %param.6), dimensions={1,2} | broadcast | bytes 67584 | tf_op jit(solution)/shard_map/broadcast_in_dim | solution.py:96
  1.3 8.5 %all-to-all-start = ((bf16[32,8,128]{2,1,0:T(8,128)(2,1)}), bf16[32,8,128]{2,1,0:T(8,128)(2,1)S(1)}, u32[]{:S(2)}, u32[]{:S(2)}) async-start(bf16[32,8,128]{2,1,0:T(8,128)(2,1)} %broadcast_in_dim.2), calls=%async_computation | async-start | bytes 131072 | tf_op jit(solution)/shard_map/all_to_all | solution.py:13
  9.8 0.7 pad_add_fusion.lists.refs_0_.refs_1_
  10.5 0.0 copy-start
  10.5 1.2 %copy-done = bf16[1,1,32,128,128]{4,3,2,1,0:T(8,128)(2,1)S(1)} copy-done((bf16[1,1,32,128,128]{4,3,2,1,0:T(8,128)(2,1)S(1)}, bf16[1,1,32,128,128]{4,3,2,1,0:T(8,128)(2,1)}, u32[]{:S(2)}) %copy-start) | copy-done | bytes 1048600
  11.7 0.1 stage.1.refs_2_.refs_4_
  11.8 2.0 %collective-permute-start = (bf16[33,128,128]{2,1,0:T(8,128)(2,1)S(1)}, bf16[33,128,128]{2,1,0:T(8,128)(2,1)S(1)}, u32[]{:S(2)}, u32[]{:S(2)}) collective-permute-start(bf16[33,128,128]{2,1,0:T(8,128)(2,1)S(1)} %stage.1.refs_2_.refs_4_), channel_id=1, source_target_pairs={{0,16},{16,0},{32,48},{48,32},{64,80},{80,64},{96,112},{112,96},{1... | collective-permute-start | bytes 3244040 | tf_op jit(solution)/shard_map/ppermute | solution.py:110
  13.8 3.7 %all-to-all-done.refs_1_.refs_0_.refs_2_ = bf16[32,8,128]{2,1,0:T(8,128)(2,1)S(1)} async-done(((bf16[32,8,128]{2,1,0:T(8,128)(2,1)}), bf16[32,8,128]{2,1,0:T(8,128)(2,1)S(1)}, u32[]{:S(2)}, u32[]{:S(2)}) %all-to-all-start) | async-done | bytes 65568 | tf_op jit(solution)/shard_map/all_to_all | solution.py:13
  17.5 1.0 %own.1.refs_2_ = f32[32,8,128]{2,1,0:T(8,128)S(1)} custom-call(s32[3,32]{1,0:T(4,128)S(1)} %pad_add_fusion.lists.refs_0_.refs_1_, bf16[32,8,128]{2,1,0:T(8,128)(2,1)S(1)} %all-to-all-done.refs_1_.refs_0_.refs_2_, bf16[33,128,128]{2,1,0:T(8,128)(2,1)S(1)} %stage.1.refs_2_.refs_4_), custom_call_target="tpu_custom_call" | custom-call | flops 99999997952 | bytes 1048576 | tf_op jit(solution)/shard_map/own/pallas_call | solution.py:112
  18.5 0.0 copy-start.1
  18.5 0.0 collective-permute-done.refs_1_
  18.5 1.1 %pair.1 = bf16[32,2,8,128]{3,2,1,0:T(8,128)(2,1)S(1)} custom-call(bf16[32,8,128]{2,1,0:T(8,128)(2,1)S(1)} %all-to-all-done.refs_1_.refs_0_.refs_2_, bf16[33,128,128]{2,1,0:T(8,128)(2,1)S(1)} %collective-permute-done.refs_1_, f32[32,8,128]{2,1,0:T(8,128)S(1)} %own.1.refs_2_), custom_call_target="tpu_custom_call" | custom-call | tf_op jit(solution)/shard_map/pair/pallas_call | solution.py:121
  19.6 33.1 %all_to_all.15.refs_3_ = bf16[32,2,8,128]{3,2,1,0:T(8,128)(2,1)S(1)} all-to-all(bf16[32,2,8,128]{3,2,1,0:T(8,128)(2,1)S(1)} %pair.1), channel_id=1, replica_groups={{992,960,928,896,864,832,800,768,736,704,672,640,608,576,544,512,480,44..., dimensions={0} | all-to-all | bytes 262144 | tf_op jit(solution)/shard_map/all_to_all | solution.py:13
  52.7 0.0 copy-done.1
  52.7 1.2 %direct.1 = (f32[16,8,128]{2,1,0:T(8,128)S(1)}, f32[8,128]{1,0:T(8,128)S(1)}) custom-call(s32[32]{0:T(128)S(1)} %copy-done.1, s32[3,32]{1,0:T(4,128)S(1)} %pad_add_fusion.lists.refs_0_.refs_1_, bf16[32,8,128]{2,1,0:T(8,128)(2,1)S(1)} %all-to-all-done.refs_1_.refs_0_.refs_2_, bf16[32,2,8,128]{3,2,1,0:T(8,128)(2,1)S(1)} %all_to_all.15.refs_3_, ...), custom_call_target="tpu_custom_call" | custom-call | tf_op jit(solution)/shard_map/direct/pallas_call | solution.py:137
  54.0 15.6 %all_to_all.16 = f32[16,8,128]{2,1,0:T(8,128)S(1)} all-to-all(f32[16,8,128]{2,1,0:T(8,128)S(1)} %get-tuple-element.8), channel_id=1, replica_groups={{15,14,13,12,11,10,9,8,7,6,5,4,3,2,1,0},{31,30,29,28,27,26,25,24,23,22,..., dimensions={0} | all-to-all | bytes 131072 | tf_op jit(solution)/shard_map/all_to_all | solution.py:13
  69.6 0.6 add.3
  (1 shorter events, 0.0 us)
Async XLA Ops:
  1.3 16.2 %all-to-all-start = ((bf16[32,8,128]{2,1,0:T(8,128)(2,1)}), bf16[32,8,128]{2,1,0:T(8,128)(2,1)S(1)}, u32[]{:S(2)}, u32[]{:S(2)}) async-start(bf16[32,8,128]{2,1,0:T(8,128)(2,1)} %broadcast_in_dim.2), calls=%async_computation | async-start | bytes 131072 | tf_op jit(solution)/shard_map/all_to_all | solution.py:13
  10.5 1.2 %copy-start = (bf16[1,1,32,128,128]{4,3,2,1,0:T(8,128)(2,1)S(1)}, bf16[1,1,32,128,128]{4,3,2,1,0:T(8,128)(2,1)}, u32[]{:S(2)}) copy-start(bf16[1,1,32,128,128]{4,3,2,1,0:T(8,128)(2,1)} %param.7) | copy-start | bytes 3145732
  11.8 6.6 %collective-permute-start = (bf16[33,128,128]{2,1,0:T(8,128)(2,1)S(1)}, bf16[33,128,128]{2,1,0:T(8,128)(2,1)S(1)}, u32[]{:S(2)}, u32[]{:S(2)}) collective-permute-start(bf16[33,128,128]{2,1,0:T(8,128)(2,1)S(1)} %stage.1.refs_2_.refs_4_), channel_id=1, source_target_pairs={{0,16},{16,0},{32,48},{48,32},{64,80},{80,64},{96,112},{112,96},{1... | collective-permute-start | bytes 3244040 | tf_op jit(solution)/shard_map/ppermute | solution.py:110
  18.5 34.3 %copy-start.1 = (s32[32]{0:T(128)S(1)}, s32[32]{0:T(128)}, u32[]{:S(2)}) copy-start(s32[32]{0:T(128)} %constant.4.clone.refs_0_) | copy-start | bytes 388
